TPU v7x, 1024 devices: a whole 4x8x16 slice. The times are simulated.
1024 devices in a mesh: dp: 128 (over z_hi, y, x, core), mp: 8 (over z_lo).
Axes of the slice: x: 4, y: 8, z: 16 (z_hi: 2, z_lo: 8; z = z_hi * 8 + z_lo), core: 2. Of those that a mesh axis runs over, the one named last changes fastest.
Arguments:
- queries: bfloat16 [32768, 3072], P('dp', 'mp'), may hold values from -6 to 6
- keys: bfloat16 [32768, 3072], P('dp', 'mp'), may hold values from -6 to 6
- values: bfloat16 [32768, 3072], P('dp', 'mp'), may hold values from -24 to 24
- w_out: bfloat16 [3072, 6144], P(None, ('mp', 'dp')), may hold values from -0.109375 to 0.109375
- cotangent: bfloat16 [32768, 6144], P('dp', 'mp'), may hold values from -6 to 6
Outputs:
- branch_out: bfloat16 [32768, 6144], P('dp', 'mp')
- grad_queries: bfloat16 [32768, 3072], P('dp', 'mp')
- grad_keys: bfloat16 [32768, 3072], P('dp', 'mp')
- grad_values: bfloat16 [32768, 3072], P('dp', 'mp')
All inputs are finite; a program needn't handle non-finite values.
Results may differ from a plain program's by a relative error of at most 0.03.
Values may be sent and summed in bfloat16 or wider, within the bound.
No kernel may reach another device: no remote copies, remote signals or barrier semaphores. Data moves between devices by JAX's collectives and lax.ppermute only.
A program may use at most 64 MiB of HBM per device.

v0:
```python
import math

import jax
import jax.numpy as jnp
from jax import lax
from jax.sharding import PartitionSpec as P

HD = 128
SEQ = 256


def on_device(queries, keys, values, w_out, cotangent):
    row_count = queries.shape[0]
    group_width = queries.shape[1]
    local_heads = group_width // HD
    image_count = row_count // SEQ
    group_count = lax.axis_size("mp")
    feature_group = cotangent.shape[1]
    score_scale = 1.0 / math.sqrt(HD)
    shape_heads = (image_count, SEQ, local_heads, HD)
    query_heads = queries.reshape(shape_heads)
    key_heads = keys.reshape(shape_heads)
    value_heads = values.reshape(shape_heads)
    scores = (
        jnp.einsum("bqhd,bkhd->bhqk", query_heads, key_heads, preferred_element_type=jnp.float32)
        * score_scale
    )
    softmax_out = jax.nn.softmax(scores, -1)
    softmax_low = softmax_out.astype(jnp.bfloat16)
    head_out = (
        jnp.einsum("bhqk,bkhd->bqhd", softmax_low, value_heads, preferred_element_type=jnp.float32)
        .astype(jnp.bfloat16)
        .reshape(row_count, group_width)
    )
    shard_width = w_out.shape[1]
    exchanged = lax.all_to_all(
        w_out.reshape(w_out.shape[0], 1, shard_width), "mp", split_axis=0, concat_axis=1, tiled=True
    )
    w_rows = lax.all_gather(exchanged, "dp", axis=2, tiled=True).reshape(
        group_width, group_count * feature_group
    )
    out_terms = jnp.dot(head_out, w_rows, preferred_element_type=jnp.float32)
    branch_out = lax.psum_scatter(
        out_terms.astype(jnp.bfloat16), "mp", scatter_dimension=1, tiled=True
    )
    cot_whole = lax.all_gather(cotangent, "mp", axis=1, tiled=True)
    pieces_grad = jnp.einsum(
        "tjd,cjd->tjc",
        cot_whole.reshape(row_count, group_count, feature_group),
        w_rows.reshape(group_width, group_count, feature_group),
        preferred_element_type=jnp.float32,
    ).astype(jnp.bfloat16)
    pieces_grad = lax.optimization_barrier(pieces_grad)
    grad_out = jnp.sum(pieces_grad.astype(jnp.float32), 1).astype(jnp.bfloat16)
    grad_heads = grad_out.reshape(shape_heads)
    soft_grad = jnp.einsum(
        "bqhd,bkhd->bhqk", grad_heads, value_heads, preferred_element_type=jnp.float32
    )
    score_grad = (
        softmax_out * (soft_grad - jnp.sum(soft_grad * softmax_out, -1, keepdims=True))
    ).astype(jnp.bfloat16)
    grad_queries = (
        (
            jnp.einsum("bhqk,bkhd->bqhd", score_grad, key_heads, preferred_element_type=jnp.float32)
            * score_scale
        )
        .astype(jnp.bfloat16)
        .reshape(row_count, group_width)
    )
    grad_keys = (
        (
            jnp.einsum(
                "bhqk,bqhd->bkhd", score_grad, query_heads, preferred_element_type=jnp.float32
            )
            * score_scale
        )
        .astype(jnp.bfloat16)
        .reshape(row_count, group_width)
    )
    grad_values = (
        jnp.einsum("bhqk,bqhd->bkhd", softmax_low, grad_heads, preferred_element_type=jnp.float32)
        .astype(jnp.bfloat16)
        .reshape(row_count, group_width)
    )
    return (branch_out, grad_queries, grad_keys, grad_values)


def solution(mesh):
    return jax.shard_map(
        on_device,
        mesh=mesh,
        in_specs=(
            P("dp", "mp"),
            P("dp", "mp"),
            P("dp", "mp"),
            P(None, ("mp", "dp")),
            P("dp", "mp"),
        ),
        out_specs=(P("dp", "mp"), P("dp", "mp"), P("dp", "mp"), P("dp", "mp")),
        check_vma=False,
    )
```

profile of v0, /device:TPU:1, one launch (start us, length us, event | category | flops | bytes accessed | tf_op | source)
XLA Modules:
  0.0 397.4 jit_solution(5479153758577676546)
XLA Ops:
  7.2 0.0 copy-start
  7.2 0.0 copy-start.1
  7.2 0.0 copy-start.2
  7.2 0.0 copy-start.3
  7.2 0.0 all-gather.6.cloned.1.call-start
  7.3 0.5 broadcast.27
  7.8 1.5 reduce.7
  9.2 0.4 copy.95
  9.7 1.2 reshape.116
  10.9 25.6 %all_to_all.18 = bf16[8,2,1152]{2,1,0:T(2,128)(2,1)S(1)} all-to-all(bf16[8,2,1152]{2,1,0:T(2,128)(2,1)S(1)} %reshape.116), channel_id=1, replica_groups=mesh['dp'=128,'mp'=8] {'mp'}, dimensions={0} | all-to-all | bytes 73728 | tf_op jit(solution)/shard_map/all_to_all | solution.py:36
  36.4 1.8 reshape.117
  38.2 1.4 copy.69
  39.6 0.6 copy.94
  40.2 0.0 all-gather.6.cloned.1.call-update
  40.3 0.0 all-gather.4.cloned.1.call-start
  40.3 0.0 copy-done
  40.3 0.9 copy.73
  41.3 0.0 all-gather.4.cloned.1.call-update
  41.3 0.0 reduce-scatter.2.cloned.1.call-start
  41.3 0.0 copy-done.1
  41.3 0.1 copy.66
  41.5 0.0 copy-done.2
  41.5 0.1 copy.62
  41.7 0.0 copy-done.3
  41.7 0.1 copy.63
  41.8 0.5 fusion.17
  42.3 0.6 convolution_convert_fusion.1
  42.9 183.0 %all-gather.6.cloned.1.call-done = bf16[384,8,1,768]{0,1,2,3:T(8,128)(2,1)} async-done(((bf16[384,8,1,6]{0,1,2,3:T(8,128)(2,1)}), bf16[384,8,1,768]{0,1,2,3:T(8,128)(2,1)}) %all-gather.6.cloned.1.call-update) | async-done | bytes 4718608 | tf_op jit(solution)/shard_map/all_gather | solution.py:39
  225.9 2.9 copy.71
  228.9 3.5 convolution_convert_fusion
  232.3 0.0 reduce-scatter.2.cloned.1.call-update
  232.4 7.1 %copy.72 = bf16[384,8,1,768]{3,0,1,2:T(8,128)(2,1)} copy(bf16[384,8,1,768]{0,1,2,3:T(8,128)(2,1)} %all-gather.6.cloned.1.call-done) | data formatting | bytes 9437184 | tf_op jit(solution)/shard_map/all_gather | solution.py:39
  239.4 64.7 %all-gather.4.cloned.1.call-done = bf16[256,6144]{0,1:T(8,128)(2,1)} async-done(((bf16[256,768]{0,1:T(8,128)(2,1)}), bf16[256,6144]{0,1:T(8,128)(2,1)}) %all-gather.4.cloned.1.call-update) | async-done | bytes 3145744 | tf_op jit(solution)/shard_map/all_gather | solution.py:46
  304.2 4.7 %fusion.6 = bf16[256,8,384]{0,2,1:T(8,128)(2,1)S(1)} fusion(bf16[256,8,768]{0,2,1:T(8,128)(2,1)} %bitcast.92, bf16[384,8,1,768]{3,0,1,2:T(8,128)(2,1)} %copy.72), kind=kOutput, calls=%fused_computation.5 | convolution fusion | flops 1208745984 | bytes 9437184 | tf_op jit(solution)/shard_map/tjd,cjd->tjc/dot_general | solution.py:47
  308.9 0.3 reduce_sum.31
  309.1 0.3 multiply_reduce_fusion
  309.5 0.1 multiply_convert_fusion
  309.6 0.2 fusion.12
  309.8 0.8 copy.80
  310.6 0.3 fusion.11
  310.9 0.8 copy.81
  311.7 0.6 convolution_convert_fusion.2
  312.4 0.8 copy.82
  313.2 77.7 %reduce-scatter.2.cloned.1.call-done = bf16[256,768]{1,0:T(8,128)(2,1)} async-done(((bf16[256,6144]{1,0:T(8,128)(2,1)}), bf16[256,768]{1,0:T(8,128)(2,1)}) %reduce-scatter.2.cloned.1.call-update) | async-done | bytes 393232 | tf_op jit(solution)/shard_map/reduce_scatter | solution.py:43
Async XLA Ops:
  7.2 33.2 %copy-start = (bf16[256,768]{1,0:T(8,128)(2,1)S(1)}, bf16[256,768]{1,0:T(8,128)(2,1)}, u32[]{:S(2)}) copy-start(bf16[256,768]{1,0:T(8,128)(2,1)} %param.9) | copy-start | bytes 1179652
  7.2 34.2 %copy-start.1 = (bf16[256,384]{1,0:T(8,128)(2,1)S(1)}, bf16[256,384]{1,0:T(8,128)(2,1)}, u32[]{:S(2)}) copy-start(bf16[256,384]{1,0:T(8,128)(2,1)} %param.7) | copy-start | bytes 589828
  7.2 34.3 %copy-start.2 = (bf16[256,384]{1,0:T(8,128)(2,1)S(1)}, bf16[256,384]{1,0:T(8,128)(2,1)}, u32[]{:S(2)}) copy-start(bf16[256,384]{1,0:T(8,128)(2,1)} %param.5) | copy-start | bytes 589828
  7.2 34.5 %copy-start.3 = (bf16[256,384]{1,0:T(8,128)(2,1)S(1)}, bf16[256,384]{1,0:T(8,128)(2,1)}, u32[]{:S(2)}) copy-start(bf16[256,384]{1,0:T(8,128)(2,1)} %param.6) | copy-start | bytes 589828
  7.2 218.7 %all-gather.6.cloned.1.call-start = ((), (), s32[]{:S(2)}) async-start(), calls=%async_computation.4 | async-start | bytes 4755456 | tf_op jit(solution)/shard_map/all_gather | solution.py:39
  40.3 263.9 %all-gather.4.cloned.1.call-start = ((), (), s32[]{:S(2)}) async-start(), calls=%async_computation.3 | async-start | bytes 3538944 | tf_op jit(solution)/shard_map/all_gather | solution.py:46
  41.3 349.6 %reduce-scatter.2.cloned.1.call-start = ((), (), s32[]{:S(2)}) async-start(), calls=%async_computation.2 | async-start | bytes 3538944 | tf_op jit(solution)/shard_map/reduce_scatter | solution.py:43
Sparse Core Ops, SparseCore 0:
  40.4 185.4 all-gather.5
  228.6 75.5 all-gather.3
  308.2 82.6 reduce-scatter.1
where the time goes:
time: 398 us; the launch traced here: 397 us
  waiting for transfers between devices  325 us (82%)
  blocking collectives  25.6 us (6%)
  local copies, waits for them, and re-layouts  19.8 us (5%)
  between operations  13.9 us (3%)
  matrix products  10.7 us (3%)
    all_gather x1, waiting for transfers between devices, on_device(): lax.all_gather(exchanged, 'dp', axis=2, tiled=True)  183 us
    reduce_scatter x1, waiting for transfers between devices, on_device(): lax.psum_scatter(out_terms.astype(jnp.bfloat16), 'mp', scatter_dimension=...  77.7 us
    all_gather x1, waiting for transfers between devices, on_device(): cot_whole = lax.all_gather(cotangent, 'mp', axis=1, tiled=True)  64.7 us
    all_to_all x1, blocking collectives, on_device(): lax.all_to_all(w_out.reshape(w_out.shape[0], 1, shard_width), 'mp', split...  25.6 us
    all_gather x2, local copies, waits for them, and re-layouts, on_device(): lax.all_gather(exchanged, 'dp', axis=2, tiled=True)  10 us
  transfers between devices with their start and end apart: 3, of which 3 were waited for; matrix products, arithmetic and copies ran while one was open for 6% of the time, Pallas kernels for 0%

commit v1 on v0

v1 whole, which is shorter than its diff:
```python
import math

import jax
import jax.numpy as jnp
import numpy as np
from jax import lax
from jax.sharding import Mesh, PartitionSpec as P

HD = 128
SEQ = 256
SIZES = (2, 8, 4, 2, 8)
DP = ("zh", "y", "x", "core")
CZ = ("core", "zl")
BF16 = jnp.bfloat16
F32 = jnp.float32


def shift(block, axis, by):
    n = lax.axis_size(axis)
    return lax.ppermute(block, axis, [(i, (i + by) % n) for i in range(n)])


def ring_gather(block, axis):
    n = lax.axis_size(axis)
    up = down = block
    blocks = [block]
    for step in range(1, n // 2 + 1):
        up = shift(up, axis, 1)
        blocks.append(up)
        if 2 * step < n:
            down = shift(down, axis, -1)
            blocks.append(down)
    return blocks


def ring_offsets(n):
    offsets = [0]
    for step in range(1, n // 2 + 1):
        offsets.append(-step)
        if 2 * step < n:
            offsets.append(step)
    return np.array(offsets)


def feature_of_row(rows_dev):
    nz, ny, nx, nc = (lax.axis_size(a) for a in DP)
    yo, xo = ring_offsets(ny), ring_offsets(nx)
    grid = np.indices((ny, nx, 2, nc, rows_dev)).reshape(5, -1)
    y = (lax.axis_index("y") + jnp.asarray(yo[grid[0]] + ny)) % ny
    x = (lax.axis_index("x") + jnp.asarray(xo[grid[1]] + nx)) % nx
    z = (lax.axis_index("zh") + jnp.asarray(grid[2])) % nz
    return (((z * ny + y) * nx + x) * nc + jnp.asarray(grid[3])) * rows_dev + jnp.asarray(
        grid[4]
    )


def by_core(own, other):
    first = lax.axis_index("core") == 0
    return jnp.where(first, own, other), jnp.where(first, other, own)


def gather_projection(w_out, groups):
    rows_dev = w_out.shape[1]
    width = w_out.shape[0] // groups
    core = lax.axis_index("core")
    shard = w_out.T.reshape(rows_dev, groups, width).transpose(1, 0, 2)
    half = groups // 2
    mine = lax.dynamic_slice_in_dim(shard, core * half, half, 0)
    theirs = lax.dynamic_slice_in_dim(shard, (1 - core) * half, half, 0)
    z_own = shift(mine, "zh", 1)
    nz = lax.axis_size("zh")
    nc = lax.axis_size("core")
    z_cross = lax.ppermute(
        theirs,
        ("zh", "core"),
        [(z * nc + c, ((z + 1) % nz) * nc + 1 - c) for z in range(nz) for c in range(nc)],
    )
    cross = shift(theirs, "core", 1)
    base = jnp.concatenate([*by_core(mine, cross), *by_core(z_own, z_cross)], 1)
    quarter = half // 2
    ny, nx = lax.axis_size("y"), lax.axis_size("x")
    rows = base.shape[1]
    first = jnp.concatenate(ring_gather(base[:quarter], "x"), 1)
    second = jnp.concatenate(ring_gather(base[quarter:], "y"), 1)
    first = jnp.concatenate(ring_gather(first, "y"), 1)
    second = jnp.stack(ring_gather(second, "x"), 1)
    second = (
        second.reshape(quarter, nx, ny, rows, width)
        .transpose(0, 2, 1, 3, 4)
        .reshape(quarter, nx * ny * rows, width)
    )
    first_pair = by_core(first, shift(first, "core", 1))
    second_pair = by_core(second, shift(second, "core", 1))
    return jnp.concatenate([first_pair[0], second_pair[0], first_pair[1], second_pair[1]], 0)


def on_device(queries, keys, values, w_out, cotangent):
    row_count = queries.shape[0]
    group_width = queries.shape[1]
    local_heads = group_width // HD
    n = lax.axis_size("zl")
    me = lax.axis_index("zl")
    core = lax.axis_index("core")
    features = cotangent.shape[1]
    score_scale = 1.0 / math.sqrt(HD)
    heads = (row_count, local_heads, HD)
    query_heads = queries.reshape(heads)
    key_heads = keys.reshape(heads)
    value_heads = values.reshape(heads)

    scores = (
        jnp.einsum("qhd,khd->hqk", query_heads, key_heads, preferred_element_type=F32)
        * score_scale
    )
    softmax_out = jax.nn.softmax(scores, -1)
    softmax_low = softmax_out.astype(BF16)
    head_out = (
        jnp.einsum("hqk,khd->qhd", softmax_low, value_heads, preferred_element_type=F32)
        .astype(BF16)
        .reshape(row_count, group_width)
    )
    heads_all = lax.all_gather(head_out, "zl", axis=1, tiled=True)

    projection = gather_projection(w_out, n)
    order = feature_of_row(w_out.shape[1])
    spread = (order[:, None] == jnp.arange(features)[None, :]).astype(BF16)

    cot_pair = jnp.concatenate(by_core(cotangent, shift(cotangent, "core", 1)), 0)
    cot_pair = lax.dot_general(
        cot_pair, spread, (((1,), (1,)), ((), ())), preferred_element_type=F32
    ).astype(BF16)

    def part(group):
        columns = lax.dynamic_index_in_dim(projection, group % n, 0, keepdims=False)
        return jnp.dot(cot_pair, columns, preferred_element_type=F32).reshape(
            2, row_count, group_width
        )

    sign = 1 - 2 * core
    sums = None
    for step in range(1, n):
        term = part(me + sign * (n - step) + n)
        pairs = [(i, i + 1) for i in range(step)] + [
            (2 * n - 1 - i, 2 * n - 2 - i) for i in range(step)
        ]
        new = []
        for image in range(2):
            total = term[image] if sums is None else sums[image].astype(F32) + term[image]
            new.append(lax.ppermute(total.astype(BF16), CZ, pairs))
        sums = new
    first_sum, second_sum = sums
    own_sum = jnp.where(core == 0, first_sum, second_sum)
    their_sum = jnp.where(core == 0, second_sum, first_sum)
    other_sum = shift(their_sum, "core", 1)
    own_columns = lax.dynamic_index_in_dim(projection, me, 0, keepdims=False)
    own_cot = lax.dynamic_slice_in_dim(cot_pair, core * row_count, row_count, 0)
    own_part = jnp.dot(own_cot, own_columns, preferred_element_type=F32)
    grad_out = (own_part + own_sum.astype(F32) + other_sum.astype(F32)).astype(BF16)

    out_rows = lax.dot_general(
        heads_all.reshape(row_count, n, group_width),
        projection,
        (((1, 2), (0, 2)), ((), ())),
        preferred_element_type=F32,
    ).astype(BF16)
    branch_out = jnp.dot(out_rows, spread, preferred_element_type=F32).astype(BF16)

    grad_heads = grad_out.reshape(heads)
    soft_grad = jnp.einsum("qhd,khd->hqk", grad_heads, value_heads, preferred_element_type=F32)
    score_grad = (
        softmax_out * (soft_grad - jnp.sum(soft_grad * softmax_out, -1, keepdims=True))
    ).astype(BF16)

    def flat(value):
        return value.astype(BF16).reshape(row_count, group_width)

    grad_queries = flat(
        jnp.einsum("hqk,khd->qhd", score_grad, key_heads, preferred_element_type=F32) * score_scale
    )
    grad_keys = flat(
        jnp.einsum("hqk,qhd->khd", score_grad, query_heads, preferred_element_type=F32)
        * score_scale
    )
    grad_values = flat(
        jnp.einsum("hqk,qhd->khd", softmax_low, grad_heads, preferred_element_type=F32)
    )
    return (branch_out, grad_queries, grad_keys, grad_values)


def solution(mesh):
    fine = Mesh(mesh.devices.reshape(SIZES), (*DP, "zl"))
    tokens = P(DP, "zl")
    return jax.shard_map(
        on_device,
        mesh=fine,
        in_specs=(tokens, tokens, tokens, P(None, ("zl", *DP)), tokens),
        out_specs=(tokens, tokens, tokens, tokens),
        check_vma=False,
    )
```

time: 398 us -> 254 us (0.64)
  waiting for transfers between devices: 325 us -> 81.4 us
  starting transfers between devices: 0.12 us -> 124 us
  blocking collectives: 25.6 us -> 0 us
  local copies, waits for them, and re-layouts: 19.8 us -> 6.32 us
  matrix products: 10.7 us -> 17.4 us
  other arithmetic: 1.84 us -> 7.32 us
    all_gather x2 -> x1, waiting for transfers between devices: 248 us -> 0.02 us  [on_device(): heads_all = lax.all_gather(head_out, 'zl', axis=1, tiled=True)]
    ppermute x0 -> x41, starting transfers between devices: none -> 124 us  [the longest x26 107 us: shift(): return lax.ppermute(block, axis, [(i, (i + by) % n) for i in range(n)])]
    ppermute x0 -> x41, waiting for transfers between devices: none -> 81.3 us  [the longest x14 65.8 us: on_device(): new.append(lax.ppermute(total.astype(BF16), CZ, pairs))]
    reduce_scatter x1 -> x0, waiting for transfers between devices: 77.7 us -> none  [on_device(): lax.psum_scatter(out_terms.astype(jnp.bfloat16), 'mp', scatter_dimension=...]
    all_to_all x1 -> x0, blocking collectives: 25.6 us -> none  [on_device(): lax.all_to_all(w_out.reshape(w_out.shape[0], 1, shard_width), 'mp', split...]
    all_gather x2 -> x0, local copies, waits for them, and re-layouts: 10 us -> none  [on_device(): lax.all_gather(exchanged, 'dp', axis=2, tiled=True)]
    dot_general x7 -> x15, matrix products: 10.3 us -> 16.1 us  [the longest x1 5.86 us: on_device(): jnp.dot(out_rows, spread, preferred_element_type=F32).astype(BF16)]
  transfers between devices with their start and end apart: 3 -> 42, of which waited for: 3 -> 6; matrix products, arithmetic and copies ran while one was open for 6% -> 10% of each run, Pallas kernels for 0% -> 0%
where the time goes in v1:
time: 254 us; the launch traced here: 252 us
  starting transfers between devices  124 us (49%)
  waiting for transfers between devices  81.4 us (32%)
  matrix products  17.4 us (7%)
  between operations  15.2 us (6%)
  other arithmetic  7.32 us (3%)
  local copies, waits for them, and re-layouts  6.32 us (2%)
    ppermute x26, starting transfers between devices, shift(): return lax.ppermute(block, axis, [(i, (i + by) % n) for i in range(n)])  107 us
    ppermute x14, waiting for transfers between devices, on_device(): new.append(lax.ppermute(total.astype(BF16), CZ, pairs))  65.8 us
    ppermute x26, waiting for transfers between devices, shift(): return lax.ppermute(block, axis, [(i, (i + by) % n) for i in range(n)])  15.5 us
    ppermute x14, starting transfers between devices, on_device(): new.append(lax.ppermute(total.astype(BF16), CZ, pairs))  10.7 us
    ppermute x1, starting transfers between devices, gather_projection(): lax.ppermute(theirs, ('zh', 'core'), [(z * nc + c, (z + 1) % nz * nc + 1...  6.33 us
    dot_general x1, matrix products, on_device(): jnp.dot(out_rows, spread, preferred_element_type=F32).astype(BF16)  5.86 us
    unnamed x45, local copies, waits for them, and re-layouts  5.3 us
  transfers between devices with their start and end apart: 42, of which 6 were waited for; matrix products, arithmetic and copies ran while one was open for 10% of the time, Pallas kernels for 0%

profile of v1, /device:TPU:1, one launch (start us, length us, event | category | flops | bytes accessed | tf_op | source)
XLA Modules:
  0.0 252.1 jit_solution(13328467319808022200)
XLA Ops:
  7.2 0.8 dynamic-slice_bitcast_fusion
  8.0 16.1 %collective-permute-start = (bf16[4,6,384]{2,1,0:T(8,128)(2,1)S(1)}, bf16[4,6,384]{2,1,0:T(8,128)(2,1)S(1)}, u32[]{:S(2)}, u32[]{:S(2)}) collective-permute-start(bf16[4,6,384]{2,1,0:T(8,128)(2,1)S(1)} %dynamic-slice_bitcast_fusion), channel_id=1, source_target_pairs={{0,8},{8,0},{1,9},{9,1},{2,10},{10,2},{3,11},{11,3},{4,12},{12,4},... | collective-permute-start | bytes 55304 | tf_op jit(solution)/shard_map/ppermute | solution.py:20
  24.1 6.3 %collective-permute-start.2 = (bf16[4,6,384]{2,1,0:T(8,128)(2,1)S(1)}, bf16[4,6,384]{2,1,0:T(8,128)(2,1)S(1)}, u32[]{:S(2)}, u32[]{:S(2)}) collective-permute-start(bf16[4,6,384]{2,1,0:T(8,128)(2,1)S(1)} %dynamic-slice_bitcast_fusion), channel_id=1, source_target_pairs={{0,520},{8,512},{512,8},{520,0},{1,521},{9,513},{513,9},{521,1},{2... | collective-permute-start | bytes 55304 | tf_op jit(solution)/shard_map/ppermute | solution.py:73
  30.4 0.8 broadcast_select_fusion.10
  31.2 7.6 %collective-permute-start.1 = (bf16[4,6,384]{2,1,0:T(8,128)(2,1)S(1)}, bf16[4,6,384]{2,1,0:T(8,128)(2,1)S(1)}, u32[]{:S(2)}, u32[]{:S(2)}) collective-permute-start(bf16[4,6,384]{2,1,0:T(8,128)(2,1)S(1)} %get-tuple-element.13), channel_id=1, source_target_pairs={{0,512},{512,0},{1,513},{513,1},{2,514},{514,2},{3,515},{515,3},{4... | collective-permute-start | bytes 55304 | tf_op jit(solution)/shard_map/ppermute | solution.py:20
  38.8 5.9 %collective-permute-done.1 = bf16[4,6,384]{2,1,0:T(8,128)(2,1)S(1)} collective-permute-done((bf16[4,6,384]{2,1,0:T(8,128)(2,1)S(1)}, bf16[4,6,384]{2,1,0:T(8,128)(2,1)S(1)}, u32[]{:S(2)}, u32[]{:S(2)}) %collective-permute-start.1) | collective-permute-done | bytes 18464 | tf_op jit(solution)/shard_map/ppermute | solution.py:20
  44.8 3.2 %collective-permute-start.3 = (bf16[2,24,384]{2,1,0:T(8,128)(2,1)S(1)}, bf16[2,24,384]{2,1,0:T(8,128)(2,1)S(1)}, u32[]{:S(2)}, u32[]{:S(2)}) collective-permute-start(bf16[2,24,384]{2,1,0:T(8,128)(2,1)S(1)} %get-tuple-element.34), channel_id=1, source_target_pairs={{0,16},{16,32},{32,48},{48,0},{1,17},{17,33},{33,49},{49,1},{2,18}... | collective-permute-start | bytes 110600 | tf_op jit(solution)/shard_map/ppermute | solution.py:20
  47.9 3.6 %collective-permute-start.25 = (bf16[256,768]{1,0:T(8,128)(2,1)}, bf16[256,768]{1,0:T(8,128)(2,1)S(1)}, u32[]{:S(2)}, u32[]{:S(2)}) collective-permute-start(bf16[256,768]{1,0:T(8,128)(2,1)} %param.14), channel_id=1, source_target_pairs={{0,8},{8,0},{1,9},{9,1},{2,10},{10,2},{3,11},{11,3},{4,12},{12,4},... | collective-permute-start | bytes 1179656 | tf_op jit(solution)/shard_map/ppermute | solution.py:20
  51.5 1.1 copy.30
  52.7 3.4 %collective-permute-start.4 = (bf16[2,24,384]{2,1,0:T(8,128)(2,1)S(1)}, bf16[2,24,384]{2,1,0:T(8,128)(2,1)S(1)}, u32[]{:S(2)}, u32[]{:S(2)}) collective-permute-start(bf16[2,24,384]{2,1,0:T(8,128)(2,1)S(1)} %get-tuple-element.34), channel_id=1, source_target_pairs={{0,48},{16,0},{32,16},{48,32},{1,49},{17,1},{33,17},{49,33},{2,50}... | collective-permute-start | bytes 110600 | tf_op jit(solution)/shard_map/ppermute | solution.py:20
  56.1 3.2 %collective-permute-start.14 = (bf16[2,24,384]{2,1,0:T(8,128)(2,1)S(1)}, bf16[2,24,384]{2,1,0:T(8,128)(2,1)S(1)}, u32[]{:S(2)}, u32[]{:S(2)}) collective-permute-start(bf16[2,24,384]{2,1,0:T(8,128)(2,1)S(1)} %get-tuple-element.37), channel_id=1, source_target_pairs={{0,64},{64,128},{128,192},{192,256},{256,320},{320,384},{384,448},... | collective-permute-start | bytes 110600 | tf_op jit(solution)/shard_map/ppermute | solution.py:20
  59.3 3.8 %collective-permute-start.15 = (bf16[2,24,384]{2,1,0:T(8,128)(2,1)S(1)}, bf16[2,24,384]{2,1,0:T(8,128)(2,1)S(1)}, u32[]{:S(2)}, u32[]{:S(2)}) collective-permute-start(bf16[2,24,384]{2,1,0:T(8,128)(2,1)S(1)} %get-tuple-element.37), channel_id=1, source_target_pairs={{0,448},{64,0},{128,64},{192,128},{256,192},{320,256},{384,320},{4... | collective-permute-start | bytes 110600 | tf_op jit(solution)/shard_map/ppermute | solution.py:20
  63.2 1.9 collective-permute-start.5
  65.1 1.9 collective-permute-start.16
  67.1 4.6 %collective-permute-start.17 = (bf16[2,24,384]{2,1,0:T(8,128)(2,1)S(1)}, bf16[2,24,384]{2,1,0:T(8,128)(2,1)S(1)}, u32[]{:S(2)}, u32[]{:S(2)}) collective-permute-start(bf16[2,24,384]{2,1,0:T(8,128)(2,1)S(1)} %collective-permute-done.15), channel_id=1, source_target_pairs={{0,448},{64,0},{128,64},{192,128},{256,192},{320,256},{384,320},{4... | collective-permute-start | bytes 110600 | tf_op jit(solution)/shard_map/ppermute | solution.py:20
  71.7 1.9 collective-permute-start.6
  73.7 4.6 %collective-permute-start.7 = (bf16[2,96,384]{2,1,0:T(8,128)(2,1)S(1)}, bf16[2,96,384]{2,1,0:T(8,128)(2,1)S(1)}, u32[]{:S(2)}, u32[]{:S(2)}) collective-permute-start(bf16[2,96,384]{2,1,0:T(8,128)(2,1)S(1)} %pad_maximum_fusion.2), channel_id=1, source_target_pairs={{0,448},{64,0},{128,64},{192,128},{256,192},{320,256},{384,320},{4... | collective-permute-start | bytes 442376 | tf_op jit(solution)/shard_map/ppermute | solution.py:20
  78.3 1.9 collective-permute-start.18
  80.2 4.6 %collective-permute-start.19 = (bf16[2,24,384]{2,1,0:T(8,128)(2,1)S(1)}, bf16[2,24,384]{2,1,0:T(8,128)(2,1)S(1)}, u32[]{:S(2)}, u32[]{:S(2)}) collective-permute-start(bf16[2,24,384]{2,1,0:T(8,128)(2,1)S(1)} %collective-permute-done.17), channel_id=1, source_target_pairs={{0,448},{64,0},{128,64},{192,128},{256,192},{320,256},{384,320},{4... | collective-permute-start | bytes 110600 | tf_op jit(solution)/shard_map/ppermute | solution.py:20
  84.8 1.9 collective-permute-start.20
  86.8 3.9 %collective-permute-done.20 = bf16[2,24,384]{2,1,0:T(8,128)(2,1)S(1)} collective-permute-done((bf16[2,24,384]{2,1,0:T(8,128)(2,1)S(1)}, bf16[2,24,384]{2,1,0:T(8,128)(2,1)S(1)}, u32[]{:S(2)}, u32[]{:S(2)}) %collective-permute-start.20) | collective-permute-done | bytes 36896 | tf_op jit(solution)/shard_map/ppermute | solution.py:20
  90.8 3.1 %collective-permute-start.21 = (bf16[2,192,384]{2,1,0:T(8,128)(2,1)S(1)}, bf16[2,192,384]{2,1,0:T(8,128)(2,1)S(1)}, u32[]{:S(2)}, u32[]{:S(2)}) collective-permute-start(bf16[2,192,384]{2,1,0:T(8,128)(2,1)S(1)} %constant_dynamic-update-slice_fusion.11), channel_id=1, source_target_pairs={{0,16},{16,32},{32,48},{48,0},{1,17},{17,33},{33,49},{49,1},{2,18}... | collective-permute-start | bytes 884744 | tf_op jit(solution)/shard_map/ppermute | solution.py:20
  93.9 3.4 %collective-permute-start.22 = (bf16[2,192,384]{2,1,0:T(8,128)(2,1)S(1)}, bf16[2,192,384]{2,1,0:T(8,128)(2,1)}, u32[]{:S(2)}, u32[]{:S(2)}) collective-permute-start(bf16[2,192,384]{2,1,0:T(8,128)(2,1)S(1)} %constant_dynamic-update-slice_fusion.11), channel_id=1, source_target_pairs={{0,48},{16,0},{32,16},{48,32},{1,49},{17,1},{33,17},{49,33},{2,50}... | collective-permute-start | bytes 884744 | tf_op jit(solution)/shard_map/ppermute | solution.py:20
  97.3 1.9 collective-permute-start.8
  99.2 4.6 %collective-permute-start.9 = (bf16[2,96,384]{2,1,0:T(8,128)(2,1)S(1)}, bf16[2,96,384]{2,1,0:T(8,128)(2,1)S(1)}, u32[]{:S(2)}, u32[]{:S(2)}) collective-permute-start(bf16[2,96,384]{2,1,0:T(8,128)(2,1)S(1)} %collective-permute-done.7), channel_id=1, source_target_pairs={{0,448},{64,0},{128,64},{192,128},{256,192},{320,256},{384,320},{4... | collective-permute-start | bytes 442376 | tf_op jit(solution)/shard_map/ppermute | solution.py:20
  104.4 1.9 collective-permute-start.10
  106.3 4.7 %collective-permute-start.11 = (bf16[2,96,384]{2,1,0:T(8,128)(2,1)S(1)}, bf16[2,96,384]{2,1,0:T(8,128)(2,1)S(1)}, u32[]{:S(2)}, u32[]{:S(2)}) collective-permute-start(bf16[2,96,384]{2,1,0:T(8,128)(2,1)S(1)} %collective-permute-done.9), channel_id=1, source_target_pairs={{0,448},{64,0},{128,64},{192,128},{256,192},{320,256},{384,320},{4... | collective-permute-start | bytes 442376 | tf_op jit(solution)/shard_map/ppermute | solution.py:20
  111.1 1.9 collective-permute-start.23
  113.1 1.9 collective-permute-start.12
  115.1 5.1 %collective-permute-done.12 = bf16[2,96,384]{2,1,0:T(8,128)(2,1)S(1)} collective-permute-done((bf16[2,96,384]{2,1,0:T(8,128)(2,1)S(1)}, bf16[2,96,384]{2,1,0:T(8,128)(2,1)S(1)}, u32[]{:S(2)}, u32[]{:S(2)}) %collective-permute-start.12) | collective-permute-done | bytes 147488 | tf_op jit(solution)/shard_map/ppermute | solution.py:20
  120.2 9.3 %collective-permute-start.13 = (bf16[2,768,384]{2,1,0:T(8,128)(2,1)S(1)}, bf16[2,768,384]{2,1,0:T(8,128)(2,1)}, u32[]{:S(2)}, u32[]{:S(2)}) collective-permute-start(bf16[2,768,384]{2,1,0:T(8,128)(2,1)S(1)} %constant_dynamic-update-slice_fusion), channel_id=1, source_target_pairs={{0,8},{8,0},{1,9},{9,1},{2,10},{10,2},{3,11},{11,3},{4,12},{12,4},... | collective-permute-start | bytes 3538952 | tf_op jit(solution)/shard_map/ppermute | solution.py:20
  129.5 1.3 fusion.86
  130.8 0.8 copy.34
  131.6 1.3 pad_maximum_fusion.1
  132.9 1.9 collective-permute-start.24
  134.9 2.3 convolution_convert_fusion.1
  137.3 0.7 fusion.69
  138.2 0.9 fusion.4
  139.1 1.5 broadcast_select_fusion.3
  140.6 1.5 broadcast_select_fusion.2
  142.1 0.8 pad_maximum_fusion
  143.6 0.7 collective-permute-start.26
  144.2 0.7 collective-permute-start.33
  145.6 0.7 collective-permute-start.27
  146.3 0.7 collective-permute-start.34
  147.7 0.7 collective-permute-start.28
  148.4 0.7 collective-permute-start.35
  149.7 0.7 collective-permute-start.29
  150.4 0.7 collective-permute-start.36
  151.8 0.7 collective-permute-start.30
  152.5 0.7 collective-permute-start.37
  153.9 0.7 collective-permute-start.31
  154.5 0.7 collective-permute-start.38
  155.9 1.3 collective-permute-start.32
  157.2 1.3 collective-permute-start.39
  158.5 63.7 %collective-permute-done.32 = bf16[256,384]{1,0:T(8,128)(2,1)S(1)} collective-permute-done((bf16[256,384]{1,0:T(8,128)(2,1)S(1)}, bf16[256,384]{1,0:T(8,128)(2,1)S(1)}, u32[]{:S(2)}, u32[]{:S(2)}) %collective-permute-start.32) | collective-permute-done | bytes 196640 | tf_op jit(solution)/shard_map/ppermute | solution.py:149
  222.2 2.1 collective-permute-done.39
  224.4 8.8 %collective-permute-start.40 = (bf16[256,384]{1,0:T(8,128)(2,1)S(1)}, bf16[256,384]{1,0:T(8,128)(2,1)S(1)}, u32[]{:S(2)}, u32[]{:S(2)}) collective-permute-start(bf16[256,384]{1,0:T(8,128)(2,1)S(1)} %broadcast_select_fusion.6), channel_id=1, source_target_pairs={{0,8},{8,0},{1,9},{9,1},{2,10},{10,2},{3,11},{11,3},{4,12},{12,4},... | collective-permute-start | bytes 589832 | tf_op jit(solution)/shard_map/ppermute | solution.py:20
  233.2 5.9 %fusion.7 = bf16[256,768]{1,0:T(8,128)(2,1)} fusion(s32[768]{0:T(1024)S(1)} %copy-done.11, bf16[256,8,384]{0,2,1:T(8,128)(2,1)} %bitcast.122, bf16[8,768,384]{2,1,0:T(8,128)(2,1)} %copy-done), kind=kOutput, calls=%fused_computation.12 | convolution fusion | flops 1510932480 | bytes 6687744 | tf_op jit(solution)/shard_map/dot_general | solution.py:166
  239.0 1.4 fusion.36
  240.6 0.6 convolution_convert_fusion.2
  242.8 0.8 copy.48
  243.6 0.8 copy.47
  244.4 0.8 copy.46
  (107 shorter events, 7.6 us)
Async XLA Ops:
  7.2 45.4 %copy-start.4 = (bf16[256,384]{1,0:T(8,128)(2,1)S(1)}, bf16[256,384]{1,0:T(8,128)(2,1)}, u32[]{:S(2)}) copy-start(bf16[256,384]{1,0:T(8,128)(2,1)} %param.11) | copy-start | bytes 589828
  7.2 226.0 %all-gather.2.cloned.1.call-start = ((), (), s32[]{:S(2)}) async-start(), calls=%async_computation | async-start | bytes 1769472 | tf_op jit(solution)/shard_map/all_gather | solution.py:122
  8.0 22.4 %collective-permute-start = (bf16[4,6,384]{2,1,0:T(8,128)(2,1)S(1)}, bf16[4,6,384]{2,1,0:T(8,128)(2,1)S(1)}, u32[]{:S(2)}, u32[]{:S(2)}) collective-permute-start(bf16[4,6,384]{2,1,0:T(8,128)(2,1)S(1)} %dynamic-slice_bitcast_fusion), channel_id=1, source_target_pairs={{0,8},{8,0},{1,9},{9,1},{2,10},{10,2},{3,11},{11,3},{4,12},{12,4},... | collective-permute-start | bytes 55304 | tf_op jit(solution)/shard_map/ppermute | solution.py:20
  24.1 14.7 %collective-permute-start.2 = (bf16[4,6,384]{2,1,0:T(8,128)(2,1)S(1)}, bf16[4,6,384]{2,1,0:T(8,128)(2,1)S(1)}, u32[]{:S(2)}, u32[]{:S(2)}) collective-permute-start(bf16[4,6,384]{2,1,0:T(8,128)(2,1)S(1)} %dynamic-slice_bitcast_fusion), channel_id=1, source_target_pairs={{0,520},{8,512},{512,8},{520,0},{1,521},{9,513},{513,9},{521,1},{2... | collective-permute-start | bytes 55304 | tf_op jit(solution)/shard_map/ppermute | solution.py:73
  31.2 13.5 %collective-permute-start.1 = (bf16[4,6,384]{2,1,0:T(8,128)(2,1)S(1)}, bf16[4,6,384]{2,1,0:T(8,128)(2,1)S(1)}, u32[]{:S(2)}, u32[]{:S(2)}) collective-permute-start(bf16[4,6,384]{2,1,0:T(8,128)(2,1)S(1)} %get-tuple-element.13), channel_id=1, source_target_pairs={{0,512},{512,0},{1,513},{513,1},{2,514},{514,2},{3,515},{515,3},{4... | collective-permute-start | bytes 55304 | tf_op jit(solution)/shard_map/ppermute | solution.py:20
  44.8 18.4 %collective-permute-start.3 = (bf16[2,24,384]{2,1,0:T(8,128)(2,1)S(1)}, bf16[2,24,384]{2,1,0:T(8,128)(2,1)S(1)}, u32[]{:S(2)}, u32[]{:S(2)}) collective-permute-start(bf16[2,24,384]{2,1,0:T(8,128)(2,1)S(1)} %get-tuple-element.34), channel_id=1, source_target_pairs={{0,16},{16,32},{32,48},{48,0},{1,17},{17,33},{33,49},{49,1},{2,18}... | collective-permute-start | bytes 110600 | tf_op jit(solution)/shard_map/ppermute | solution.py:20
  47.9 90.2 %collective-permute-start.25 = (bf16[256,768]{1,0:T(8,128)(2,1)}, bf16[256,768]{1,0:T(8,128)(2,1)S(1)}, u32[]{:S(2)}, u32[]{:S(2)}) collective-permute-start(bf16[256,768]{1,0:T(8,128)(2,1)} %param.14), channel_id=1, source_target_pairs={{0,8},{8,0},{1,9},{9,1},{2,10},{10,2},{3,11},{11,3},{4,12},{12,4},... | collective-permute-start | bytes 1179656 | tf_op jit(solution)/shard_map/ppermute | solution.py:20
  52.7 18.9 %collective-permute-start.4 = (bf16[2,24,384]{2,1,0:T(8,128)(2,1)S(1)}, bf16[2,24,384]{2,1,0:T(8,128)(2,1)S(1)}, u32[]{:S(2)}, u32[]{:S(2)}) collective-permute-start(bf16[2,24,384]{2,1,0:T(8,128)(2,1)S(1)} %get-tuple-element.34), channel_id=1, source_target_pairs={{0,48},{16,0},{32,16},{48,32},{1,49},{17,1},{33,17},{49,33},{2,50}... | collective-permute-start | bytes 110600 | tf_op jit(solution)/shard_map/ppermute | solution.py:20
  56.1 9.0 %collective-permute-start.14 = (bf16[2,24,384]{2,1,0:T(8,128)(2,1)S(1)}, bf16[2,24,384]{2,1,0:T(8,128)(2,1)S(1)}, u32[]{:S(2)}, u32[]{:S(2)}) collective-permute-start(bf16[2,24,384]{2,1,0:T(8,128)(2,1)S(1)} %get-tuple-element.37), channel_id=1, source_target_pairs={{0,64},{64,128},{128,192},{192,256},{256,320},{320,384},{384,448},... | collective-permute-start | bytes 110600 | tf_op jit(solution)/shard_map/ppermute | solution.py:20
  59.3 7.7 %collective-permute-start.15 = (bf16[2,24,384]{2,1,0:T(8,128)(2,1)S(1)}, bf16[2,24,384]{2,1,0:T(8,128)(2,1)S(1)}, u32[]{:S(2)}, u32[]{:S(2)}) collective-permute-start(bf16[2,24,384]{2,1,0:T(8,128)(2,1)S(1)} %get-tuple-element.37), channel_id=1, source_target_pairs={{0,448},{64,0},{128,64},{192,128},{256,192},{320,256},{384,320},{4... | collective-permute-start | bytes 110600 | tf_op jit(solution)/shard_map/ppermute | solution.py:20
  63.2 8.5 %collective-permute-start.5 = (bf16[2,24,384]{2,1,0:T(8,128)(2,1)S(1)}, bf16[2,24,384]{2,1,0:T(8,128)(2,1)S(1)}, u32[]{:S(2)}, u32[]{:S(2)}) collective-permute-start(bf16[2,24,384]{2,1,0:T(8,128)(2,1)S(1)} %collective-permute-done.3), channel_id=1, source_target_pairs={{0,16},{16,32},{32,48},{48,0},{1,17},{17,33},{33,49},{49,1},{2,18}... | collective-permute-start | bytes 110600 | tf_op jit(solution)/shard_map/ppermute | solution.py:20
  65.1 13.1 %collective-permute-start.16 = (bf16[2,24,384]{2,1,0:T(8,128)(2,1)S(1)}, bf16[2,24,384]{2,1,0:T(8,128)(2,1)S(1)}, u32[]{:S(2)}, u32[]{:S(2)}) collective-permute-start(bf16[2,24,384]{2,1,0:T(8,128)(2,1)S(1)} %collective-permute-done.14), channel_id=1, source_target_pairs={{0,64},{64,128},{128,192},{192,256},{256,320},{320,384},{384,448},... | collective-permute-start | bytes 110600 | tf_op jit(solution)/shard_map/ppermute | solution.py:20
  67.1 13.1 %collective-permute-start.17 = (bf16[2,24,384]{2,1,0:T(8,128)(2,1)S(1)}, bf16[2,24,384]{2,1,0:T(8,128)(2,1)S(1)}, u32[]{:S(2)}, u32[]{:S(2)}) collective-permute-start(bf16[2,24,384]{2,1,0:T(8,128)(2,1)S(1)} %collective-permute-done.15), channel_id=1, source_target_pairs={{0,448},{64,0},{128,64},{192,128},{256,192},{320,256},{384,320},{4... | collective-permute-start | bytes 110600 | tf_op jit(solution)/shard_map/ppermute | solution.py:20
  71.7 25.5 %collective-permute-start.6 = (bf16[2,96,384]{2,1,0:T(8,128)(2,1)S(1)}, bf16[2,96,384]{2,1,0:T(8,128)(2,1)S(1)}, u32[]{:S(2)}, u32[]{:S(2)}) collective-permute-start(bf16[2,96,384]{2,1,0:T(8,128)(2,1)S(1)} %pad_maximum_fusion.2), channel_id=1, source_target_pairs={{0,64},{64,128},{128,192},{192,256},{256,320},{320,384},{384,448},... | collective-permute-start | bytes 442376 | tf_op jit(solution)/shard_map/ppermute | solution.py:20
  73.7 25.6 %collective-permute-start.7 = (bf16[2,96,384]{2,1,0:T(8,128)(2,1)S(1)}, bf16[2,96,384]{2,1,0:T(8,128)(2,1)S(1)}, u32[]{:S(2)}, u32[]{:S(2)}) collective-permute-start(bf16[2,96,384]{2,1,0:T(8,128)(2,1)S(1)} %pad_maximum_fusion.2), channel_id=1, source_target_pairs={{0,448},{64,0},{128,64},{192,128},{256,192},{320,256},{384,320},{4... | collective-permute-start | bytes 442376 | tf_op jit(solution)/shard_map/ppermute | solution.py:20
  78.3 6.6 %collective-permute-start.18 = (bf16[2,24,384]{2,1,0:T(8,128)(2,1)S(1)}, bf16[2,24,384]{2,1,0:T(8,128)(2,1)S(1)}, u32[]{:S(2)}, u32[]{:S(2)}) collective-permute-start(bf16[2,24,384]{2,1,0:T(8,128)(2,1)S(1)} %collective-permute-done.16), channel_id=1, source_target_pairs={{0,64},{64,128},{128,192},{192,256},{256,320},{320,384},{384,448},... | collective-permute-start | bytes 110600 | tf_op jit(solution)/shard_map/ppermute | solution.py:20
  80.2 6.6 %collective-permute-start.19 = (bf16[2,24,384]{2,1,0:T(8,128)(2,1)S(1)}, bf16[2,24,384]{2,1,0:T(8,128)(2,1)S(1)}, u32[]{:S(2)}, u32[]{:S(2)}) collective-permute-start(bf16[2,24,384]{2,1,0:T(8,128)(2,1)S(1)} %collective-permute-done.17), channel_id=1, source_target_pairs={{0,448},{64,0},{128,64},{192,128},{256,192},{320,256},{384,320},{4... | collective-permute-start | bytes 110600 | tf_op jit(solution)/shard_map/ppermute | solution.py:20
  84.8 5.9 %collective-permute-start.20 = (bf16[2,24,384]{2,1,0:T(8,128)(2,1)S(1)}, bf16[2,24,384]{2,1,0:T(8,128)(2,1)S(1)}, u32[]{:S(2)}, u32[]{:S(2)}) collective-permute-start(bf16[2,24,384]{2,1,0:T(8,128)(2,1)S(1)} %collective-permute-done.18), channel_id=1, source_target_pairs={{0,64},{64,128},{128,192},{192,256},{256,320},{320,384},{384,448},... | collective-permute-start | bytes 110600 | tf_op jit(solution)/shard_map/ppermute | solution.py:20
  90.8 20.3 %collective-permute-start.21 = (bf16[2,192,384]{2,1,0:T(8,128)(2,1)S(1)}, bf16[2,192,384]{2,1,0:T(8,128)(2,1)S(1)}, u32[]{:S(2)}, u32[]{:S(2)}) collective-permute-start(bf16[2,192,384]{2,1,0:T(8,128)(2,1)S(1)} %constant_dynamic-update-slice_fusion.11), channel_id=1, source_target_pairs={{0,16},{16,32},{32,48},{48,0},{1,17},{17,33},{33,49},{49,1},{2,18}... | collective-permute-start | bytes 884744 | tf_op jit(solution)/shard_map/ppermute | solution.py:20
  93.9 37.7 %collective-permute-start.22 = (bf16[2,192,384]{2,1,0:T(8,128)(2,1)S(1)}, bf16[2,192,384]{2,1,0:T(8,128)(2,1)}, u32[]{:S(2)}, u32[]{:S(2)}) collective-permute-start(bf16[2,192,384]{2,1,0:T(8,128)(2,1)S(1)} %constant_dynamic-update-slice_fusion.11), channel_id=1, source_target_pairs={{0,48},{16,0},{32,16},{48,32},{1,49},{17,1},{33,17},{49,33},{2,50}... | collective-permute-start | bytes 884744 | tf_op jit(solution)/shard_map/ppermute | solution.py:20
  97.3 7.1 %collective-permute-start.8 = (bf16[2,96,384]{2,1,0:T(8,128)(2,1)S(1)}, bf16[2,96,384]{2,1,0:T(8,128)(2,1)S(1)}, u32[]{:S(2)}, u32[]{:S(2)}) collective-permute-start(bf16[2,96,384]{2,1,0:T(8,128)(2,1)S(1)} %collective-permute-done.6), channel_id=1, source_target_pairs={{0,64},{64,128},{128,192},{192,256},{256,320},{320,384},{384,448},... | collective-permute-start | bytes 442376 | tf_op jit(solution)/shard_map/ppermute | solution.py:20
  99.2 7.1 %collective-permute-start.9 = (bf16[2,96,384]{2,1,0:T(8,128)(2,1)S(1)}, bf16[2,96,384]{2,1,0:T(8,128)(2,1)S(1)}, u32[]{:S(2)}, u32[]{:S(2)}) collective-permute-start(bf16[2,96,384]{2,1,0:T(8,128)(2,1)S(1)} %collective-permute-done.7), channel_id=1, source_target_pairs={{0,448},{64,0},{128,64},{192,128},{256,192},{320,256},{384,320},{4... | collective-permute-start | bytes 442376 | tf_op jit(solution)/shard_map/ppermute | solution.py:20
  104.4 8.7 %collective-permute-start.10 = (bf16[2,96,384]{2,1,0:T(8,128)(2,1)S(1)}, bf16[2,96,384]{2,1,0:T(8,128)(2,1)S(1)}, u32[]{:S(2)}, u32[]{:S(2)}) collective-permute-start(bf16[2,96,384]{2,1,0:T(8,128)(2,1)S(1)} %collective-permute-done.8), channel_id=1, source_target_pairs={{0,64},{64,128},{128,192},{192,256},{256,320},{320,384},{384,448},... | collective-permute-start | bytes 442376 | tf_op jit(solution)/shard_map/ppermute | solution.py:20
  106.3 24.4 %copy-start.5 = (bf16[256,384]{1,0:T(8,128)(2,1)S(1)}, bf16[256,384]{1,0:T(8,128)(2,1)}, u32[]{:S(2)}) copy-start(bf16[256,384]{1,0:T(8,128)(2,1)} %param.12) | copy-start | bytes 589828
  106.3 8.7 %collective-permute-start.11 = (bf16[2,96,384]{2,1,0:T(8,128)(2,1)S(1)}, bf16[2,96,384]{2,1,0:T(8,128)(2,1)S(1)}, u32[]{:S(2)}, u32[]{:S(2)}) collective-permute-start(bf16[2,96,384]{2,1,0:T(8,128)(2,1)S(1)} %collective-permute-done.9), channel_id=1, source_target_pairs={{0,448},{64,0},{128,64},{192,128},{256,192},{320,256},{384,320},{4... | collective-permute-start | bytes 442376 | tf_op jit(solution)/shard_map/ppermute | solution.py:20
  111.1 20.5 %copy-start.3 = (bf16[2,192,384]{2,1,0:T(8,128)(2,1)}, bf16[2,192,384]{2,1,0:T(8,128)(2,1)S(1)}, u32[]{:S(2)}) copy-start(bf16[2,192,384]{2,1,0:T(8,128)(2,1)S(1)} %collective-permute-done.21) | copy-start | bytes 884740
  111.1 20.5 %collective-permute-start.23 = (bf16[2,192,384]{2,1,0:T(8,128)(2,1)S(1)}, bf16[2,192,384]{2,1,0:T(8,128)(2,1)}, u32[]{:S(2)}, u32[]{:S(2)}) collective-permute-start(bf16[2,192,384]{2,1,0:T(8,128)(2,1)S(1)} %collective-permute-done.21), channel_id=1, source_target_pairs={{0,16},{16,32},{32,48},{48,0},{1,17},{17,33},{33,49},{49,1},{2,18}... | collective-permute-start | bytes 884744 | tf_op jit(solution)/shard_map/ppermute | solution.py:20
  113.1 7.1 %collective-permute-start.12 = (bf16[2,96,384]{2,1,0:T(8,128)(2,1)S(1)}, bf16[2,96,384]{2,1,0:T(8,128)(2,1)S(1)}, u32[]{:S(2)}, u32[]{:S(2)}) collective-permute-start(bf16[2,96,384]{2,1,0:T(8,128)(2,1)S(1)} %collective-permute-done.10), channel_id=1, source_target_pairs={{0,64},{64,128},{128,192},{192,256},{256,320},{320,384},{384,448},... | collective-permute-start | bytes 442376 | tf_op jit(solution)/shard_map/ppermute | solution.py:20
  120.2 18.9 %collective-permute-start.13 = (bf16[2,768,384]{2,1,0:T(8,128)(2,1)S(1)}, bf16[2,768,384]{2,1,0:T(8,128)(2,1)}, u32[]{:S(2)}, u32[]{:S(2)}) collective-permute-start(bf16[2,768,384]{2,1,0:T(8,128)(2,1)S(1)} %constant_dynamic-update-slice_fusion), channel_id=1, source_target_pairs={{0,8},{8,0},{1,9},{9,1},{2,10},{10,2},{3,11},{11,3},{4,12},{12,4},... | collective-permute-start | bytes 3538952 | tf_op jit(solution)/shard_map/ppermute | solution.py:20
  132.9 7.7 %collective-permute-start.24 = (bf16[2,768,384]{2,1,0:T(8,128)(2,1)S(1)}, bf16[2,768,384]{2,1,0:T(8,128)(2,1)}, u32[]{:S(2)}, u32[]{:S(2)}) collective-permute-start(bf16[2,768,384]{2,1,0:T(8,128)(2,1)S(1)} %bitcast.101), channel_id=1, source_target_pairs={{0,8},{8,0},{1,9},{9,1},{2,10},{10,2},{3,11},{11,3},{4,12},{12,4},... | collective-permute-start | bytes 3538952 | tf_op jit(solution)/shard_map/ppermute | solution.py:20
  134.8 2.5 copy-start.7
  134.9 2.5 copy-start.8
  134.9 2.5 copy-start.9
  134.9 3.2 %copy-start.2 = (bf16[256,768]{1,0:T(8,128)(2,1)S(1)}, bf16[256,768]{1,0:T(8,128)(2,1)}, u32[]{:S(2)}) copy-start(bf16[256,768]{1,0:T(8,128)(2,1)} %param.14) | copy-start | bytes 1179652
  138.1 1.0 copy-start.10
  142.9 12.3 %copy-start = (bf16[8,768,384]{2,1,0:T(8,128)(2,1)}, bf16[8,768,384]{2,1,0:T(8,128)(2,1)S(1)}, u32[]{:S(2)}) copy-start(bf16[8,768,384]{2,1,0:T(8,128)(2,1)S(1)} %pad_maximum_fusion) | copy-start | bytes 14155780
  143.6 2.0 collective-permute-start.26
  144.2 1.3 collective-permute-start.33
  145.6 2.0 collective-permute-start.27
  146.3 1.3 collective-permute-start.34
  147.7 2.0 collective-permute-start.28
  148.4 1.3 collective-permute-start.35
  149.7 2.0 collective-permute-start.29
  150.4 1.3 collective-permute-start.36
  151.8 2.0 collective-permute-start.30
  152.5 1.3 collective-permute-start.37
  153.9 2.0 collective-permute-start.31
  154.5 1.3 collective-permute-start.38
  155.8 77.3 %copy-start.11 = (s32[768]{0:T(1024)S(1)}, s32[768]{0:T(1024)}, u32[]{:S(2)}) copy-start(s32[768]{0:T(1024)} %copy-done.10) | copy-start | bytes 9220
  155.9 66.3 %collective-permute-start.32 = (bf16[256,384]{1,0:T(8,128)(2,1)S(1)}, bf16[256,384]{1,0:T(8,128)(2,1)S(1)}, u32[]{:S(2)}, u32[]{:S(2)}) collective-permute-start(bf16[256,384]{1,0:T(8,128)(2,1)S(1)} %get-tuple-element.18), channel_id=1, source_target_pairs={{0,1},{1,2},{2,3},{3,4},{4,5},{5,6},{6,7},{15,14},{14,13},{13,12},... | collective-permute-start | bytes 589832 | tf_op jit(solution)/shard_map/ppermute | solution.py:149
  157.2 67.1 %collective-permute-start.39 = (bf16[256,384]{1,0:T(8,128)(2,1)S(1)}, bf16[256,384]{1,0:T(8,128)(2,1)S(1)}, u32[]{:S(2)}, u32[]{:S(2)}) collective-permute-start(bf16[256,384]{1,0:T(8,128)(2,1)S(1)} %get-tuple-element.19), channel_id=1, source_target_pairs={{0,1},{1,2},{2,3},{3,4},{4,5},{5,6},{6,7},{15,14},{14,13},{13,12},... | collective-permute-start | bytes 589832 | tf_op jit(solution)/shard_map/ppermute | solution.py:149
  224.4 14.7 %collective-permute-start.40 = (bf16[256,384]{1,0:T(8,128)(2,1)S(1)}, bf16[256,384]{1,0:T(8,128)(2,1)S(1)}, u32[]{:S(2)}, u32[]{:S(2)}) collective-permute-start(bf16[256,384]{1,0:T(8,128)(2,1)S(1)} %broadcast_select_fusion.6), channel_id=1, source_target_pairs={{0,8},{8,0},{1,9},{9,1},{2,10},{10,2},{3,11},{11,3},{4,12},{12,4},... | collective-permute-start | bytes 589832 | tf_op jit(solution)/shard_map/ppermute | solution.py:20
  240.6 1.1 copy-start.1
  240.6 1.2 copy-start.6
Sparse Core Ops, SparseCore 0:
  137.3 68.7 all-gather.1

commit v2 on v1

v2 whole, which is shorter than its diff:
```python
import math

import jax
import jax.numpy as jnp
import numpy as np
from jax import lax
from jax.sharding import Mesh, PartitionSpec as P

HD = 128
SEQ = 256
SIZES = (2, 8, 4, 2, 8)
DP = ("zh", "y", "x", "core")
BF16 = jnp.bfloat16
F32 = jnp.float32


def folded(n):
    return [*range(0, n, 2), *reversed(range(1, n, 2))]


def swap_core(block):
    return lax.ppermute(block, "core", [(0, 1), (1, 0)])


def by_core(own, other):
    first = lax.axis_index("core") == 0
    return jnp.where(first, own, other), jnp.where(first, other, own)


def feature_of_row(rows_dev):
    nz, ny, nx, nc = (lax.axis_size(a) for a in DP)
    y, z, x, c, r = np.indices((ny, nz, nx, nc, rows_dev)).reshape(5, -1)
    return (((z * ny + y) * nx + x) * nc + c) * rows_dev + r


def gather_projection(w_out):
    near = lax.all_gather(w_out.T, ("zh", "x", "core"), axis=0, tiled=True)
    half = near.shape[1] // 2
    mine = lax.dynamic_slice_in_dim(near, lax.axis_index("core") * half, half, 1)
    whole = lax.all_gather(mine, "y", axis=0, tiled=True)
    return jnp.concatenate(by_core(whole, swap_core(whole)), 1)


def on_device(queries, keys, values, w_out, cotangent):
    row_count = queries.shape[0]
    group_width = queries.shape[1]
    local_heads = group_width // HD
    n = lax.axis_size("zl")
    features = cotangent.shape[1]
    score_scale = 1.0 / math.sqrt(HD)
    heads = (row_count, local_heads, HD)
    query_heads = queries.reshape(heads)
    key_heads = keys.reshape(heads)
    value_heads = values.reshape(heads)

    scores = (
        jnp.einsum("qhd,khd->hqk", query_heads, key_heads, preferred_element_type=F32)
        * score_scale
    )
    softmax_out = jax.nn.softmax(scores, -1)
    softmax_low = softmax_out.astype(BF16)
    head_out = (
        jnp.einsum("hqk,khd->qhd", softmax_low, value_heads, preferred_element_type=F32)
        .astype(BF16)
        .reshape(row_count, group_width)
    )
    line = folded(n)
    heads_all = lax.all_gather(head_out, "zl", axis=1, tiled=True, axis_index_groups=[line])

    projection = gather_projection(w_out)
    order = jnp.asarray(feature_of_row(w_out.shape[1]))
    spread = (order[:, None] == jnp.arange(features)[None, :]).astype(BF16)
    cot_rows = lax.dot_general(
        cotangent, spread, (((1,), (1,)), ((), ())), preferred_element_type=F32
    ).astype(BF16)

    terms = jnp.dot(cot_rows, projection, preferred_element_type=F32).astype(BF16)
    terms = jnp.stack([terms[:, g * group_width : (g + 1) * group_width] for g in line], 0)
    grad_out = lax.psum_scatter(
        terms, "zl", scatter_dimension=0, tiled=False, axis_index_groups=[line]
    )

    heads_all = jnp.concatenate(
        [
            heads_all[:, line.index(g) * group_width : (line.index(g) + 1) * group_width]
            for g in range(n)
        ],
        1,
    )
    out_rows = lax.dot_general(
        heads_all, projection, (((1,), (1,)), ((), ())), preferred_element_type=F32
    ).astype(BF16)
    branch_out = jnp.dot(out_rows, spread, preferred_element_type=F32).astype(BF16)

    grad_heads = grad_out.reshape(heads)
    soft_grad = jnp.einsum("qhd,khd->hqk", grad_heads, value_heads, preferred_element_type=F32)
    score_grad = (
        softmax_out * (soft_grad - jnp.sum(soft_grad * softmax_out, -1, keepdims=True))
    ).astype(BF16)

    def flat(value):
        return value.astype(BF16).reshape(row_count, group_width)

    grad_queries = flat(
        jnp.einsum("hqk,khd->qhd", score_grad, key_heads, preferred_element_type=F32) * score_scale
    )
    grad_keys = flat(
        jnp.einsum("hqk,qhd->khd", score_grad, query_heads, preferred_element_type=F32)
        * score_scale
    )
    grad_values = flat(
        jnp.einsum("hqk,qhd->khd", softmax_low, grad_heads, preferred_element_type=F32)
    )
    return (branch_out, grad_queries, grad_keys, grad_values)


def solution(mesh):
    fine = Mesh(mesh.devices.reshape(SIZES), (*DP, "zl"))
    tokens = P(DP, "zl")
    return jax.shard_map(
        on_device,
        mesh=fine,
        in_specs=(tokens, tokens, tokens, P(None, ("zl", *DP)), tokens),
        out_specs=(tokens, tokens, tokens, tokens),
        check_vma=False,
    )
```

time: 254 us -> 250 us (0.984)
  starting transfers between devices: 124 us -> 5.81 us
  blocking collectives: 0 us -> 62.7 us
  waiting for transfers between devices: 81.4 us -> 114 us
  local copies, waits for them, and re-layouts: 6.32 us -> 29.8 us
  other arithmetic: 7.32 us -> 4.22 us
  matrix products: 17.4 us -> 14.6 us
    ppermute x41 -> x1, starting transfers between devices: 124 us -> 5.69 us  [swap_core(): return lax.ppermute(block, 'core', [(0, 1), (1, 0)])]
    ppermute x41 -> x1, waiting for transfers between devices: 81.3 us -> 1.23 us  [swap_core(): return lax.ppermute(block, 'core', [(0, 1), (1, 0)])]
    all_gather x1 -> x2, waiting for transfers between devices: 0.02 us -> 71.8 us  [the longest x1 42.1 us: gather_projection(): whole = lax.all_gather(mine, 'y', axis=0, tiled=True)]
    all_gather x0 -> x1, blocking collectives: none -> 62.7 us  [gather_projection(): near = lax.all_gather(w_out.T, ('zh', 'x', 'core'), axis=0, tiled=True)]
    reduce_scatter x0 -> x1, waiting for transfers between devices: none -> 41.1 us  [on_device(): lax.psum_scatter(terms, 'zl', scatter_dimension=0, tiled=False, axis_inde...]
    unnamed x45 -> x32, local copies, waits for them, and re-layouts: 5.3 us -> 24.7 us
    dot_general x9 -> x1, matrix products: 6.46 us -> 5.22 us  [on_device(): jnp.dot(cot_rows, projection, preferred_element_type=F32).astype(BF16)]
  transfers between devices with their start and end apart: 42 -> 4, of which waited for: 6 -> 4; matrix products, arithmetic and copies ran while one was open for 10% -> 17% of each run, Pallas kernels for 0% -> 0%
where the time goes in v2:
time: 250 us; the launch traced here: 247 us
  waiting for transfers between devices  114 us (46%)
  blocking collectives  62.7 us (25%)
  local copies, waits for them, and re-layouts  29.8 us (12%)
  between operations  15.6 us (6%)
  matrix products  14.6 us (6%)
  starting transfers between devices  5.81 us (2%)
  other arithmetic  4.22 us (2%)
    all_gather x1, blocking collectives, gather_projection(): near = lax.all_gather(w_out.T, ('zh', 'x', 'core'), axis=0, tiled=True)  62.7 us
    all_gather x1, waiting for transfers between devices, gather_projection(): whole = lax.all_gather(mine, 'y', axis=0, tiled=True)  42.1 us
    reduce_scatter x1, waiting for transfers between devices, on_device(): lax.psum_scatter(terms, 'zl', scatter_dimension=0, tiled=False, axis_inde...  41.1 us
    all_gather x1, waiting for transfers between devices, on_device(): lax.all_gather(head_out, 'zl', axis=1, tiled=True, axis_index_groups=[line])  29.8 us
    unnamed x32, local copies, waits for them, and re-layouts  24.7 us
    ppermute x1, starting transfers between devices, swap_core(): return lax.ppermute(block, 'core', [(0, 1), (1, 0)])  5.69 us
    dot_general x1, matrix products, on_device(): jnp.dot(cot_rows, projection, preferred_element_type=F32).astype(BF16)  5.22 us
    dot_general x1, matrix products, on_device(): jnp.dot(out_rows, spread, preferred_element_type=F32).astype(BF16)  5.19 us
  transfers between devices with their start and end apart: 4, of which 4 were waited for; matrix products, arithmetic and copies ran while one was open for 17% of the time, Pallas kernels for 0%

profile of v2, /device:TPU:1, one launch (start us, length us, event | category | flops | bytes accessed | tf_op | source)
XLA Modules:
  0.0 247.0 jit_solution(8041424749918236702)
XLA Ops:
  8.0 0.0 copy-start
  8.0 0.0 copy-start.2
  8.0 0.0 all-gather.6.cloned.1.call-start
  8.1 0.0 copy-start.3
  8.1 62.7 %all-gather = bf16[16,6,3072]{2,1,0:T(8,128)(2,1)S(1)} all-gather(bf16[1,6,3072]{2,1,0:T(8,128)(2,1)} %bitcast.83), channel_id=1, replica_groups=mesh['zh'=2,'y'=8,'x'=4,'core'=2,'zl'=8] {'zh','x','core'}, dimensions={0}, use_global_device_ids=true | all-gather | bytes 626688 | tf_op jit(solution)/shard_map/all_gather | solution.py:37
  70.8 0.0 copy-start.4
  70.8 0.2 reshape.41
  71.0 0.7 constant_dynamic-slice_fusion
  71.7 0.0 all-gather.6.cloned.1.call-update
  71.7 0.0 all-gather.4.cloned.1.call-start
  71.8 42.1 %all-gather.6.cloned.1.call-done = bf16[768,1536]{1,0:T(8,128)(2,1)} async-done(((bf16[96,1536]{1,0:T(8,128)(2,1)}), bf16[768,1536]{1,0:T(8,128)(2,1)}) %all-gather.6.cloned.1.call-update) | async-done | bytes 2359312 | tf_op jit(solution)/shard_map/all_gather | solution.py:40
  113.8 5.7 %collective-permute-start = (bf16[768,1536]{1,0:T(8,128)(2,1)}, bf16[768,1536]{1,0:T(8,128)(2,1)}, u32[]{:S(2)}, u32[]{:S(2)}) collective-permute-start(bf16[768,1536]{1,0:T(8,128)(2,1)} %all-gather.6.cloned.1.call-done), channel_id=1, source_target_pairs={{0,8},{8,0},{1,9},{9,1},{2,10},{10,2},{3,11},{11,3},{4,12},{12,4},... | collective-permute-start | bytes 7077896 | tf_op jit(solution)/shard_map/ppermute | solution.py:22
  119.5 0.0 copy-done.2
  119.6 0.1 copy.40
  119.7 0.0 copy-done.3
  119.7 0.1 copy.41
  119.9 0.0 copy-done.4
  119.9 0.1 copy.44
  120.0 1.4 fusion.28
  121.4 1.3 convolution_convert_fusion.1
  122.7 0.0 all-gather.4.cloned.1.call-update
  122.7 0.0 reduce-scatter.2.cloned.1.call-start
  122.8 0.0 copy-start.5
  122.8 1.2 collective-permute-done
  124.0 4.1 %broadcast_select_fusion.1 = (bf16[768,1536]{1,0:T(8,128)(2,1)S(1)}, bf16[768,1536]{1,0:T(8,128)(2,1)}) fusion(bf16[768,1536]{1,0:T(8,128)(2,1)} %all-gather.6.cloned.1.call-done, bf16[768,1536]{1,0:T(8,128)(2,1)} %collective-permute-done, pred[]{:T(512)S(6)} %eq.16), kind=kLoop, calls=%fused_computation.8 | loop fusion | flops 2359296 | bytes 9437185 | tf_op jit(solution)/shard_map/jit(_where)/select_n | solution.py:27
  128.1 0.0 copy-done
  128.1 0.0 copy-done.5
  128.1 5.2 %convolution_convert_fusion = bf16[256,3072]{1,0:T(8,128)(2,1)} fusion(bf16[768,1536]{1,0:T(8,128)(2,1)} %get-tuple-element.17, bf16[768,1536]{1,0:T(8,128)(2,1)S(1)} %get-tuple-element.16, bf16[256,768]{1,0:T(8,128)(2,1)S(1)} %copy-done, s32[768]{0:T(1024)S(1)} %copy-done.5), kind=kOutput, calls=%fused_computation.2 | convolution fusion | flops 1520959488 | bytes 6687744 | tf_op jit(solution)/shard_map/dot_general | solution.py:77
  133.4 1.6 fusion.20
  135.0 1.6 fusion.19
  136.6 1.6 fusion.18
  138.2 1.6 fusion.17
  139.8 1.6 fusion.16
  141.5 1.6 fusion.15
  143.1 1.6 fusion.14
  144.7 1.6 fusion.13
  146.3 0.0 reduce-scatter.2.cloned.1.call-update
  146.4 29.8 %all-gather.4.cloned.1.call-done = bf16[256,3072]{0,1:T(8,128)(2,1)} async-done(((bf16[256,384]{0,1:T(8,128)(2,1)}), bf16[256,3072]{0,1:T(8,128)(2,1)}) %all-gather.4.cloned.1.call-update) | async-done | bytes 1572880 | tf_op jit(solution)/shard_map/all_gather | solution.py:68
  176.1 1.6 slice_dynamic-update-slice_fusion.6
  177.7 1.6 slice_dynamic-update-slice_fusion.5
  179.3 1.6 slice_dynamic-update-slice_fusion.4
  181.0 1.6 slice_dynamic-update-slice_fusion.3
  182.6 1.6 slice_dynamic-update-slice_fusion.2
  184.2 1.6 slice_dynamic-update-slice_fusion.1
  185.8 1.8 slice_dynamic-update-slice_fusion
  187.6 5.2 %fusion.7 = bf16[256,768]{1,0:T(8,128)(2,1)} fusion(s32[768]{0:T(1024)S(1)} %copy-done.5, bf16[256,3072]{0,1:T(8,128)(2,1)} %slice_dynamic-update-slice_fusion, bf16[768,1536]{1,0:T(8,128)(2,1)} %get-tuple-element.17, bf16[768,1536]{1,0:T(8,128)(2,1)S(1)} %get-tuple-element.16), kind=kOutput, calls=%fused_computation.13 | convolution fusion | flops 1520369664 | bytes 6687744 | tf_op jit(solution)/shard_map/dot_general | solution.py:93
  192.8 41.1 %reduce-scatter.2.cloned.1.call-done = bf16[1,256,384]{2,1,0:T(8,128)(2,1)} async-done(((bf16[8,256,384]{2,1,0:T(8,128)(2,1)}), bf16[1,256,384]{2,1,0:T(8,128)(2,1)}) %reduce-scatter.2.cloned.1.call-update) | async-done | bytes 196624 | tf_op jit(solution)/shard_map/reduce_scatter | solution.py:79
  233.9 1.1 copy.46
  235.0 0.0 copy-start.1
  235.0 0.6 convolution_convert_fusion.2
  235.6 0.5 copy-done.1
  236.1 0.3 multiply_reduce_fusion
  236.4 0.1 multiply_convert_fusion
  236.6 0.3 fusion.11
  236.9 0.2 fusion.12
  237.1 0.8 copy.54
  237.9 0.8 copy.53
  238.7 0.8 copy.52
Async XLA Ops:
  8.0 120.1 %copy-start = (bf16[256,768]{1,0:T(8,128)(2,1)S(1)}, bf16[256,768]{1,0:T(8,128)(2,1)}, u32[]{:S(2)}) copy-start(bf16[256,768]{1,0:T(8,128)(2,1)} %param.10) | copy-start | bytes 1179652
  8.0 111.5 %copy-start.2 = (bf16[256,384]{1,0:T(8,128)(2,1)S(1)}, bf16[256,384]{1,0:T(8,128)(2,1)}, u32[]{:S(2)}) copy-start(bf16[256,384]{1,0:T(8,128)(2,1)} %param.6) | copy-start | bytes 589828
  8.0 105.8 %all-gather.6.cloned.1.call-start = ((), (), s32[]{:S(2)}) async-start(), calls=%async_computation.2 | async-start | bytes 2654208 | tf_op jit(solution)/shard_map/all_gather | solution.py:40
  8.1 111.6 %copy-start.3 = (bf16[256,384]{1,0:T(8,128)(2,1)S(1)}, bf16[256,384]{1,0:T(8,128)(2,1)}, u32[]{:S(2)}) copy-start(bf16[256,384]{1,0:T(8,128)(2,1)} %param.7) | copy-start | bytes 589828
  70.8 49.1 %copy-start.4 = (bf16[256,384]{1,0:T(8,128)(2,1)S(1)}, bf16[256,384]{1,0:T(8,128)(2,1)}, u32[]{:S(2)}) copy-start(bf16[256,384]{1,0:T(8,128)(2,1)} %param.8) | copy-start | bytes 589828
  71.7 104.4 %all-gather.4.cloned.1.call-start = ((), (), s32[]{:S(2)}) async-start(), calls=%async_computation.1 | async-start | bytes 1769472 | tf_op jit(solution)/shard_map/all_gather | solution.py:68
  113.8 10.2 %collective-permute-start = (bf16[768,1536]{1,0:T(8,128)(2,1)}, bf16[768,1536]{1,0:T(8,128)(2,1)}, u32[]{:S(2)}, u32[]{:S(2)}) collective-permute-start(bf16[768,1536]{1,0:T(8,128)(2,1)} %all-gather.6.cloned.1.call-done), channel_id=1, source_target_pairs={{0,8},{8,0},{1,9},{9,1},{2,10},{10,2},{3,11},{11,3},{4,12},{12,4},... | collective-permute-start | bytes 7077896 | tf_op jit(solution)/shard_map/ppermute | solution.py:22
  122.7 111.2 %reduce-scatter.2.cloned.1.call-start = ((), (), s32[]{:S(2)}) async-start(), calls=%async_computation.3 | async-start | bytes 1769472 | tf_op jit(solution)/shard_map/reduce_scatter | solution.py:79
  122.8 5.3 %copy-start.5 = (s32[768]{0:T(1024)S(1)}, s32[768]{0:T(1024)}, u32[]{:S(2)}) copy-start(s32[768]{0:T(1024)} %constant.22.clone) | copy-start | bytes 9220
  235.0 1.1 copy-start.1
Sparse Core Ops, SparseCore 0:
  71.8 41.9 all-gather.5
Sparse Core Ops, SparseCore 1:
  122.8 53.3 all-gather.3
  179.4 54.4 reduce-scatter.1

commit v3 on v2

v3 whole, which is shorter than its diff:
```python
import functools
import math

import jax
import jax.numpy as jnp
import numpy as np
from jax import lax
from jax.experimental import pallas as pl
from jax.experimental.pallas import tpu as pltpu
from jax.sharding import Mesh, PartitionSpec as P

HD = 128
SEQ = 256
SIZES = (2, 8, 4, 2, 8)
DP = ("zh", "y", "x", "core")
BF16 = jnp.bfloat16
F32 = jnp.float32
PARAMS = pltpu.CompilerParams(vmem_limit_bytes=40 * 1024 * 1024)
NT = (((1,), (1,)), ((), ()))
TN = (((0,), (0,)), ((), ()))


def folded(n):
    return [*range(0, n, 2), *reversed(range(1, n, 2))]


def shift(block, axis, by):
    n = lax.axis_size(axis)
    return lax.ppermute(block, axis, [(i, (i + by) % n) for i in range(n)])


def by_core(own, other):
    first = lax.axis_index("core") == 0
    return jnp.where(first, own, other), jnp.where(first, other, own)


def dot(a, b):
    return jnp.dot(a, b, preferred_element_type=F32)


def dot_nt(a, b):
    return lax.dot_general(a, b, NT, preferred_element_type=F32)


def dot_tn(a, b):
    return lax.dot_general(a, b, TN, preferred_element_type=F32)


def cost(flops, nbytes, transcendentals=0):
    return pl.CostEstimate(flops=flops, bytes_accessed=nbytes, transcendentals=transcendentals)


def forward_kernel(scale, q_ref, k_ref, v_ref, o_ref, p_ref):
    for head in range(q_ref.shape[1] // HD):
        cols = slice(head * HD, (head + 1) * HD)
        scores = dot_nt(q_ref[:, cols], k_ref[:, cols]) * scale
        powers = jnp.exp(scores - jnp.max(scores, axis=1, keepdims=True))
        soft = powers / jnp.sum(powers, axis=1, keepdims=True)
        p_ref[head] = soft
        o_ref[:, cols] = dot(soft.astype(BF16), v_ref[:, cols]).astype(BF16)


def backward_kernel(scale, q_ref, k_ref, v_ref, p_ref, g_ref, dq_ref, dk_ref, dv_ref):
    for head in range(q_ref.shape[1] // HD):
        cols = slice(head * HD, (head + 1) * HD)
        soft = p_ref[head]
        grad = g_ref[:, cols]
        soft_grad = dot_nt(grad, v_ref[:, cols])
        inner = jnp.sum(soft_grad * soft, axis=1, keepdims=True)
        score_grad = (soft * (soft_grad - inner)).astype(BF16)
        dv_ref[:, cols] = dot_tn(soft.astype(BF16), grad).astype(BF16)
        dq_ref[:, cols] = (dot(score_grad, k_ref[:, cols]) * scale).astype(BF16)
        dk_ref[:, cols] = (dot_tn(score_grad, q_ref[:, cols]) * scale).astype(BF16)


def terms_kernel(slot_ref, cot_ref, w_ref, *refs):
    refs[-1][0] = dot(cot_ref[...], w_ref[...]).astype(BF16)


def output_kernel(slots, core_ref, o_ref, own_ref, other_ref, sown_ref, sother_ref, out_ref):
    width = o_ref.shape[2]
    for core in range(2):

        @pl.when(core_ref[0] == core)
        def _():
            total = None
            for half, w_ref, s_ref in (
                (core, own_ref, sown_ref),
                (1 - core, other_ref, sother_ref),
            ):
                rows = sum(
                    dot_nt(o_ref[slot], w_ref[:, j * width : (j + 1) * width])
                    for j, slot in enumerate(slots[half])
                )
                placed = dot(rows.astype(BF16), s_ref[...])
                total = placed if total is None else total + placed
            out_ref[...] = total.astype(BF16)


def spread_of(rows_dev, features, core):
    nz, ny, nx, nc = (lax.axis_size(a) for a in DP)
    x0, z0 = lax.axis_index("x"), lax.axis_index("zh")
    place, x, z, c, r = np.indices((ny, nx, nz, nc, rows_dev)).reshape(5, -1)
    y = jnp.where(core == 0, place, ny - 1 - place)
    x = (x0 + x) % nx
    z = (z0 + z) % nz
    feature = (((z * ny + y) * nx + x) * nc + c) * rows_dev + r
    return (feature[:, None] == jnp.arange(features)[None, :]).astype(BF16)


def first_stage(w_out):
    shard = w_out.T
    core = lax.axis_index("core")
    half = shard.shape[1] // 2
    both = jnp.concatenate([shard, shift(shard, "zh", 1)], 0).reshape(2, *shard.shape)
    mine = lax.dynamic_slice_in_dim(both, core * half, half, 2)
    theirs = shift(lax.dynamic_slice_in_dim(both, (1 - core) * half, half, 2), "core", 1)
    base = jnp.stack(by_core(mine, theirs), 1).reshape(-1, half)
    nx = lax.axis_size("x")
    return jnp.concatenate([base] + [shift(base, "x", -i) for i in range(1, nx)], 0)


def on_device(queries, keys, values, w_out, cotangent):
    row_count, group_width = queries.shape
    features = cotangent.shape[1]
    local_heads = group_width // HD
    n = lax.axis_size("zl")
    ny = lax.axis_size("y")
    core = lax.axis_index("core")
    scale = 1.0 / math.sqrt(HD)
    line = folded(n)
    slots = [[line.index(h * n // 2 + j) for j in range(n // 2)] for h in range(2)]
    tokens = jax.ShapeDtypeStruct((row_count, group_width), BF16)

    attention_flops = 2 * row_count * row_count * group_width
    head_out, soft = pl.pallas_call(
        functools.partial(forward_kernel, scale),
        out_shape=(
            tokens,
            jax.ShapeDtypeStruct((local_heads, row_count, row_count), F32),
        ),
        compiler_params=PARAMS,
        cost_estimate=cost(2 * attention_flops, 1 << 21, local_heads * row_count**2),
        name="attention_forward",
    )(queries, keys, values)
    heads_all = lax.all_gather(head_out, "zl", axis=0, axis_index_groups=[line])

    w_out, head_out = lax.optimization_barrier((w_out, head_out))
    block = first_stage(w_out)
    ring = list(range(ny))
    own = lax.all_gather(
        block,
        ("core", "y"),
        axis=0,
        tiled=True,
        axis_index_groups=[ring, [2 * ny - 1 - i for i in ring]],
    )
    own, heads_all = lax.optimization_barrier((own, heads_all))
    other = shift(own, "core", 1)
    spread_own = spread_of(w_out.shape[1], features, core)
    spread_other = spread_of(w_out.shape[1], features, 1 - core)
    cot_own = dot_nt(cotangent, spread_own).astype(BF16)
    cot_other = dot_nt(cotangent, spread_other).astype(BF16)

    def terms(half, cot, columns, *into):
        places = jnp.where(half == 0, jnp.asarray(slots[0]), jnp.asarray(slots[1]))
        return pl.pallas_call(
            terms_kernel,
            out_shape=jax.ShapeDtypeStruct((n, row_count, group_width), BF16),
            grid_spec=pltpu.PrefetchScalarGridSpec(
                num_scalar_prefetch=1,
                grid=(n // 2,),
                in_specs=[
                    pl.BlockSpec((row_count, features), lambda j, place: (0, 0)),
                    pl.BlockSpec((features, group_width), lambda j, place: (0, j)),
                ]
                + [pl.BlockSpec(memory_space=pl.ANY)] * len(into),
                out_specs=pl.BlockSpec(
                    (1, row_count, group_width), lambda j, place: (place[j], 0, 0)
                ),
            ),
            input_output_aliases={3: 0} if into else {},
            compiler_params=PARAMS,
            cost_estimate=cost(row_count * features * group_width * n, 4 << 20),
            name="gradient_terms",
        )(places.astype(jnp.int32), cot, columns, *into)

    terms_all = terms(core, cot_own, own)
    terms_all = terms(1 - core, cot_other, other, terms_all)
    grad_out = lax.psum_scatter(
        terms_all, "zl", scatter_dimension=0, tiled=False, axis_index_groups=[line]
    )

    vmem = pl.BlockSpec(memory_space=pltpu.VMEM)
    branch_out = pl.pallas_call(
        functools.partial(output_kernel, slots),
        out_shape=jax.ShapeDtypeStruct((row_count, features), BF16),
        in_specs=[pl.BlockSpec(memory_space=pltpu.SMEM)] + [vmem] * 5,
        out_specs=vmem,
        compiler_params=PARAMS,
        cost_estimate=cost(2 * row_count * features * group_width * n, 8 << 20),
        name="output_projection",
    )(
        jnp.reshape(core, (1,)).astype(jnp.int32),
        heads_all,
        own,
        other,
        spread_own,
        spread_other,
    )

    grads = pl.pallas_call(
        functools.partial(backward_kernel, scale),
        out_shape=(tokens, tokens, tokens),
        compiler_params=PARAMS,
        cost_estimate=cost(4 * attention_flops, 1 << 21),
        name="attention_backward",
    )(queries, keys, values, soft, grad_out)
    return (branch_out, *grads)


def solution(mesh):
    fine = Mesh(mesh.devices.reshape(SIZES), (*DP, "zl"))
    tokens = P(DP, "zl")
    return jax.shard_map(
        on_device,
        mesh=fine,
        in_specs=(tokens, tokens, tokens, P(None, ("zl", *DP)), tokens),
        out_specs=(tokens, tokens, tokens, tokens),
        check_vma=False,
    )
```

time: 250 us -> 207 us (0.83)
  blocking collectives: 62.7 us -> 0 us
  starting transfers between devices: 5.81 us -> 43 us
  local copies, waits for them, and re-layouts: 29.8 us -> 9.26 us
  Pallas kernels: 0 us -> 14.4 us
  matrix products: 14.6 us -> 1.33 us
  waiting for transfers between devices: 114 us -> 119 us
    all_gather x1 -> x0, blocking collectives: 62.7 us -> none  [gather_projection(): near = lax.all_gather(w_out.T, ('zh', 'x', 'core'), axis=0, tiled=True)]
    ppermute x1 -> x6, starting transfers between devices: 5.69 us -> 42.9 us  [shift(): return lax.ppermute(block, axis, [(i, (i + by) % n) for i in range(n)])]
    unnamed x32 -> x30, local copies, waits for them, and re-layouts: 24.7 us -> 9.17 us
    pallas_call x0 -> x5, Pallas kernels: none -> 14.4 us  [the longest x2 6.48 us: terms(): pl.pallas_call(terms_kernel, out_shape=jax.ShapeDtypeStruct((n, row_count...]
    dot_general x7 -> x2, matrix products: 13.2 us -> 1.33 us  [dot_nt(): return lax.dot_general(a, b, NT, preferred_element_type=F32)]
    reduce_scatter x1, waiting for transfers between devices: 41.1 us -> 45.9 us  [on_device(): lax.psum_scatter(terms_all, 'zl', scatter_dimension=0, tiled=False, axis_...]
    select_n x1, other arithmetic: 4.1 us -> 0.01 us  [terms(): places = jnp.where(half == 0, jnp.asarray(slots[0]), jnp.asarray(slots[1]))]
    ppermute x1 -> x6, waiting for transfers between devices: 1.23 us -> 5.26 us  [shift(): return lax.ppermute(block, axis, [(i, (i + by) % n) for i in range(n)])]
  transfers between devices with their start and end apart: 4 -> 9, of which waited for: 4 -> 7; matrix products, arithmetic and copies ran while one was open for 17% -> 2% of each run, Pallas kernels for 0% -> 4%
where the time goes in v3:
time: 207 us; the launch traced here: 204 us
  waiting for transfers between devices  119 us (57%)
  starting transfers between devices  43 us (21%)
  Pallas kernels  14.4 us (7%)
  between operations  14 us (7%)
  local copies, waits for them, and re-layouts  9.26 us (4%)
  other arithmetic  2.99 us (1%)
    all_gather x1, waiting for transfers between devices, on_device(): lax.all_gather(block, ('core', 'y'), axis=0, tiled=True, axis_index_group...  48.9 us
    reduce_scatter x1, waiting for transfers between devices, on_device(): lax.psum_scatter(terms_all, 'zl', scatter_dimension=0, tiled=False, axis_...  45.9 us
    ppermute x6, starting transfers between devices, shift(): return lax.ppermute(block, axis, [(i, (i + by) % n) for i in range(n)])  42.9 us
    all_gather x1, waiting for transfers between devices, on_device(): heads_all = lax.all_gather(head_out, 'zl', axis=0, axis_index_groups=[line])  19.2 us
    unnamed x30, local copies, waits for them, and re-layouts  9.17 us
    pallas_call x2, Pallas kernels, terms(): pl.pallas_call(terms_kernel, out_shape=jax.ShapeDtypeStruct((n, row_count...  6.48 us
    ppermute x6, waiting for transfers between devices, shift(): return lax.ppermute(block, axis, [(i, (i + by) % n) for i in range(n)])  5.26 us
    pallas_call x1, Pallas kernels, on_device(): pl.pallas_call(functools.partial(output_kernel, slots), out_shape=jax.Sha...  4.32 us
  transfers between devices with their start and end apart: 9, of which 7 were waited for; matrix products, arithmetic and copies ran while one was open for 2% of the time, Pallas kernels for 4%

profile of v3, /device:TPU:1, one launch (start us, length us, event | category | flops | bytes accessed | tf_op | source)
XLA Modules:
  0.0 204.2 jit_solution(15061162486170494524)
XLA Ops:
  7.2 0.0 copy-start
  7.2 0.0 copy-start.13
  7.2 0.0 copy-start.14
  7.2 0.0 copy-start.11
  7.2 0.0 copy-start.12
  7.2 0.0 all-gather.6.cloned.1.call-start
  7.3 0.0 copy-start.4
  7.3 1.0 copy-done.4
  8.2 0.0 copy-start.6
  8.2 0.9 copy-done.6
  9.2 0.0 copy-start.8
  9.2 0.9 copy-done.8
  10.1 1.7 attention_forward.1
  11.8 0.0 all-gather.6.cloned.1.call-update
  11.8 0.0 all-gather.4.cloned.1.call-start
  11.9 19.9 %collective-permute-start = (bf16[6,3072]{1,0:T(8,128)(2,1)}, bf16[6,3072]{1,0:T(8,128)(2,1)S(1)}, u32[]{:S(2)}, u32[]{:S(2)}) collective-permute-start(bf16[6,3072]{1,0:T(8,128)(2,1)} %bitcast.16), channel_id=1, source_target_pairs={{0,512},{512,0},{1,513},{513,1},{2,514},{514,2},{3,515},{515,3},{4... | collective-permute-start | bytes 110600 | tf_op jit(solution)/shard_map/ppermute | solution.py:29
  31.8 1.8 collective-permute-done
  33.6 0.8 pad_maximum_fusion.1
  34.5 9.2 %collective-permute-start.1 = (bf16[2,6,1536]{2,1,0:T(8,128)(2,1)S(1)}, bf16[2,6,1536]{2,1,0:T(8,128)(2,1)S(1)}, u32[]{:S(2)}, u32[]{:S(2)}) collective-permute-start(bf16[2,6,1536]{2,1,0:T(8,128)(2,1)S(1)} %constant_dynamic-slice_fusion), channel_id=1, source_target_pairs={{0,8},{8,0},{1,9},{9,1},{2,10},{10,2},{3,11},{11,3},{4,12},{12,4},... | collective-permute-start | bytes 110600 | tf_op jit(solution)/shard_map/ppermute | solution.py:29
  43.8 0.9 collective-permute-done.1
  44.7 1.9 collective-permute-start.4
  46.7 1.9 collective-permute-start.3
  48.6 4.6 %collective-permute-start.2 = (bf16[24,1536]{1,0:T(8,128)(2,1)S(1)}, bf16[24,1536]{1,0:T(8,128)(2,1)S(1)}, u32[]{:S(2)}, u32[]{:S(2)}) collective-permute-start(bf16[24,1536]{1,0:T(8,128)(2,1)S(1)} %reshape.21), channel_id=1, source_target_pairs={{0,48},{16,0},{32,16},{48,32},{1,49},{17,1},{33,17},{49,33},{2,50}... | collective-permute-start | bytes 221192 | tf_op jit(solution)/shard_map/ppermute | solution.py:29
  53.2 0.0 collective-permute-done.4
  53.2 0.1 collective-permute-done.3
  53.3 2.5 %collective-permute-done.2 = bf16[24,1536]{1,0:T(8,128)(2,1)S(1)} collective-permute-done((bf16[24,1536]{1,0:T(8,128)(2,1)S(1)}, bf16[24,1536]{1,0:T(8,128)(2,1)S(1)}, u32[]{:S(2)}, u32[]{:S(2)}) %collective-permute-start.2) | collective-permute-done | bytes 73760 | tf_op jit(solution)/shard_map/ppermute | solution.py:29
  55.8 0.7 pad_maximum_fusion
  56.5 0.0 all-gather.4.cloned.1.call-update
  56.5 0.0 reduce-scatter.2.cloned.1.call-start
  56.6 19.2 %all-gather.6.cloned.1.call-done = bf16[2048,384]{1,0:T(8,128)(2,1)} async-done(((bf16[256,384]{1,0:T(8,128)(2,1)}), bf16[2048,384]{1,0:T(8,128)(2,1)}) %all-gather.6.cloned.1.call-update) | async-done | bytes 1572880 | tf_op jit(solution)/shard_map/all_gather | solution.py:146
  75.8 48.9 %all-gather.4.cloned.1.call-done.own_ref.w_ref = bf16[768,1536]{1,0:T(8,128)(2,1)} async-done(((bf16[96,1536]{1,0:T(8,128)(2,1)}), bf16[768,1536]{1,0:T(8,128)(2,1)}) %all-gather.4.cloned.1.call-update) | async-done | bytes 2359312 | tf_op jit(solution)/shard_map/all_gather | solution.py:151
  124.6 5.3 %collective-permute-start.5 = (bf16[768,1536]{1,0:T(8,128)(2,1)}, bf16[768,1536]{1,0:T(8,128)(2,1)S(1)}, u32[]{:S(2)}, u32[]{:S(2)}) collective-permute-start(bf16[768,1536]{1,0:T(8,128)(2,1)} %all-gather.4.cloned.1.call-done.own_ref.w_ref), channel_id=1, source_target_pairs={{0,8},{8,0},{1,9},{9,1},{2,10},{10,2},{3,11},{11,3},{4,12},{12,4},... | collective-permute-start | bytes 7077896 | tf_op jit(solution)/shard_map/ppermute | solution.py:29
  130.0 0.0 copy-done.13
  130.0 0.0 copy-done.14
  130.0 0.0 copy-start.1
  130.0 0.0 copy-done.11
  130.0 0.0 copy-done.12
  130.0 0.9 multiply_add_fusion
  130.9 0.0 copy-done
  130.9 0.7 fusion.6.cot_ref
  131.6 0.7 fusion.7.cot_ref
  132.3 0.0 copy-done.1
  132.3 3.2 %gradient_terms.2.refs_0_ = bf16[8,256,384]{2,1,0:T(8,128)(2,1)} custom-call(s32[4]{0:T(128)S(1)} %get-tuple-element.24.slot_ref, bf16[256,768]{1,0:T(8,128)(2,1)S(1)} %fusion.7.cot_ref, bf16[768,1536]{1,0:T(8,128)(2,1)S(1)} %copy-done.1), custom_call_target="tpu_custom_call" | custom-call | flops 603979776 | bytes 4194304 | tf_op jit(solution)/shard_map/gradient_terms/pallas_call | solution.py:167
  135.6 0.0 collective-permute-done.5.other_ref.w_ref
  135.6 3.2 %gradient_terms.3 = bf16[8,256,384]{2,1,0:T(8,128)(2,1)} custom-call(s32[4]{0:T(128)S(1)} %get-tuple-element.25.slot_ref, bf16[256,768]{1,0:T(8,128)(2,1)S(1)} %fusion.6.cot_ref, bf16[768,1536]{1,0:T(8,128)(2,1)S(1)} %collective-permute-done.5.other_ref.w_ref, bf16[8,256,384]{2,1,0:T(8,128)(2,1)} %gradient_terms.2.refs_0_), custom_call_target="tpu_custom_call", output_to_operand_aliasing={{}: (3, {})} | custom-call | flops 603979776 | bytes 4194304 | tf_op jit(solution)/shard_map/gradient_terms/pallas_call | solution.py:167
  138.8 0.0 reduce-scatter.2.cloned.1.call-update
  138.8 0.0 copy-start.2
  138.8 0.4 fusion.1
  139.3 1.2 copy-done.2
  140.5 0.0 copy-start.3
  140.5 1.4 copy-done.3
  141.9 4.3 %output_projection.1 = bf16[256,768]{1,0:T(8,128)(2,1)} custom-call(s32[1]{0:T(128)} %bitcast.core_ref, bf16[8,256,384]{2,1,0:T(8,128)(2,1)S(1)} %bitcast.14, bf16[768,1536]{1,0:T(8,128)(2,1)S(1)} %copy-done.2, bf16[768,1536]{1,0:T(8,128)(2,1)S(1)} %collective-permute-done.5.other_ref.w_ref, bf16[768,768]{1,0:T(8,128)(2,1)S(1)} %get-tuple-element.27.sown_ref, ...), custom_call_target="tpu_custom_call" | custom-call | flops 1207959552 | bytes 8388608 | tf_op jit(solution)/shard_map/output_projection/pallas_call | solution.py:195
  146.2 45.9 %reduce-scatter.2.cloned.1.call-done = bf16[1,256,384]{2,1,0:T(8,128)(2,1)} async-done(((bf16[8,256,384]{2,1,0:T(8,128)(2,1)}), bf16[1,256,384]{2,1,0:T(8,128)(2,1)}) %reduce-scatter.2.cloned.1.call-update) | async-done | bytes 196624 | tf_op jit(solution)/shard_map/reduce_scatter | solution.py:190
  192.1 0.0 copy-start.5
  192.1 0.9 copy-done.5
  193.0 0.0 copy-start.7
  193.0 0.9 copy-done.7
  193.9 0.0 copy-start.9
  193.9 0.9 copy-done.9
  194.8 0.0 copy-start.10
  194.8 0.9 copy-done.10
  195.8 1.9 attention_backward.1
  (7 shorter events, 0.1 us)
Async XLA Ops:
  7.2 123.8 %copy-start = (bf16[256,768]{1,0:T(8,128)(2,1)S(1)}, bf16[256,768]{1,0:T(8,128)(2,1)}, u32[]{:S(2)}) copy-start(bf16[256,768]{1,0:T(8,128)(2,1)} %param.25) | copy-start | bytes 1179652
  7.2 122.8 %copy-start.13 = (s32[4]{0:T(128)S(1)}, s32[4]{0:T(128)}, u32[]{:S(2)}) copy-start(s32[4]{0:T(128)} %constant.85.clone) | copy-start | bytes 52
  7.2 122.8 %copy-start.14 = (s32[4]{0:T(128)S(1)}, s32[4]{0:T(128)}, u32[]{:S(2)}) copy-start(s32[4]{0:T(128)} %constant.86.clone) | copy-start | bytes 52
  7.2 122.8 %copy-start.11 = (s32[768]{0:T(1024)S(1)}, s32[768]{0:T(1024)}, u32[]{:S(2)}) copy-start(s32[768]{0:T(1024)} %constant.84.clone) | copy-start | bytes 9220
  7.2 122.8 %copy-start.12 = (s32[768]{0:T(1024)S(1)}, s32[768]{0:T(1024)}, u32[]{:S(2)}) copy-start(s32[768]{0:T(1024)} %constant.83.clone) | copy-start | bytes 9220
  7.2 68.5 %all-gather.6.cloned.1.call-start = ((), (), s32[]{:S(2)}) async-start(), calls=%async_computation.3 | async-start | bytes 1769472 | tf_op jit(solution)/shard_map/all_gather | solution.py:146
  7.3 1.0 copy-start.4
  8.2 0.9 copy-start.6
  9.2 0.9 copy-start.8
  11.8 112.8 %all-gather.4.cloned.1.call-start = ((), (), s32[]{:S(2)}) async-start(), calls=%async_computation.1 | async-start | bytes 2654208 | tf_op jit(solution)/shard_map/all_gather | solution.py:151
  11.9 21.7 %collective-permute-start = (bf16[6,3072]{1,0:T(8,128)(2,1)}, bf16[6,3072]{1,0:T(8,128)(2,1)S(1)}, u32[]{:S(2)}, u32[]{:S(2)}) collective-permute-start(bf16[6,3072]{1,0:T(8,128)(2,1)} %bitcast.16), channel_id=1, source_target_pairs={{0,512},{512,0},{1,513},{513,1},{2,514},{514,2},{3,515},{515,3},{4... | collective-permute-start | bytes 110600 | tf_op jit(solution)/shard_map/ppermute | solution.py:29
  34.5 10.1 %collective-permute-start.1 = (bf16[2,6,1536]{2,1,0:T(8,128)(2,1)S(1)}, bf16[2,6,1536]{2,1,0:T(8,128)(2,1)S(1)}, u32[]{:S(2)}, u32[]{:S(2)}) collective-permute-start(bf16[2,6,1536]{2,1,0:T(8,128)(2,1)S(1)} %constant_dynamic-slice_fusion), channel_id=1, source_target_pairs={{0,8},{8,0},{1,9},{9,1},{2,10},{10,2},{3,11},{11,3},{4,12},{12,4},... | collective-permute-start | bytes 110600 | tf_op jit(solution)/shard_map/ppermute | solution.py:29
  44.7 8.4 %collective-permute-start.4 = (bf16[24,1536]{1,0:T(8,128)(2,1)S(1)}, bf16[24,1536]{1,0:T(8,128)(2,1)S(1)}, u32[]{:S(2)}, u32[]{:S(2)}) collective-permute-start(bf16[24,1536]{1,0:T(8,128)(2,1)S(1)} %reshape.21), channel_id=1, source_target_pairs={{0,16},{16,32},{32,48},{48,0},{1,17},{17,33},{33,49},{49,1},{2,18}... | collective-permute-start | bytes 221192 | tf_op jit(solution)/shard_map/ppermute | solution.py:29
  46.7 6.6 %collective-permute-start.3 = (bf16[24,1536]{1,0:T(8,128)(2,1)S(1)}, bf16[24,1536]{1,0:T(8,128)(2,1)S(1)}, u32[]{:S(2)}, u32[]{:S(2)}) collective-permute-start(bf16[24,1536]{1,0:T(8,128)(2,1)S(1)} %reshape.21), channel_id=1, source_target_pairs={{0,32},{16,48},{32,0},{48,16},{1,33},{17,49},{33,1},{49,17},{2,34}... | collective-permute-start | bytes 221192 | tf_op jit(solution)/shard_map/ppermute | solution.py:29
  48.6 7.2 %collective-permute-start.2 = (bf16[24,1536]{1,0:T(8,128)(2,1)S(1)}, bf16[24,1536]{1,0:T(8,128)(2,1)S(1)}, u32[]{:S(2)}, u32[]{:S(2)}) collective-permute-start(bf16[24,1536]{1,0:T(8,128)(2,1)S(1)} %reshape.21), channel_id=1, source_target_pairs={{0,48},{16,0},{32,16},{48,32},{1,49},{17,1},{33,17},{49,33},{2,50}... | collective-permute-start | bytes 221192 | tf_op jit(solution)/shard_map/ppermute | solution.py:29
  56.5 135.5 %reduce-scatter.2.cloned.1.call-start = ((), (), s32[]{:S(2)}) async-start(), calls=%async_computation.2 | async-start | bytes 1769472 | tf_op jit(solution)/shard_map/reduce_scatter | solution.py:190
  124.6 10.9 %collective-permute-start.5 = (bf16[768,1536]{1,0:T(8,128)(2,1)}, bf16[768,1536]{1,0:T(8,128)(2,1)S(1)}, u32[]{:S(2)}, u32[]{:S(2)}) collective-permute-start(bf16[768,1536]{1,0:T(8,128)(2,1)} %all-gather.4.cloned.1.call-done.own_ref.w_ref), channel_id=1, source_target_pairs={{0,8},{8,0},{1,9},{9,1},{2,10},{10,2},{3,11},{11,3},{4,12},{12,4},... | collective-permute-start | bytes 7077896 | tf_op jit(solution)/shard_map/ppermute | solution.py:29
  130.0 2.3 %copy-start.1 = (bf16[768,1536]{1,0:T(8,128)(2,1)S(1)}, bf16[768,1536]{1,0:T(8,128)(2,1)}, u32[]{:S(2)}) copy-start(bf16[768,1536]{1,0:T(8,128)(2,1)} %all-gather.4.cloned.1.call-done.own_ref.w_ref) | copy-start | bytes 7077892
  138.8 1.7 copy-start.2
  140.5 1.4 copy-start.3
  192.1 0.9 copy-start.5
  193.0 0.9 copy-start.7
  193.9 0.9 copy-start.9
  194.8 0.9 copy-start.10
Sparse Core Ops, SparseCore 0:
  11.9 63.7 all-gather.5
  79.0 45.6 all-gather.3
  138.9 53.0 reduce-scatter.1

commit v4 on v3

v4 whole, which is shorter than its diff:
```python
import functools
import math

import jax
import jax.numpy as jnp
import numpy as np
from jax import lax
from jax.experimental import pallas as pl
from jax.experimental.pallas import tpu as pltpu
from jax.sharding import Mesh, PartitionSpec as P

HD = 128
SEQ = 256
SIZES = (2, 8, 4, 2, 8)
DP = ("zh", "y", "x", "core")
BF16 = jnp.bfloat16
F32 = jnp.float32
PARAMS = pltpu.CompilerParams(vmem_limit_bytes=40 * 1024 * 1024)
WIDE = pltpu.CompilerParams(vmem_limit_bytes=60 * 1024 * 1024)
NT = (((1,), (1,)), ((), ()))
TN = (((0,), (0,)), ((), ()))


def folded(n):
    return [*range(0, n, 2), *reversed(range(1, n, 2))]


def shift(block, axis, by):
    n = lax.axis_size(axis)
    return lax.ppermute(block, axis, [(i, (i + by) % n) for i in range(n)])


def by_core(own, other):
    first = lax.axis_index("core") == 0
    return jnp.where(first, own, other), jnp.where(first, other, own)


def dot(a, b):
    return jnp.dot(a, b, preferred_element_type=F32)


def dot_nt(a, b):
    return lax.dot_general(a, b, NT, preferred_element_type=F32)


def dot_tn(a, b):
    return lax.dot_general(a, b, TN, preferred_element_type=F32)


def cost(flops, nbytes, transcendentals=0):
    return pl.CostEstimate(flops=flops, bytes_accessed=nbytes, transcendentals=transcendentals)


def forward_kernel(scale, q_ref, k_ref, v_ref, o_ref, p_ref):
    scores = dot_nt(q_ref[...], k_ref[...]) * scale
    powers = jnp.exp(scores - jnp.max(scores, axis=1, keepdims=True))
    soft = powers / jnp.sum(powers, axis=1, keepdims=True)
    p_ref[0] = soft
    o_ref[...] = dot(soft.astype(BF16), v_ref[...]).astype(BF16)


def backward_kernel(scale, q_ref, k_ref, v_ref, p_ref, g_ref, dq_ref, dk_ref, dv_ref):
    soft = p_ref[0]
    grad = g_ref[...]
    soft_grad = dot_nt(grad, v_ref[...])
    inner = jnp.sum(soft_grad * soft, axis=1, keepdims=True)
    score_grad = (soft * (soft_grad - inner)).astype(BF16)
    dv_ref[...] = dot_tn(soft.astype(BF16), grad).astype(BF16)
    dq_ref[...] = (dot(score_grad, k_ref[...]) * scale).astype(BF16)
    dk_ref[...] = (dot_tn(score_grad, q_ref[...]) * scale).astype(BF16)


def terms_kernel(slot_ref, cot_ref, near_ref, far_ref, *refs):
    near = near_ref.shape[0]
    total = dot(cot_ref[:, :near], near_ref[...]) + dot(cot_ref[:, near:], far_ref[...])
    refs[-1][0] = total.astype(BF16)


def output_kernel(slots, core_ref, o_ref, own_near, own_far, other_near, other_far, s_ref, out_ref):
    width = o_ref.shape[2]
    near = own_near.shape[0]
    for core in range(2):

        @pl.when(core_ref[0] == core)
        def _():
            total = None
            for place, (first, last) in ((0, (own_near, other_near)), (near, (own_far, other_far))):
                rows = None
                for half, w_ref in ((core, first), (1 - core, last)):
                    for j, slot in enumerate(slots[half]):
                        term = dot_nt(o_ref[slot], w_ref[:, j * width : (j + 1) * width])
                        rows = term if rows is None else rows + term
                placed = dot(rows.astype(BF16), s_ref[place : place + rows.shape[1], :])
                total = placed if total is None else total + placed
            out_ref[...] = total.astype(BF16)


def ring_offsets(n):
    offsets = [0]
    for step in range(1, n // 2 + 1):
        offsets.append(-step)
        if 2 * step < n:
            offsets.append(step)
    return np.array(offsets)


def ring_gather(block, axis, beside, join):
    n = lax.axis_size(axis)
    up = down = block
    blocks = [block]
    for step in range(1, n // 2 + 1):
        if step == join:
            up, beside = lax.optimization_barrier((up, beside))
        up = shift(up, axis, 1)
        blocks.append(up)
        if 2 * step < n:
            down = shift(down, axis, -1)
            blocks.append(down)
    return blocks, beside


def spread_of(rows_dev, features):
    nz, ny, nx, nc = (lax.axis_size(a) for a in DP)
    x0, y0, z0 = (lax.axis_index(a) for a in ("x", "y", "zh"))
    place, x, z, c, r = np.indices((ny, nx, nz, nc, rows_dev)).reshape(5, -1)
    y = (y0 + ny + ring_offsets(ny)[place]) % ny
    x = (x0 + x) % nx
    z = (z0 + z) % nz
    feature = (((z * ny + y) * nx + x) * nc + c) * rows_dev + r
    return (feature[:, None] == jnp.arange(features)[None, :]).astype(BF16)


def first_stage(shard, across):
    core = lax.axis_index("core")
    half = shard.shape[1] // 2
    both = jnp.concatenate([shard, across], 0).reshape(2, *shard.shape)
    mine = lax.dynamic_slice_in_dim(both, core * half, half, 2)
    theirs = shift(lax.dynamic_slice_in_dim(both, (1 - core) * half, half, 2), "core", 1)
    base = jnp.stack(by_core(mine, theirs), 1).reshape(-1, half)
    nx = lax.axis_size("x")
    return jnp.concatenate([base] + [shift(base, "x", -i) for i in range(1, nx)], 0)


def on_device(queries, keys, values, w_out, cotangent):
    row_count, group_width = queries.shape
    features = cotangent.shape[1]
    local_heads = group_width // HD
    n = lax.axis_size("zl")
    ny = lax.axis_size("y")
    core = lax.axis_index("core")
    scale = 1.0 / math.sqrt(HD)
    line = folded(n)
    slots = [[line.index(h * n // 2 + j) for j in range(n // 2)] for h in range(2)]
    tokens = jax.ShapeDtypeStruct((row_count, group_width), BF16)

    attention_flops = 2 * row_count * row_count * group_width
    head = pl.BlockSpec((row_count, HD), lambda h: (0, h))
    square = pl.BlockSpec((1, row_count, row_count), lambda h: (h, 0, 0))
    across = shift(w_out.T, "zh", 1)
    head_out, soft = pl.pallas_call(
        functools.partial(forward_kernel, scale),
        out_shape=(
            tokens,
            jax.ShapeDtypeStruct((local_heads, row_count, row_count), F32),
        ),
        grid=(local_heads,),
        in_specs=[head] * 3,
        out_specs=(head, square),
        compiler_params=WIDE,
        cost_estimate=cost(2 * attention_flops, 1 << 21, local_heads * row_count**2),
        name="attention_forward",
    )(queries, keys, values)
    heads_all = lax.all_gather(head_out, "zl", axis=0, axis_index_groups=[line])
    spread = spread_of(w_out.shape[1], features)
    cot_rows = dot_nt(cotangent, spread).astype(BF16)

    across, head_out, cot_rows = lax.optimization_barrier((across, head_out, cot_rows))
    blocks, heads_all = ring_gather(first_stage(w_out.T, across), "y", heads_all, 4)
    early = 2 * ((ny + 2) // 4) + 1
    own_near = jnp.concatenate(blocks[:early], 0)
    other_near = shift(own_near, "core", 1)
    own_far = jnp.concatenate(blocks[early:], 0)
    other_far = shift(own_far, "core", 1)

    def terms(half, near, far, *into):
        places = jnp.where(half == 0, jnp.asarray(slots[0]), jnp.asarray(slots[1]))
        return pl.pallas_call(
            terms_kernel,
            out_shape=jax.ShapeDtypeStruct((n, row_count, group_width), BF16),
            grid_spec=pltpu.PrefetchScalarGridSpec(
                num_scalar_prefetch=1,
                grid=(n // 2,),
                in_specs=[
                    pl.BlockSpec((row_count, features), lambda j, place: (0, 0)),
                    pl.BlockSpec((near.shape[0], group_width), lambda j, place: (0, j)),
                    pl.BlockSpec((far.shape[0], group_width), lambda j, place: (0, j)),
                ]
                + [pl.BlockSpec(memory_space=pl.ANY)] * len(into),
                out_specs=pl.BlockSpec(
                    (1, row_count, group_width), lambda j, place: (place[j], 0, 0)
                ),
            ),
            input_output_aliases={4: 0} if into else {},
            compiler_params=PARAMS,
            cost_estimate=cost(row_count * features * group_width * n, 4 << 20),
            name="gradient_terms",
        )(places.astype(jnp.int32), cot_rows, near, far, *into)

    terms_all = terms(core, own_near, own_far)
    terms_all = terms(1 - core, other_near, other_far, terms_all)
    grad_out = lax.psum_scatter(
        terms_all, "zl", scatter_dimension=0, tiled=False, axis_index_groups=[line]
    )

    vmem = pl.BlockSpec(memory_space=pltpu.VMEM)
    branch_out = pl.pallas_call(
        functools.partial(output_kernel, slots),
        out_shape=jax.ShapeDtypeStruct((row_count, features), BF16),
        in_specs=[pl.BlockSpec(memory_space=pltpu.SMEM)] + [vmem] * 6,
        out_specs=vmem,
        compiler_params=PARAMS,
        cost_estimate=cost(2 * row_count * features * group_width * n, 8 << 20),
        name="output_projection",
    )(
        jnp.reshape(core, (1,)).astype(jnp.int32),
        heads_all,
        own_near,
        own_far,
        other_near,
        other_far,
        spread,
    )

    grads = pl.pallas_call(
        functools.partial(backward_kernel, scale),
        out_shape=(tokens, tokens, tokens),
        grid=(local_heads,),
        in_specs=[head] * 3 + [square, head],
        out_specs=(head, head, head),
        compiler_params=WIDE,
        cost_estimate=cost(4 * attention_flops, 1 << 21),
        name="attention_backward",
    )(queries, keys, values, soft, grad_out)
    return (branch_out, *grads)


def solution(mesh):
    fine = Mesh(mesh.devices.reshape(SIZES), (*DP, "zl"))
    tokens = P(DP, "zl")
    return jax.shard_map(
        on_device,
        mesh=fine,
        in_specs=(tokens, tokens, tokens, P(None, ("zl", *DP)), tokens),
        out_specs=(tokens, tokens, tokens, tokens),
        check_vma=False,
    )
```

time: 207 us -> 181 us (0.87)
  waiting for transfers between devices: 119 us -> 60.8 us
  starting transfers between devices: 43 us -> 70.2 us
  Pallas kernels: 14.4 us -> 22.2 us
    all_gather x1 -> x0, waiting for transfers between devices: 48.9 us -> none  [on_device(): lax.all_gather(block, ('core', 'y'), axis=0, tiled=True, axis_index_group...]
    ppermute x6 -> x14, starting transfers between devices: 42.9 us -> 70.1 us  [shift(): return lax.ppermute(block, axis, [(i, (i + by) % n) for i in range(n)])]
    all_gather x1, waiting for transfers between devices: 19.2 us -> 7.05 us  [on_device(): heads_all = lax.all_gather(head_out, 'zl', axis=0, axis_index_groups=[line])]
    ppermute x6 -> x14, waiting for transfers between devices: 5.26 us -> 9.14 us  [shift(): return lax.ppermute(block, axis, [(i, (i + by) % n) for i in range(n)])]
    unnamed x30 -> x23, local copies, waits for them, and re-layouts: 9.17 us -> 5.97 us
    pallas_call x2, Pallas kernels: 6.48 us -> 9.65 us  [terms(): pl.pallas_call(terms_kernel, out_shape=jax.ShapeDtypeStruct((n, row_count...]
  transfers between devices with their start and end apart: 9 -> 16, of which waited for: 7 -> 8; matrix products, arithmetic and copies ran while one was open for 2% -> 4% of each run, Pallas kernels for 4% -> 8%
where the time goes in v4:
time: 181 us; the launch traced here: 178 us
  starting transfers between devices  70.2 us (39%)
  waiting for transfers between devices  60.8 us (34%)
  Pallas kernels  22.2 us (12%)
  between operations  14.4 us (8%)
  local copies, waits for them, and re-layouts  7.76 us (4%)
    ppermute x14, starting transfers between devices, shift(): return lax.ppermute(block, axis, [(i, (i + by) % n) for i in range(n)])  70.1 us
    reduce_scatter x1, waiting for transfers between devices, on_device(): lax.psum_scatter(terms_all, 'zl', scatter_dimension=0, tiled=False, axis_...  44.6 us
    pallas_call x2, Pallas kernels, terms(): pl.pallas_call(terms_kernel, out_shape=jax.ShapeDtypeStruct((n, row_count...  9.65 us
    ppermute x14, waiting for transfers between devices, shift(): return lax.ppermute(block, axis, [(i, (i + by) % n) for i in range(n)])  9.14 us
    all_gather x1, waiting for transfers between devices, on_device(): heads_all = lax.all_gather(head_out, 'zl', axis=0, axis_index_groups=[line])  7.05 us
    unnamed x23, local copies, waits for them, and re-layouts  5.97 us
    pallas_call x1, Pallas kernels, on_device(): pl.pallas_call(functools.partial(output_kernel, slots), out_shape=jax.Sha...  5.19 us
    pallas_call x1, Pallas kernels, on_device(): pl.pallas_call(functools.partial(backward_kernel, scale), out_shape=(toke...  3.77 us
  transfers between devices with their start and end apart: 16, of which 8 were waited for; matrix products, arithmetic and copies ran while one was open for 4% of the time, Pallas kernels for 8%

profile of v4, /device:TPU:1, one launch (start us, length us, event | category | flops | bytes accessed | tf_op | source)
XLA Modules:
  0.0 177.9 jit_solution(1049167875263814317)
XLA Ops:
  7.2 0.0 copy-start
  7.2 0.0 copy-start.4
  7.2 0.0 all-gather.3.cloned.1.call-start
  7.2 20.0 %collective-permute-start = (bf16[6,3072]{1,0:T(8,128)(2,1)}, bf16[6,3072]{1,0:T(8,128)(2,1)S(1)}, u32[]{:S(2)}, u32[]{:S(2)}) collective-permute-start(bf16[6,3072]{1,0:T(8,128)(2,1)} %bitcast.13), channel_id=1, source_target_pairs={{0,512},{512,0},{1,513},{513,1},{2,514},{514,2},{3,515},{515,3},{4... | collective-permute-start | bytes 110600 | tf_op jit(solution)/shard_map/ppermute | solution.py:30
  27.3 0.8 fusion.12
  28.1 0.0 copy-done
  28.1 1.4 fusion.3.cot_ref
  29.5 3.5 %attention_forward.1 = (bf16[256,384]{1,0:T(8,128)(2,1)}, f32[3,256,256]{2,1,0:T(8,128)}) custom-call(bf16[256,384]{1,0:T(8,128)(2,1)} %q_ref.3, bf16[256,384]{1,0:T(8,128)(2,1)} %k_ref.3, bf16[256,384]{1,0:T(8,128)(2,1)} %v_ref.3), custom_call_target="tpu_custom_call" | custom-call | flops 100663296 | bytes 2097152 | tf_op jit(solution)/shard_map/attention_forward/pallas_call | solution.py:160
  33.0 0.0 collective-permute-done
  33.0 0.0 copy-done.4
  33.2 5.3 %collective-permute-start.1 = (bf16[2,6,1536]{2,1,0:T(8,128)(2,1)S(1)}, bf16[2,6,1536]{2,1,0:T(8,128)(2,1)S(1)}, u32[]{:S(2)}, u32[]{:S(2)}) collective-permute-start(bf16[2,6,1536]{2,1,0:T(8,128)(2,1)S(1)} %constant_dynamic-slice_fusion), channel_id=1, source_target_pairs={{0,8},{8,0},{1,9},{9,1},{2,10},{10,2},{3,11},{11,3},{4,12},{12,4},... | collective-permute-start | bytes 110600 | tf_op jit(solution)/shard_map/ppermute | solution.py:30
  38.4 0.0 all-gather.3.cloned.1.call-update
  38.5 0.0 reduce-scatter.2.cloned.1.call-start
  38.5 0.8 collective-permute-done.1
  39.4 1.9 %collective-permute-start.4 = (bf16[24,1536]{1,0:T(8,128)(2,1)S(1)}, bf16[24,1536]{1,0:T(8,128)(2,1)S(1)}, u32[]{:S(2)}, u32[]{:S(2)}) collective-permute-start(bf16[24,1536]{1,0:T(8,128)(2,1)S(1)} %reshape.20), channel_id=1, source_target_pairs={{0,16},{16,32},{32,48},{48,0},{1,17},{17,33},{33,49},{49,1},{2,18}... | collective-permute-start | bytes 221192 | tf_op jit(solution)/shard_map/ppermute | solution.py:30
  41.3 3.1 %collective-permute-start.3 = (bf16[24,1536]{1,0:T(8,128)(2,1)S(1)}, bf16[24,1536]{1,0:T(8,128)(2,1)S(1)}, u32[]{:S(2)}, u32[]{:S(2)}) collective-permute-start(bf16[24,1536]{1,0:T(8,128)(2,1)S(1)} %reshape.20), channel_id=1, source_target_pairs={{0,32},{16,48},{32,0},{48,16},{1,33},{17,49},{33,1},{49,17},{2,34}... | collective-permute-start | bytes 221192 | tf_op jit(solution)/shard_map/ppermute | solution.py:30
  44.5 3.4 %collective-permute-start.2 = (bf16[24,1536]{1,0:T(8,128)(2,1)S(1)}, bf16[24,1536]{1,0:T(8,128)(2,1)S(1)}, u32[]{:S(2)}, u32[]{:S(2)}) collective-permute-start(bf16[24,1536]{1,0:T(8,128)(2,1)S(1)} %reshape.20), channel_id=1, source_target_pairs={{0,48},{16,0},{32,16},{48,32},{1,49},{17,1},{33,17},{49,33},{2,50}... | collective-permute-start | bytes 221192 | tf_op jit(solution)/shard_map/ppermute | solution.py:30
  47.9 2.3 %collective-permute-done.2 = bf16[24,1536]{1,0:T(8,128)(2,1)S(1)} collective-permute-done((bf16[24,1536]{1,0:T(8,128)(2,1)S(1)}, bf16[24,1536]{1,0:T(8,128)(2,1)S(1)}, u32[]{:S(2)}, u32[]{:S(2)}) %collective-permute-start.2) | collective-permute-done | bytes 73760 | tf_op jit(solution)/shard_map/ppermute | solution.py:30
  50.2 0.0 collective-permute-done.3
  50.2 0.0 collective-permute-done.4
  50.2 4.5 %collective-permute-start.8 = (bf16[96,1536]{1,0:T(8,128)(2,1)S(1)}, bf16[96,1536]{1,0:T(8,128)(2,1)S(1)}, u32[]{:S(2)}, u32[]{:S(2)}) collective-permute-start(bf16[96,1536]{1,0:T(8,128)(2,1)S(1)} %get-tuple-element.25), channel_id=1, source_target_pairs={{0,448},{64,0},{128,64},{192,128},{256,192},{320,256},{384,320},{4... | collective-permute-start | bytes 884744 | tf_op jit(solution)/shard_map/ppermute | solution.py:30
  54.8 1.9 %collective-permute-start.5 = (bf16[96,1536]{1,0:T(8,128)(2,1)S(1)}, bf16[96,1536]{1,0:T(8,128)(2,1)S(1)}, u32[]{:S(2)}, u32[]{:S(2)}) collective-permute-start(bf16[96,1536]{1,0:T(8,128)(2,1)S(1)} %get-tuple-element.25), channel_id=1, source_target_pairs={{0,64},{64,128},{128,192},{192,256},{256,320},{320,384},{384,448},... | collective-permute-start | bytes 884744 | tf_op jit(solution)/shard_map/ppermute | solution.py:30
  56.7 2.3 %collective-permute-done.8 = bf16[96,1536]{1,0:T(8,128)(2,1)S(1)} collective-permute-done((bf16[96,1536]{1,0:T(8,128)(2,1)S(1)}, bf16[96,1536]{1,0:T(8,128)(2,1)S(1)}, u32[]{:S(2)}, u32[]{:S(2)}) %collective-permute-start.8) | collective-permute-done | bytes 294944 | tf_op jit(solution)/shard_map/ppermute | solution.py:30
  59.0 5.4 %collective-permute-start.9 = (bf16[96,1536]{1,0:T(8,128)(2,1)S(1)}, bf16[96,1536]{1,0:T(8,128)(2,1)}, u32[]{:S(2)}, u32[]{:S(2)}) collective-permute-start(bf16[96,1536]{1,0:T(8,128)(2,1)S(1)} %collective-permute-done.8), channel_id=1, source_target_pairs={{0,448},{64,0},{128,64},{192,128},{256,192},{320,256},{384,320},{4... | collective-permute-start | bytes 884744 | tf_op jit(solution)/shard_map/ppermute | solution.py:30
  64.3 0.0 collective-permute-done.5
  64.4 1.9 %collective-permute-start.6 = (bf16[96,1536]{1,0:T(8,128)(2,1)S(1)}, bf16[96,1536]{1,0:T(8,128)(2,1)S(1)}, u32[]{:S(2)}, u32[]{:S(2)}) collective-permute-start(bf16[96,1536]{1,0:T(8,128)(2,1)S(1)} %collective-permute-done.5), channel_id=1, source_target_pairs={{0,64},{64,128},{128,192},{192,256},{256,320},{320,384},{384,448},... | collective-permute-start | bytes 884744 | tf_op jit(solution)/shard_map/ppermute | solution.py:30
  66.3 0.0 copy-start.5
  66.4 0.0 copy-start.6
  66.4 1.6 collective-permute-done.9
  68.0 5.1 %collective-permute-start.10 = (bf16[96,1536]{1,0:T(8,128)(2,1)}, bf16[96,1536]{1,0:T(8,128)(2,1)}, u32[]{:S(2)}, u32[]{:S(2)}) collective-permute-start(bf16[96,1536]{1,0:T(8,128)(2,1)} %collective-permute-done.9), channel_id=1, source_target_pairs={{0,448},{64,0},{128,64},{192,128},{256,192},{320,256},{384,320},{4... | collective-permute-start | bytes 884744 | tf_op jit(solution)/shard_map/ppermute | solution.py:30
  73.1 0.3 collective-permute-done.6
  73.4 1.9 %collective-permute-start.7 = (bf16[96,1536]{1,0:T(8,128)(2,1)S(1)}, bf16[96,1536]{1,0:T(8,128)(2,1)}, u32[]{:S(2)}, u32[]{:S(2)}) collective-permute-start(bf16[96,1536]{1,0:T(8,128)(2,1)S(1)} %collective-permute-done.6), channel_id=1, source_target_pairs={{0,64},{64,128},{128,192},{192,256},{256,320},{320,384},{384,448},... | collective-permute-start | bytes 884744 | tf_op jit(solution)/shard_map/ppermute | solution.py:30
  75.3 1.0 constant_dynamic-update-slice_fusion.4.own_near.near_ref
  76.3 6.1 %collective-permute-start.12 = (bf16[480,1536]{1,0:T(8,128)(2,1)S(1)}, bf16[480,1536]{1,0:T(8,128)(2,1)S(1)}, u32[]{:S(2)}, u32[]{:S(2)}) collective-permute-start(bf16[480,1536]{1,0:T(8,128)(2,1)S(1)} %constant_dynamic-update-slice_fusion.4.own_near.near_ref), channel_id=1, source_target_pairs={{0,8},{8,0},{1,9},{9,1},{2,10},{10,2},{3,11},{11,3},{4,12},{12,4},... | collective-permute-start | bytes 4423688 | tf_op jit(solution)/shard_map/ppermute | solution.py:30
  82.4 0.0 collective-permute-done.7
  82.4 7.1 %all-gather.3.cloned.1.call-done = bf16[2048,384]{1,0:T(8,128)(2,1)} async-done(((bf16[256,384]{1,0:T(8,128)(2,1)}), bf16[2048,384]{1,0:T(8,128)(2,1)}) %all-gather.3.cloned.1.call-update) | async-done | bytes 1572880 | tf_op jit(solution)/shard_map/all_gather | solution.py:173
  89.4 3.5 %collective-permute-start.11 = (bf16[96,1536]{1,0:T(8,128)(2,1)}, bf16[96,1536]{1,0:T(8,128)(2,1)S(1)}, u32[]{:S(2)}, u32[]{:S(2)}) collective-permute-start(bf16[96,1536]{1,0:T(8,128)(2,1)} %collective-permute-done.7), channel_id=1, source_target_pairs={{0,64},{64,128},{128,192},{192,256},{256,320},{320,384},{384,448},... | collective-permute-start | bytes 884744 | tf_op jit(solution)/shard_map/ppermute | solution.py:30
  93.0 1.7 constant_dynamic-update-slice_fusion.14
  94.7 0.0 collective-permute-done.10
  94.7 1.7 constant_dynamic-update-slice_fusion.13
  96.4 1.9 %collective-permute-done.11 = bf16[96,1536]{1,0:T(8,128)(2,1)S(1)} collective-permute-done((bf16[96,1536]{1,0:T(8,128)(2,1)}, bf16[96,1536]{1,0:T(8,128)(2,1)S(1)}, u32[]{:S(2)}, u32[]{:S(2)}) %collective-permute-start.11) | collective-permute-done | bytes 294944 | tf_op jit(solution)/shard_map/ppermute | solution.py:30
  98.3 0.7 constant_dynamic-update-slice_fusion.12.own_far.far_ref
  99.0 6.0 %collective-permute-start.13 = (bf16[288,1536]{1,0:T(8,128)(2,1)}, bf16[288,1536]{1,0:T(8,128)(2,1)}, u32[]{:S(2)}, u32[]{:S(2)}) collective-permute-start(bf16[288,1536]{1,0:T(8,128)(2,1)} %constant_dynamic-update-slice_fusion.12.own_far.far_ref), channel_id=1, source_target_pairs={{0,8},{8,0},{1,9},{9,1},{2,10},{10,2},{3,11},{11,3},{4,12},{12,4},... | collective-permute-start | bytes 2654216 | tf_op jit(solution)/shard_map/ppermute | solution.py:30
  105.1 0.0 copy-done.5
  105.1 0.0 copy-done.6
  105.1 0.0 copy-start.1
  105.1 1.0 copy-done.1
  106.1 0.0 copy-start.2
  106.1 4.8 %gradient_terms.2.refs_0_ = bf16[8,256,384]{2,1,0:T(8,128)(2,1)} custom-call(s32[4]{0:T(128)S(1)} %get-tuple-element.32.slot_ref, bf16[256,768]{1,0:T(8,128)(2,1)S(1)} %copy-done.1, bf16[480,1536]{1,0:T(8,128)(2,1)S(1)} %constant_dynamic-update-slice_fusion.4.own_near.near_ref, bf16[288,1536]{1,0:T(8,128)(2,1)} %constant_dynamic-update-slice_fusion.12.own_far.far_ref), custom_call_target="tpu_custom_call" | custom-call | flops 603979776 | bytes 4194304 | tf_op jit(solution)/shard_map/gradient_terms/pallas_call | solution.py:187
  110.9 0.0 collective-permute-done.12.other_near.near_ref
  110.9 0.0 collective-permute-done.13.other_far.far_ref
  110.9 0.0 copy-done.2
  110.9 4.8 %gradient_terms.3 = bf16[8,256,384]{2,1,0:T(8,128)(2,1)} custom-call(s32[4]{0:T(128)S(1)} %get-tuple-element.33.slot_ref, bf16[256,768]{1,0:T(8,128)(2,1)S(1)} %copy-done.2, bf16[480,1536]{1,0:T(8,128)(2,1)S(1)} %collective-permute-done.12.other_near.near_ref, ...), custom_call_target="tpu_custom_call", output_to_operand_aliasing={{}: (4, {})} | custom-call | flops 603979776 | bytes 4194304 | tf_op jit(solution)/shard_map/gradient_terms/pallas_call | solution.py:187
  115.8 0.0 reduce-scatter.2.cloned.1.call-update
  115.8 0.3 fusion.s_ref
  116.1 0.0 copy-start.3
  116.1 1.4 copy-done.3
  117.5 5.2 %output_projection.1 = bf16[256,768]{1,0:T(8,128)(2,1)} custom-call(s32[1]{0:T(128)} %bitcast.core_ref, bf16[8,256,384]{2,1,0:T(8,128)(2,1)S(1)} %bitcast.11, bf16[480,1536]{1,0:T(8,128)(2,1)S(1)} %constant_dynamic-update-slice_fusion.4.own_near.near_ref, bf16[288,1536]{1,0:T(8,128)(2,1)} %constant_dynamic-update-slice_fusion.12.own_far.far_ref, ...), custom_call_target="tpu_custom_call" | custom-call | flops 1207959552 | bytes 8388608 | tf_op jit(solution)/shard_map/output_projection/pallas_call | solution.py:216
  122.7 44.6 %reduce-scatter.2.cloned.1.call-done = bf16[1,256,384]{2,1,0:T(8,128)(2,1)} async-done(((bf16[8,256,384]{2,1,0:T(8,128)(2,1)}), bf16[1,256,384]{2,1,0:T(8,128)(2,1)}) %reduce-scatter.2.cloned.1.call-update) | async-done | bytes 196624 | tf_op jit(solution)/shard_map/reduce_scatter | solution.py:211
  167.3 3.8 %attention_backward.1 = (bf16[256,384]{1,0:T(8,128)(2,1)}, bf16[256,384]{1,0:T(8,128)(2,1)}, bf16[256,384]{1,0:T(8,128)(2,1)}) custom-call(bf16[256,384]{1,0:T(8,128)(2,1)} %q_ref.3, bf16[256,384]{1,0:T(8,128)(2,1)} %k_ref.3, bf16[256,384]{1,0:T(8,128)(2,1)} %v_ref.3, f32[3,256,256]{2,1,0:T(8,128)} %get-tuple-element.17.p_ref, bf16[256,384]{1,0:T(8,128)(2,1)} %bitcast.12), custom_call_target="tpu_custom_call" | custom-call | flops 201326592 | bytes 2097152 | tf_op jit(solution)/shard_map/attention_backward/pallas_call | solution.py:234
  (15 shorter events, 0.3 us)
Async XLA Ops:
  7.2 20.9 %copy-start = (bf16[256,768]{1,0:T(8,128)(2,1)S(1)}, bf16[256,768]{1,0:T(8,128)(2,1)}, u32[]{:S(2)}) copy-start(bf16[256,768]{1,0:T(8,128)(2,1)} %param.18) | copy-start | bytes 1179652
  7.2 25.9 %copy-start.4 = (bf16[3072,6]{0,1:T(8,128)(2,1)S(1)}, bf16[3072,6]{0,1:T(8,128)(2,1)}, u32[]{:S(2)}) copy-start(bf16[3072,6]{0,1:T(8,128)(2,1)} %param.17) | copy-start | bytes 110596
  7.2 82.2 %all-gather.3.cloned.1.call-start = ((), (), s32[]{:S(2)}) async-start(), calls=%async_computation.2 | async-start | bytes 1769472 | tf_op jit(solution)/shard_map/all_gather | solution.py:173
  7.2 25.8 %collective-permute-start = (bf16[6,3072]{1,0:T(8,128)(2,1)}, bf16[6,3072]{1,0:T(8,128)(2,1)S(1)}, u32[]{:S(2)}, u32[]{:S(2)}) collective-permute-start(bf16[6,3072]{1,0:T(8,128)(2,1)} %bitcast.13), channel_id=1, source_target_pairs={{0,512},{512,0},{1,513},{513,1},{2,514},{514,2},{3,515},{515,3},{4... | collective-permute-start | bytes 110600 | tf_op jit(solution)/shard_map/ppermute | solution.py:30
  33.2 6.2 %collective-permute-start.1 = (bf16[2,6,1536]{2,1,0:T(8,128)(2,1)S(1)}, bf16[2,6,1536]{2,1,0:T(8,128)(2,1)S(1)}, u32[]{:S(2)}, u32[]{:S(2)}) collective-permute-start(bf16[2,6,1536]{2,1,0:T(8,128)(2,1)S(1)} %constant_dynamic-slice_fusion), channel_id=1, source_target_pairs={{0,8},{8,0},{1,9},{9,1},{2,10},{10,2},{3,11},{11,3},{4,12},{12,4},... | collective-permute-start | bytes 110600 | tf_op jit(solution)/shard_map/ppermute | solution.py:30
  38.5 128.8 %reduce-scatter.2.cloned.1.call-start = ((), (), s32[]{:S(2)}) async-start(), calls=%async_computation.1 | async-start | bytes 1769472 | tf_op jit(solution)/shard_map/reduce_scatter | solution.py:211
  39.4 10.8 %collective-permute-start.4 = (bf16[24,1536]{1,0:T(8,128)(2,1)S(1)}, bf16[24,1536]{1,0:T(8,128)(2,1)S(1)}, u32[]{:S(2)}, u32[]{:S(2)}) collective-permute-start(bf16[24,1536]{1,0:T(8,128)(2,1)S(1)} %reshape.20), channel_id=1, source_target_pairs={{0,16},{16,32},{32,48},{48,0},{1,17},{17,33},{33,49},{49,1},{2,18}... | collective-permute-start | bytes 221192 | tf_op jit(solution)/shard_map/ppermute | solution.py:30
  41.3 8.8 %collective-permute-start.3 = (bf16[24,1536]{1,0:T(8,128)(2,1)S(1)}, bf16[24,1536]{1,0:T(8,128)(2,1)S(1)}, u32[]{:S(2)}, u32[]{:S(2)}) collective-permute-start(bf16[24,1536]{1,0:T(8,128)(2,1)S(1)} %reshape.20), channel_id=1, source_target_pairs={{0,32},{16,48},{32,0},{48,16},{1,33},{17,49},{33,1},{49,17},{2,34}... | collective-permute-start | bytes 221192 | tf_op jit(solution)/shard_map/ppermute | solution.py:30
  44.5 5.7 %collective-permute-start.2 = (bf16[24,1536]{1,0:T(8,128)(2,1)S(1)}, bf16[24,1536]{1,0:T(8,128)(2,1)S(1)}, u32[]{:S(2)}, u32[]{:S(2)}) collective-permute-start(bf16[24,1536]{1,0:T(8,128)(2,1)S(1)} %reshape.20), channel_id=1, source_target_pairs={{0,48},{16,0},{32,16},{48,32},{1,49},{17,1},{33,17},{49,33},{2,50}... | collective-permute-start | bytes 221192 | tf_op jit(solution)/shard_map/ppermute | solution.py:30
  50.2 8.8 %collective-permute-start.8 = (bf16[96,1536]{1,0:T(8,128)(2,1)S(1)}, bf16[96,1536]{1,0:T(8,128)(2,1)S(1)}, u32[]{:S(2)}, u32[]{:S(2)}) collective-permute-start(bf16[96,1536]{1,0:T(8,128)(2,1)S(1)} %get-tuple-element.25), channel_id=1, source_target_pairs={{0,448},{64,0},{128,64},{192,128},{256,192},{320,256},{384,320},{4... | collective-permute-start | bytes 884744 | tf_op jit(solution)/shard_map/ppermute | solution.py:30
  54.8 9.6 %collective-permute-start.5 = (bf16[96,1536]{1,0:T(8,128)(2,1)S(1)}, bf16[96,1536]{1,0:T(8,128)(2,1)S(1)}, u32[]{:S(2)}, u32[]{:S(2)}) collective-permute-start(bf16[96,1536]{1,0:T(8,128)(2,1)S(1)} %get-tuple-element.25), channel_id=1, source_target_pairs={{0,64},{64,128},{128,192},{192,256},{256,320},{320,384},{384,448},... | collective-permute-start | bytes 884744 | tf_op jit(solution)/shard_map/ppermute | solution.py:30
  59.0 9.0 %collective-permute-start.9 = (bf16[96,1536]{1,0:T(8,128)(2,1)S(1)}, bf16[96,1536]{1,0:T(8,128)(2,1)}, u32[]{:S(2)}, u32[]{:S(2)}) collective-permute-start(bf16[96,1536]{1,0:T(8,128)(2,1)S(1)} %collective-permute-done.8), channel_id=1, source_target_pairs={{0,448},{64,0},{128,64},{192,128},{256,192},{320,256},{384,320},{4... | collective-permute-start | bytes 884744 | tf_op jit(solution)/shard_map/ppermute | solution.py:30
  64.4 9.0 %collective-permute-start.6 = (bf16[96,1536]{1,0:T(8,128)(2,1)S(1)}, bf16[96,1536]{1,0:T(8,128)(2,1)S(1)}, u32[]{:S(2)}, u32[]{:S(2)}) collective-permute-start(bf16[96,1536]{1,0:T(8,128)(2,1)S(1)} %collective-permute-done.5), channel_id=1, source_target_pairs={{0,64},{64,128},{128,192},{192,256},{256,320},{320,384},{384,448},... | collective-permute-start | bytes 884744 | tf_op jit(solution)/shard_map/ppermute | solution.py:30
  66.3 38.7 %copy-start.5 = (s32[4]{0:T(128)S(1)}, s32[4]{0:T(128)}, u32[]{:S(2)}) copy-start(s32[4]{0:T(128)} %constant.88.clone) | copy-start | bytes 52
  66.4 38.7 %copy-start.6 = (s32[4]{0:T(128)S(1)}, s32[4]{0:T(128)}, u32[]{:S(2)}) copy-start(s32[4]{0:T(128)} %constant.87.clone) | copy-start | bytes 52
  68.0 26.7 %collective-permute-start.10 = (bf16[96,1536]{1,0:T(8,128)(2,1)}, bf16[96,1536]{1,0:T(8,128)(2,1)}, u32[]{:S(2)}, u32[]{:S(2)}) collective-permute-start(bf16[96,1536]{1,0:T(8,128)(2,1)} %collective-permute-done.9), channel_id=1, source_target_pairs={{0,448},{64,0},{128,64},{192,128},{256,192},{320,256},{384,320},{4... | collective-permute-start | bytes 884744 | tf_op jit(solution)/shard_map/ppermute | solution.py:30
  73.4 9.0 %collective-permute-start.7 = (bf16[96,1536]{1,0:T(8,128)(2,1)S(1)}, bf16[96,1536]{1,0:T(8,128)(2,1)}, u32[]{:S(2)}, u32[]{:S(2)}) collective-permute-start(bf16[96,1536]{1,0:T(8,128)(2,1)S(1)} %collective-permute-done.6), channel_id=1, source_target_pairs={{0,64},{64,128},{128,192},{192,256},{256,320},{320,384},{384,448},... | collective-permute-start | bytes 884744 | tf_op jit(solution)/shard_map/ppermute | solution.py:30
  76.3 34.6 %collective-permute-start.12 = (bf16[480,1536]{1,0:T(8,128)(2,1)S(1)}, bf16[480,1536]{1,0:T(8,128)(2,1)S(1)}, u32[]{:S(2)}, u32[]{:S(2)}) collective-permute-start(bf16[480,1536]{1,0:T(8,128)(2,1)S(1)} %constant_dynamic-update-slice_fusion.4.own_near.near_ref), channel_id=1, source_target_pairs={{0,8},{8,0},{1,9},{9,1},{2,10},{10,2},{3,11},{11,3},{4,12},{12,4},... | collective-permute-start | bytes 4423688 | tf_op jit(solution)/shard_map/ppermute | solution.py:30
  89.4 8.9 %collective-permute-start.11 = (bf16[96,1536]{1,0:T(8,128)(2,1)}, bf16[96,1536]{1,0:T(8,128)(2,1)S(1)}, u32[]{:S(2)}, u32[]{:S(2)}) collective-permute-start(bf16[96,1536]{1,0:T(8,128)(2,1)} %collective-permute-done.7), channel_id=1, source_target_pairs={{0,64},{64,128},{128,192},{192,256},{256,320},{320,384},{384,448},... | collective-permute-start | bytes 884744 | tf_op jit(solution)/shard_map/ppermute | solution.py:30
  99.0 11.9 %collective-permute-start.13 = (bf16[288,1536]{1,0:T(8,128)(2,1)}, bf16[288,1536]{1,0:T(8,128)(2,1)}, u32[]{:S(2)}, u32[]{:S(2)}) collective-permute-start(bf16[288,1536]{1,0:T(8,128)(2,1)} %constant_dynamic-update-slice_fusion.12.own_far.far_ref), channel_id=1, source_target_pairs={{0,8},{8,0},{1,9},{9,1},{2,10},{10,2},{3,11},{11,3},{4,12},{12,4},... | collective-permute-start | bytes 2654216 | tf_op jit(solution)/shard_map/ppermute | solution.py:30
  105.1 1.0 copy-start.1
  106.1 4.8 %copy-start.2 = (bf16[256,768]{1,0:T(8,128)(2,1)S(1)}, bf16[256,768]{1,0:T(8,128)(2,1)}, u32[]{:S(2)}) copy-start(bf16[256,768]{1,0:T(8,128)(2,1)} %fusion.3.cot_ref) | copy-start | bytes 1179652
  116.1 1.4 copy-start.3
Sparse Core Ops, SparseCore 0:
  38.6 50.7 all-gather.2
  115.9 51.2 reduce-scatter.1

commit v5 on v4

--- a/solution.py
+++ b/solution.py
@@ -70,21 +70,45 @@
     dk_ref[...] = (dot_tn(score_grad, q_ref[...]) * scale).astype(BF16)
 
 
-def terms_kernel(slot_ref, cot_ref, near_ref, far_ref, *refs):
-    near = near_ref.shape[0]
-    total = dot(cot_ref[:, :near], near_ref[...]) + dot(cot_ref[:, near:], far_ref[...])
-    refs[-1][0] = total.astype(BF16)
-
-
-def output_kernel(slots, core_ref, o_ref, own_near, own_far, other_near, other_far, s_ref, out_ref):
+def sums_kernel(cot_ref, near_ref, out_ref):
+    out_ref[...] = dot(cot_ref[:, : near_ref.shape[0]], near_ref[...])
+
+
+def terms_kernel(
+    slots, at_ref, cot_ref, own_sum, other_sum, own_mid, own_last, other_mid, other_last, out_ref
+):
+    width = out_ref.shape[2]
+    last = cot_ref.shape[1] - own_last.shape[0]
+    mid = last - own_mid.shape[0]
+    for core in range(2):
+
+        @pl.when(at_ref[0] == core)
+        def _():
+            for half, sum_ref, mid_ref, last_ref in (
+                (core, own_sum, own_mid, own_last),
+                (1 - core, other_sum, other_mid, other_last),
+            ):
+                for i, slot in enumerate(slots[half]):
+                    cols = pl.ds(pl.multiple_of((2 * i + at_ref[1]) * width, width), width)
+                    term = sum_ref[:, cols] + dot(cot_ref[:, mid:last], mid_ref[:, cols])
+                    term += dot(cot_ref[:, last:], last_ref[:, cols])
+                    out_ref[slot] = term.astype(BF16)
+
+
+def output_kernel(
+    slots, core_ref, o_ref, own_near, own_mid, own_last, other_near, other_mid, other_last, s_ref, out_ref
+):
     width = o_ref.shape[2]
-    near = own_near.shape[0]
     for core in range(2):
 
         @pl.when(core_ref[0] == core)
         def _():
-            total = None
-            for place, (first, last) in ((0, (own_near, other_near)), (near, (own_far, other_far))):
+            total, place = None, 0
+            for first, last in (
+                (own_near, other_near),
+                (own_mid, other_mid),
+                (own_last, other_last),
+            ):
                 rows = None
                 for half, w_ref in ((core, first), (1 - core, last)):
                     for j, slot in enumerate(slots[half]):
@@ -92,6 +116,7 @@
                         rows = term if rows is None else rows + term
                 placed = dot(rows.astype(BF16), s_ref[place : place + rows.shape[1], :])
                 total = placed if total is None else total + placed
+                place += rows.shape[1]
             out_ref[...] = total.astype(BF16)
 
 
@@ -104,19 +129,17 @@
     return np.array(offsets)
 
 
-def ring_gather(block, axis, beside, join):
+def ring_gather(block, axis):
     n = lax.axis_size(axis)
     up = down = block
     blocks = [block]
     for step in range(1, n // 2 + 1):
-        if step == join:
-            up, beside = lax.optimization_barrier((up, beside))
         up = shift(up, axis, 1)
         blocks.append(up)
         if 2 * step < n:
             down = shift(down, axis, -1)
             blocks.append(down)
-    return blocks, beside
+    return blocks
 
 
 def spread_of(rows_dev, features):
@@ -149,8 +172,14 @@
     ny = lax.axis_size("y")
     core = lax.axis_index("core")
     scale = 1.0 / math.sqrt(HD)
-    line = folded(n)
-    slots = [[line.index(h * n // 2 + j) for j in range(n // 2)] for h in range(2)]
+    half_line = folded(n // 2)
+    same_parity = [[2 * m + q for m in half_line] for q in range(2)]
+    pairs = [(i, i ^ 1) for i in range(n)]
+    parity = lax.axis_index("zl") % 2
+    slots = [
+        [2 * half_line.index((h * n // 2 + j) // 2) + j % 2 for j in range(n // 2)]
+        for h in range(2)
+    ]
     tokens = jax.ShapeDtypeStruct((row_count, group_width), BF16)
 
     attention_flops = 2 * row_count * row_count * group_width
@@ -170,53 +199,85 @@
         cost_estimate=cost(2 * attention_flops, 1 << 21, local_heads * row_count**2),
         name="attention_forward",
     )(queries, keys, values)
-    heads_all = lax.all_gather(head_out, "zl", axis=0, axis_index_groups=[line])
+    pair_out = lax.ppermute(head_out, "zl", pairs)
+    heads_pair = jnp.stack(
+        [
+            jnp.where(parity == 0, head_out, pair_out),
+            jnp.where(parity == 0, pair_out, head_out),
+        ],
+        0,
+    )
+    heads_all = lax.all_gather(
+        heads_pair, "zl", axis=0, tiled=True, axis_index_groups=same_parity
+    )
     spread = spread_of(w_out.shape[1], features)
     cot_rows = dot_nt(cotangent, spread).astype(BF16)
 
     across, head_out, cot_rows = lax.optimization_barrier((across, head_out, cot_rows))
-    blocks, heads_all = ring_gather(first_stage(w_out.T, across), "y", heads_all, 4)
+    blocks = ring_gather(first_stage(w_out.T, across), "y")
     early = 2 * ((ny + 2) // 4) + 1
+    vmem = pl.BlockSpec(memory_space=pltpu.VMEM)
+    smem = pl.BlockSpec(memory_space=pltpu.SMEM)
+
+    def sums(near):
+        return pl.pallas_call(
+            sums_kernel,
+            out_shape=jax.ShapeDtypeStruct((row_count, near.shape[1]), F32),
+            in_specs=[vmem] * 2,
+            out_specs=vmem,
+            compiler_params=PARAMS,
+            cost_estimate=cost(row_count * features * group_width * n, 4 << 20),
+            name="gradient_sums",
+        )(cot_rows, near)
+
     own_near = jnp.concatenate(blocks[:early], 0)
     other_near = shift(own_near, "core", 1)
-    own_far = jnp.concatenate(blocks[early:], 0)
-    other_far = shift(own_far, "core", 1)
-
-    def terms(half, near, far, *into):
-        places = jnp.where(half == 0, jnp.asarray(slots[0]), jnp.asarray(slots[1]))
+    own_mid = jnp.concatenate(blocks[early:-1], 0)
+    other_mid = shift(own_mid, "core", 1)
+    own_sum = sums(own_near)
+    other_sum = sums(other_near)
+    own_last, own_sum, other_sum = lax.optimization_barrier(
+        (blocks[-1], own_sum, other_sum)
+    )
+    other_last = shift(own_last, "core", 1)
+
+    pair_slots = [[half_line.index(h * n // 4 + i) for i in range(n // 4)] for h in range(2)]
+
+    def terms(which):
         return pl.pallas_call(
-            terms_kernel,
-            out_shape=jax.ShapeDtypeStruct((n, row_count, group_width), BF16),
-            grid_spec=pltpu.PrefetchScalarGridSpec(
-                num_scalar_prefetch=1,
-                grid=(n // 2,),
-                in_specs=[
-                    pl.BlockSpec((row_count, features), lambda j, place: (0, 0)),
-                    pl.BlockSpec((near.shape[0], group_width), lambda j, place: (0, j)),
-                    pl.BlockSpec((far.shape[0], group_width), lambda j, place: (0, j)),
-                ]
-                + [pl.BlockSpec(memory_space=pl.ANY)] * len(into),
-                out_specs=pl.BlockSpec(
-                    (1, row_count, group_width), lambda j, place: (place[j], 0, 0)
-                ),
-            ),
-            input_output_aliases={4: 0} if into else {},
+            functools.partial(terms_kernel, pair_slots),
+            out_shape=jax.ShapeDtypeStruct((n // 2, row_count, group_width), BF16),
+            in_specs=[smem] + [vmem] * 7,
+            out_specs=vmem,
             compiler_params=PARAMS,
-            cost_estimate=cost(row_count * features * group_width * n, 4 << 20),
+            cost_estimate=cost(row_count * own_last.shape[0] * group_width * n, 4 << 20),
             name="gradient_terms",
-        )(places.astype(jnp.int32), cot_rows, near, far, *into)
-
-    terms_all = terms(core, own_near, own_far)
-    terms_all = terms(1 - core, other_near, other_far, terms_all)
+        )(
+            jnp.stack([core, which]).astype(jnp.int32),
+            cot_rows,
+            own_sum,
+            other_sum,
+            own_mid,
+            own_last,
+            other_mid,
+            other_last,
+        )
+
+    came = lax.ppermute(terms(1 - parity), "zl", pairs)
+    came, heads_all = lax.optimization_barrier((came, heads_all))
+    pair_terms = (terms(parity).astype(F32) + came.astype(F32)).astype(BF16)
     grad_out = lax.psum_scatter(
-        terms_all, "zl", scatter_dimension=0, tiled=False, axis_index_groups=[line]
-    )
-
-    vmem = pl.BlockSpec(memory_space=pltpu.VMEM)
+        pair_terms,
+        "zl",
+        scatter_dimension=0,
+        tiled=False,
+        axis_index_groups=same_parity,
+    )
+
     branch_out = pl.pallas_call(
         functools.partial(output_kernel, slots),
         out_shape=jax.ShapeDtypeStruct((row_count, features), BF16),
-        in_specs=[pl.BlockSpec(memory_space=pltpu.SMEM)] + [vmem] * 6,
+        in_specs=[smem] + [vmem] * 8,
         out_specs=vmem,
         compiler_params=PARAMS,
         cost_estimate=cost(2 * row_count * features * group_width * n, 8 << 20),
@@ -225,9 +286,11 @@
         jnp.reshape(core, (1,)).astype(jnp.int32),
         heads_all,
         own_near,
-        own_far,
+        own_mid,
+        own_last,
         other_near,
-        other_far,
+        other_mid,
+        other_last,
         spread,
     )
 

time: 181 us -> 235 us (1.30)
  waiting for transfers between devices: 60.8 us -> 107 us
  other arithmetic: 1.12 us -> 4.56 us
  local copies, waits for them, and re-layouts: 7.76 us -> 11.1 us
    all_gather x1, waiting for transfers between devices: 7.05 us -> 31.4 us  [on_device(): lax.all_gather(heads_pair, 'zl', axis=0, tiled=True, axis_index_groups=sa...]
    reduce_scatter x1, waiting for transfers between devices: 44.6 us -> 58.8 us  [on_device(): lax.psum_scatter(pair_terms, 'zl', scatter_dimension=0, tiled=False, axis...]
    ppermute x0 -> x2, starting transfers between devices: none -> 4.85 us  [the longest x1 2.44 us: on_device(): pair_out = lax.ppermute(head_out, 'zl', pairs)]
    ppermute x0 -> x2, waiting for transfers between devices: none -> 4.16 us  [the longest x1 4.15 us: on_device(): came = lax.ppermute(terms(1 - parity), 'zl', pairs)]
    ppermute x14 -> x15, waiting for transfers between devices: 9.14 us -> 13.1 us  [shift(): return lax.ppermute(block, axis, [(i, (i + by) % n) for i in range(n)])]
    unnamed x23 -> x24, local copies, waits for them, and re-layouts: 5.97 us -> 9.53 us
    ppermute x14 -> x15, starting transfers between devices: 70.1 us -> 66.8 us  [shift(): return lax.ppermute(block, axis, [(i, (i + by) % n) for i in range(n)])]
    convert_element_type x0 -> x1, other arithmetic: none -> 2.45 us  [on_device(): pair_terms = (terms(parity).astype(F32) + came.astype(F32)).astype(BF16)]
  transfers between devices with their start and end apart: 16 -> 19, of which waited for: 8 -> 12; matrix products, arithmetic and copies ran while one was open for 4% -> 4% of each run, Pallas kernels for 8% -> 9%
where the time goes in v5:
time: 235 us; the launch traced here: 234 us
  waiting for transfers between devices  107 us (46%)
  starting transfers between devices  71.7 us (31%)
  Pallas kernels  23.6 us (10%)
  between operations  14.4 us (6%)
  local copies, waits for them, and re-layouts  11.1 us (5%)
  other arithmetic  4.56 us (2%)
    ppermute x15, starting transfers between devices, shift(): return lax.ppermute(block, axis, [(i, (i + by) % n) for i in range(n)])  66.8 us
    reduce_scatter x1, waiting for transfers between devices, on_device(): lax.psum_scatter(pair_terms, 'zl', scatter_dimension=0, tiled=False, axis...  58.8 us
    all_gather x1, waiting for transfers between devices, on_device(): lax.all_gather(heads_pair, 'zl', axis=0, tiled=True, axis_index_groups=sa...  31.4 us
    ppermute x15, waiting for transfers between devices, shift(): return lax.ppermute(block, axis, [(i, (i + by) % n) for i in range(n)])  13.1 us
    unnamed x24, local copies, waits for them, and re-layouts  9.53 us
    pallas_call x1, Pallas kernels, on_device(): pl.pallas_call(functools.partial(output_kernel, slots), out_shape=jax.Sha...  7.05 us
    pallas_call x2, Pallas kernels, terms(): pl.pallas_call(functools.partial(terms_kernel, pair_slots), out_shape=jax...  5.17 us
  transfers between devices with their start and end apart: 19, of which 12 were waited for; matrix products, arithmetic and copies ran while one was open for 4% of the time, Pallas kernels for 9%

profile of v5, /device:TPU:1, one launch (start us, length us, event | category | flops | bytes accessed | tf_op | source)
XLA Modules:
  0.0 233.5 jit_solution(16479519045455401174)
XLA Ops:
  7.2 0.0 copy-start
  7.2 0.0 all-gather.2.cloned.1.call-start
  7.2 20.0 %collective-permute-start = (bf16[6,3072]{1,0:T(8,128)(2,1)}, bf16[6,3072]{1,0:T(8,128)(2,1)S(1)}, u32[]{:S(2)}, u32[]{:S(2)}) collective-permute-start(bf16[6,3072]{1,0:T(8,128)(2,1)} %bitcast.17), channel_id=1, source_target_pairs={{0,512},{512,0},{1,513},{513,1},{2,514},{514,2},{3,515},{515,3},{4... | collective-permute-start | bytes 110600 | tf_op jit(solution)/shard_map/ppermute | solution.py:30
  27.3 0.8 fusion.12
  28.1 0.7 fusion.3.cot_ref
  28.8 3.7 %attention_forward.1 = (bf16[256,384]{1,0:T(8,128)(2,1)}, f32[3,256,256]{2,1,0:T(8,128)}) custom-call(bf16[256,384]{1,0:T(8,128)(2,1)} %q_ref.3, bf16[256,384]{1,0:T(8,128)(2,1)} %k_ref.3, bf16[256,384]{1,0:T(8,128)(2,1)} %v_ref.3), custom_call_target="tpu_custom_call" | custom-call | flops 100663296 | bytes 2097152 | tf_op jit(solution)/shard_map/attention_forward/pallas_call | solution.py:189
  32.6 5.9 %collective-permute-start.1 = (bf16[2,6,1536]{2,1,0:T(8,128)(2,1)S(1)}, bf16[2,6,1536]{2,1,0:T(8,128)(2,1)S(1)}, u32[]{:S(2)}, u32[]{:S(2)}) collective-permute-start(bf16[2,6,1536]{2,1,0:T(8,128)(2,1)S(1)} %constant_dynamic-slice_fusion), channel_id=1, source_target_pairs={{0,8},{8,0},{1,9},{9,1},{2,10},{10,2},{3,11},{11,3},{4,12},{12,4},... | collective-permute-start | bytes 110600 | tf_op jit(solution)/shard_map/ppermute | solution.py:30
  38.5 0.9 collective-permute-done.1
  39.4 1.9 collective-permute-start.2
  41.3 0.6 constant_dynamic-update-slice_fusion.11
  42.0 1.9 collective-permute-start.3
  43.9 3.4 %collective-permute-start.4 = (bf16[24,1536]{1,0:T(8,128)(2,1)S(1)}, bf16[24,1536]{1,0:T(8,128)(2,1)S(1)}, u32[]{:S(2)}, u32[]{:S(2)}) collective-permute-start(bf16[24,1536]{1,0:T(8,128)(2,1)S(1)} %reshape.20), channel_id=1, source_target_pairs={{0,16},{16,32},{32,48},{48,0},{1,17},{17,33},{33,49},{49,1},{2,18}... | collective-permute-start | bytes 221192 | tf_op jit(solution)/shard_map/ppermute | solution.py:30
  47.3 0.6 constant_dynamic-update-slice_fusion.10
  47.9 0.7 collective-permute-done.3
  48.6 0.6 constant_dynamic-update-slice_fusion.9
  49.2 2.2 collective-permute-done.4
  51.4 0.6 constant_dynamic-update-slice_fusion.8
  52.0 2.0 collective-permute-start.5
  54.0 4.5 %collective-permute-start.9 = (bf16[96,1536]{1,0:T(8,128)(2,1)S(1)}, bf16[96,1536]{1,0:T(8,128)(2,1)S(1)}, u32[]{:S(2)}, u32[]{:S(2)}) collective-permute-start(bf16[96,1536]{1,0:T(8,128)(2,1)S(1)} %get-tuple-element.33), channel_id=1, source_target_pairs={{0,448},{64,0},{128,64},{192,128},{256,192},{320,256},{384,320},{4... | collective-permute-start | bytes 884744 | tf_op jit(solution)/shard_map/ppermute | solution.py:30
  58.5 2.4 %collective-permute-start.16 = (bf16[256,384]{1,0:T(8,128)(2,1)S(1)}, bf16[256,384]{1,0:T(8,128)(2,1)S(1)}, u32[]{:S(2)}, u32[]{:S(2)}) collective-permute-start(bf16[256,384]{1,0:T(8,128)(2,1)S(1)} %copy-done.6), channel_id=1, source_target_pairs={{0,1},{1,0},{2,3},{3,2},{4,5},{5,4},{6,7},{7,6},{8,9},{9,8},{10,11... | collective-permute-start | bytes 589832 | tf_op jit(solution)/shard_map/ppermute | solution.py:202
  61.0 0.8 collective-permute-done.5
  61.8 1.9 collective-permute-start.6
  63.8 4.6 %collective-permute-start.10 = (bf16[96,1536]{1,0:T(8,128)(2,1)S(1)}, bf16[96,1536]{1,0:T(8,128)(2,1)S(1)}, u32[]{:S(2)}, u32[]{:S(2)}) collective-permute-start(bf16[96,1536]{1,0:T(8,128)(2,1)S(1)} %collective-permute-done.9), channel_id=1, source_target_pairs={{0,448},{64,0},{128,64},{192,128},{256,192},{320,256},{384,320},{4... | collective-permute-start | bytes 884744 | tf_op jit(solution)/shard_map/ppermute | solution.py:30
  68.3 0.7 constant_dynamic-update-slice_fusion.7
  69.1 0.7 constant_dynamic-update-slice_fusion.6
  69.8 0.7 collective-permute-done.6
  70.5 0.7 constant_dynamic-update-slice_fusion.5
  71.2 0.7 collective-permute-done.10
  72.0 0.7 constant_dynamic-update-slice_fusion.4.near_ref.own_near
  72.7 5.7 %collective-permute-start.11 = (bf16[480,1536]{1,0:T(8,128)(2,1)}, bf16[480,1536]{1,0:T(8,128)(2,1)}, u32[]{:S(2)}, u32[]{:S(2)}) collective-permute-start(bf16[480,1536]{1,0:T(8,128)(2,1)} %constant_dynamic-update-slice_fusion.4.near_ref.own_near), channel_id=1, source_target_pairs={{0,8},{8,0},{1,9},{9,1},{2,10},{10,2},{3,11},{11,3},{4,12},{12,4},... | collective-permute-start | bytes 4423688 | tf_op jit(solution)/shard_map/ppermute | solution.py:30
  78.5 0.0 collective-permute-done.16
  78.5 0.8 pad_maximum_fusion
  79.3 0.0 all-gather.2.cloned.1.call-update
  79.4 0.0 reduce-scatter.2.cloned.1.call-start
  79.4 2.1 collective-permute-start.7
  81.5 5.2 %collective-permute-start.12 = (bf16[96,1536]{1,0:T(8,128)(2,1)S(1)}, bf16[96,1536]{1,0:T(8,128)(2,1)S(1)}, u32[]{:S(2)}, u32[]{:S(2)}) collective-permute-start(bf16[96,1536]{1,0:T(8,128)(2,1)S(1)} %collective-permute-done.10), channel_id=1, source_target_pairs={{0,448},{64,0},{128,64},{192,128},{256,192},{320,256},{384,320},{4... | collective-permute-start | bytes 884744 | tf_op jit(solution)/shard_map/ppermute | solution.py:30
  86.7 5.4 %collective-permute-done.7 = bf16[96,1536]{1,0:T(8,128)(2,1)S(1)} collective-permute-done((bf16[96,1536]{1,0:T(8,128)(2,1)S(1)}, bf16[96,1536]{1,0:T(8,128)(2,1)S(1)}, u32[]{:S(2)}, u32[]{:S(2)}) %collective-permute-start.7) | collective-permute-done | bytes 294944 | tf_op jit(solution)/shard_map/ppermute | solution.py:30
  92.1 1.9 collective-permute-start.8
  94.0 0.8 constant_dynamic-update-slice_fusion.13
  94.8 0.0 collective-permute-done.12
  94.8 0.8 constant_dynamic-update-slice_fusion.12.own_mid
  95.5 2.5 %collective-permute-start.13 = (bf16[192,1536]{1,0:T(8,128)(2,1)}, bf16[192,1536]{1,0:T(8,128)(2,1)}, u32[]{:S(2)}, u32[]{:S(2)}) collective-permute-start(bf16[192,1536]{1,0:T(8,128)(2,1)} %constant_dynamic-update-slice_fusion.12.own_mid), channel_id=1, source_target_pairs={{0,8},{8,0},{1,9},{9,1},{2,10},{10,2},{3,11},{11,3},{4,12},{12,4},... | collective-permute-start | bytes 1769480 | tf_op jit(solution)/shard_map/ppermute | solution.py:30
  98.0 2.0 gradient_sums.2.own_sum
  100.1 1.0 copy-done.2
  101.1 1.9 gradient_sums.3.other_sum
  103.0 0.3 collective-permute-done.8.own_last
  103.3 3.4 %collective-permute-start.14 = (bf16[96,1536]{1,0:T(8,128)(2,1)}, bf16[96,1536]{1,0:T(8,128)(2,1)}, u32[]{:S(2)}, u32[]{:S(2)}) collective-permute-start(bf16[96,1536]{1,0:T(8,128)(2,1)} %collective-permute-done.8.own_last), channel_id=1, source_target_pairs={{0,8},{8,0},{1,9},{9,1},{2,10},{10,2},{3,11},{11,3},{4,12},{12,4},... | collective-permute-start | bytes 884744 | tf_op jit(solution)/shard_map/ppermute | solution.py:30
  106.6 0.1 pad_add_fusion.at_ref
  106.7 1.4 collective-permute-done.14.other_last
  108.2 1.0 copy-done.3
  109.1 3.0 %gradient_terms.2 = bf16[4,256,384]{2,1,0:T(8,128)(2,1)} custom-call(s32[2]{0:T(128)S(1)} %pad_add_fusion.at_ref, bf16[256,768]{1,0:T(8,128)(2,1)S(1)} %copy-done.3, f32[256,1536]{1,0:T(8,128)S(1)} %gradient_sums.2.own_sum, f32[256,1536]{1,0:T(8,128)S(1)} %gradient_sums.3.other_sum, bf16[192,1536]{1,0:T(8,128)(2,1)} %constant_dynamic-update-slice_fusion.12.own_mid, ...), custom_call_target="tpu_custom_call" | custom-call | flops 75497472 | bytes 4194304 | tf_op jit(solution)/shard_map/gradient_terms/pallas_call | solution.py:247
  112.2 2.4 %collective-permute-start.15 = (bf16[4,256,384]{2,1,0:T(8,128)(2,1)}, bf16[4,256,384]{2,1,0:T(8,128)(2,1)}, u32[]{:S(2)}, u32[]{:S(2)}) collective-permute-start(bf16[4,256,384]{2,1,0:T(8,128)(2,1)} %gradient_terms.2), channel_id=1, source_target_pairs={{0,1},{1,0},{2,3},{3,2},{4,5},{5,4},{6,7},{7,6},{8,9},{9,8},{10,11... | collective-permute-start | bytes 2359304 | tf_op jit(solution)/shard_map/ppermute | solution.py:266
  114.6 0.1 pad_add_fusion.1.at_ref
  114.7 2.1 gradient_terms.3
  116.8 0.9 copy-done.4
  117.7 31.4 %all-gather.2.cloned.1.call-done.o_ref = bf16[8,256,384]{2,1,0:T(8,128)(2,1)} async-done(((bf16[2,256,384]{2,1,0:T(8,128)(2,1)}), bf16[8,256,384]{2,1,0:T(8,128)(2,1)}) %all-gather.2.cloned.1.call-update) | async-done | bytes 1572880 | tf_op jit(solution)/shard_map/all_gather | solution.py:210
  149.1 4.2 %collective-permute-done.15 = bf16[4,256,384]{2,1,0:T(8,128)(2,1)} collective-permute-done((bf16[4,256,384]{2,1,0:T(8,128)(2,1)}, bf16[4,256,384]{2,1,0:T(8,128)(2,1)}, u32[]{:S(2)}, u32[]{:S(2)}) %collective-permute-start.15) | collective-permute-done | bytes 786464 | tf_op jit(solution)/shard_map/ppermute | solution.py:266
  153.2 2.5 %add_convert_fusion = bf16[4,256,384]{2,1,0:T(8,128)(2,1)} fusion(bf16[4,256,384]{2,1,0:T(8,128)(2,1)} %collective-permute-done.15, bf16[4,256,384]{2,1,0:T(8,128)(2,1)} %copy-done.4), kind=kLoop, calls=%fused_computation.3 | loop fusion | flops 1572864 | bytes 2359296 | tf_op jit(solution)/shard_map/convert_element_type | solution.py:268
  155.7 0.0 reduce-scatter.2.cloned.1.call-update
  155.7 0.3 fusion.s_ref
  156.0 1.1 copy-done.5
  157.1 7.1 %output_projection.1 = bf16[256,768]{1,0:T(8,128)(2,1)} custom-call(s32[1]{0:T(128)} %bitcast.core_ref, bf16[8,256,384]{2,1,0:T(8,128)(2,1)S(1)} %copy-done.5, bf16[480,1536]{1,0:T(8,128)(2,1)} %constant_dynamic-update-slice_fusion.4.near_ref.own_near, bf16[192,1536]{1,0:T(8,128)(2,1)} %constant_dynamic-update-slice_fusion.12.own_mid, ...), custom_call_target="tpu_custom_call" | custom-call | flops 1207959552 | bytes 8388608 | tf_op jit(solution)/shard_map/output_projection/pallas_call | solution.py:277
  164.1 58.8 %reduce-scatter.2.cloned.1.call-done = bf16[1,256,384]{2,1,0:T(8,128)(2,1)} async-done(((bf16[4,256,384]{2,1,0:T(8,128)(2,1)}), bf16[1,256,384]{2,1,0:T(8,128)(2,1)}) %reduce-scatter.2.cloned.1.call-update) | async-done | bytes 196624 | tf_op jit(solution)/shard_map/reduce_scatter | solution.py:269
  222.9 3.8 %attention_backward.1 = (bf16[256,384]{1,0:T(8,128)(2,1)}, bf16[256,384]{1,0:T(8,128)(2,1)}, bf16[256,384]{1,0:T(8,128)(2,1)}) custom-call(bf16[256,384]{1,0:T(8,128)(2,1)} %q_ref.3, bf16[256,384]{1,0:T(8,128)(2,1)} %k_ref.3, bf16[256,384]{1,0:T(8,128)(2,1)} %v_ref.3, f32[3,256,256]{2,1,0:T(8,128)} %get-tuple-element.23.p_ref, bf16[256,384]{1,0:T(8,128)(2,1)} %bitcast.16), custom_call_target="tpu_custom_call" | custom-call | flops 201326592 | bytes 2097152 | tf_op jit(solution)/shard_map/attention_backward/pallas_call | solution.py:297
  (24 shorter events, 0.2 us)
Async XLA Ops:
  7.2 20.9 %copy-start = (bf16[256,768]{1,0:T(8,128)(2,1)S(1)}, bf16[256,768]{1,0:T(8,128)(2,1)}, u32[]{:S(2)}) copy-start(bf16[256,768]{1,0:T(8,128)(2,1)} %param.14) | copy-start | bytes 1179652
  7.2 25.3 %copy-start.7 = (bf16[3072,6]{0,1:T(8,128)(2,1)S(1)}, bf16[3072,6]{0,1:T(8,128)(2,1)}, u32[]{:S(2)}) copy-start(bf16[3072,6]{0,1:T(8,128)(2,1)} %param.13) | copy-start | bytes 110596
  7.2 141.9 %all-gather.2.cloned.1.call-start = ((), (), s32[]{:S(2)}) async-start(), calls=%async_computation.1 | async-start | bytes 1966080 | tf_op jit(solution)/shard_map/all_gather | solution.py:210
  7.2 25.2 %collective-permute-start = (bf16[6,3072]{1,0:T(8,128)(2,1)}, bf16[6,3072]{1,0:T(8,128)(2,1)S(1)}, u32[]{:S(2)}, u32[]{:S(2)}) collective-permute-start(bf16[6,3072]{1,0:T(8,128)(2,1)} %bitcast.17), channel_id=1, source_target_pairs={{0,512},{512,0},{1,513},{513,1},{2,514},{514,2},{3,515},{515,3},{4... | collective-permute-start | bytes 110600 | tf_op jit(solution)/shard_map/ppermute | solution.py:30
  28.8 69.3 %copy-start.1 = (bf16[256,768]{1,0:T(8,128)(2,1)}, bf16[256,768]{1,0:T(8,128)(2,1)S(1)}, u32[]{:S(2)}) copy-start(bf16[256,768]{1,0:T(8,128)(2,1)S(1)} %fusion.3.cot_ref) | copy-start | bytes 1179652
  32.5 26.1 %copy-start.6 = (bf16[256,384]{1,0:T(8,128)(2,1)S(1)}, bf16[256,384]{1,0:T(8,128)(2,1)}, u32[]{:S(2)}) copy-start(bf16[256,384]{1,0:T(8,128)(2,1)} %get-tuple-element.16) | copy-start | bytes 589828
  32.6 6.7 %collective-permute-start.1 = (bf16[2,6,1536]{2,1,0:T(8,128)(2,1)S(1)}, bf16[2,6,1536]{2,1,0:T(8,128)(2,1)S(1)}, u32[]{:S(2)}, u32[]{:S(2)}) collective-permute-start(bf16[2,6,1536]{2,1,0:T(8,128)(2,1)S(1)} %constant_dynamic-slice_fusion), channel_id=1, source_target_pairs={{0,8},{8,0},{1,9},{9,1},{2,10},{10,2},{3,11},{11,3},{4,12},{12,4},... | collective-permute-start | bytes 110600 | tf_op jit(solution)/shard_map/ppermute | solution.py:30
  39.4 7.9 %collective-permute-start.2 = (bf16[24,1536]{1,0:T(8,128)(2,1)S(1)}, bf16[24,1536]{1,0:T(8,128)(2,1)S(1)}, u32[]{:S(2)}, u32[]{:S(2)}) collective-permute-start(bf16[24,1536]{1,0:T(8,128)(2,1)S(1)} %reshape.20), channel_id=1, source_target_pairs={{0,48},{16,0},{32,16},{48,32},{1,49},{17,1},{33,17},{49,33},{2,50}... | collective-permute-start | bytes 221192 | tf_op jit(solution)/shard_map/ppermute | solution.py:30
  42.0 6.6 %collective-permute-start.3 = (bf16[24,1536]{1,0:T(8,128)(2,1)S(1)}, bf16[24,1536]{1,0:T(8,128)(2,1)S(1)}, u32[]{:S(2)}, u32[]{:S(2)}) collective-permute-start(bf16[24,1536]{1,0:T(8,128)(2,1)S(1)} %reshape.20), channel_id=1, source_target_pairs={{0,32},{16,48},{32,0},{48,16},{1,33},{17,49},{33,1},{49,17},{2,34}... | collective-permute-start | bytes 221192 | tf_op jit(solution)/shard_map/ppermute | solution.py:30
  43.9 7.5 %collective-permute-start.4 = (bf16[24,1536]{1,0:T(8,128)(2,1)S(1)}, bf16[24,1536]{1,0:T(8,128)(2,1)S(1)}, u32[]{:S(2)}, u32[]{:S(2)}) collective-permute-start(bf16[24,1536]{1,0:T(8,128)(2,1)S(1)} %reshape.20), channel_id=1, source_target_pairs={{0,16},{16,32},{32,48},{48,0},{1,17},{17,33},{33,49},{49,1},{2,18}... | collective-permute-start | bytes 221192 | tf_op jit(solution)/shard_map/ppermute | solution.py:30
  52.0 9.8 %collective-permute-start.5 = (bf16[96,1536]{1,0:T(8,128)(2,1)S(1)}, bf16[96,1536]{1,0:T(8,128)(2,1)S(1)}, u32[]{:S(2)}, u32[]{:S(2)}) collective-permute-start(bf16[96,1536]{1,0:T(8,128)(2,1)S(1)} %get-tuple-element.33), channel_id=1, source_target_pairs={{0,64},{64,128},{128,192},{192,256},{256,320},{320,384},{384,448},... | collective-permute-start | bytes 884744 | tf_op jit(solution)/shard_map/ppermute | solution.py:30
  54.0 9.7 %collective-permute-start.9 = (bf16[96,1536]{1,0:T(8,128)(2,1)S(1)}, bf16[96,1536]{1,0:T(8,128)(2,1)S(1)}, u32[]{:S(2)}, u32[]{:S(2)}) collective-permute-start(bf16[96,1536]{1,0:T(8,128)(2,1)S(1)} %get-tuple-element.33), channel_id=1, source_target_pairs={{0,448},{64,0},{128,64},{192,128},{256,192},{320,256},{384,320},{4... | collective-permute-start | bytes 884744 | tf_op jit(solution)/shard_map/ppermute | solution.py:30
  58.5 20.0 %collective-permute-start.16 = (bf16[256,384]{1,0:T(8,128)(2,1)S(1)}, bf16[256,384]{1,0:T(8,128)(2,1)S(1)}, u32[]{:S(2)}, u32[]{:S(2)}) collective-permute-start(bf16[256,384]{1,0:T(8,128)(2,1)S(1)} %copy-done.6), channel_id=1, source_target_pairs={{0,1},{1,0},{2,3},{3,2},{4,5},{5,4},{6,7},{7,6},{8,9},{9,8},{10,11... | collective-permute-start | bytes 589832 | tf_op jit(solution)/shard_map/ppermute | solution.py:202
  61.8 8.7 %collective-permute-start.6 = (bf16[96,1536]{1,0:T(8,128)(2,1)S(1)}, bf16[96,1536]{1,0:T(8,128)(2,1)S(1)}, u32[]{:S(2)}, u32[]{:S(2)}) collective-permute-start(bf16[96,1536]{1,0:T(8,128)(2,1)S(1)} %collective-permute-done.5), channel_id=1, source_target_pairs={{0,64},{64,128},{128,192},{192,256},{256,320},{320,384},{384,448},... | collective-permute-start | bytes 884744 | tf_op jit(solution)/shard_map/ppermute | solution.py:30
  63.8 8.2 %collective-permute-start.10 = (bf16[96,1536]{1,0:T(8,128)(2,1)S(1)}, bf16[96,1536]{1,0:T(8,128)(2,1)S(1)}, u32[]{:S(2)}, u32[]{:S(2)}) collective-permute-start(bf16[96,1536]{1,0:T(8,128)(2,1)S(1)} %collective-permute-done.9), channel_id=1, source_target_pairs={{0,448},{64,0},{128,64},{192,128},{256,192},{320,256},{384,320},{4... | collective-permute-start | bytes 884744 | tf_op jit(solution)/shard_map/ppermute | solution.py:30
  72.7 27.3 %collective-permute-start.11 = (bf16[480,1536]{1,0:T(8,128)(2,1)}, bf16[480,1536]{1,0:T(8,128)(2,1)}, u32[]{:S(2)}, u32[]{:S(2)}) collective-permute-start(bf16[480,1536]{1,0:T(8,128)(2,1)} %constant_dynamic-update-slice_fusion.4.near_ref.own_near), channel_id=1, source_target_pairs={{0,8},{8,0},{1,9},{9,1},{2,10},{10,2},{3,11},{11,3},{4,12},{12,4},... | collective-permute-start | bytes 4423688 | tf_op jit(solution)/shard_map/ppermute | solution.py:30
  79.4 143.5 %reduce-scatter.2.cloned.1.call-start = ((), (), s32[]{:S(2)}) async-start(), calls=%async_computation.2 | async-start | bytes 983040 | tf_op jit(solution)/shard_map/reduce_scatter | solution.py:269
  79.4 12.7 %collective-permute-start.7 = (bf16[96,1536]{1,0:T(8,128)(2,1)S(1)}, bf16[96,1536]{1,0:T(8,128)(2,1)S(1)}, u32[]{:S(2)}, u32[]{:S(2)}) collective-permute-start(bf16[96,1536]{1,0:T(8,128)(2,1)S(1)} %collective-permute-done.6), channel_id=1, source_target_pairs={{0,64},{64,128},{128,192},{192,256},{256,320},{320,384},{384,448},... | collective-permute-start | bytes 884744 | tf_op jit(solution)/shard_map/ppermute | solution.py:30
  81.5 13.3 %collective-permute-start.12 = (bf16[96,1536]{1,0:T(8,128)(2,1)S(1)}, bf16[96,1536]{1,0:T(8,128)(2,1)S(1)}, u32[]{:S(2)}, u32[]{:S(2)}) collective-permute-start(bf16[96,1536]{1,0:T(8,128)(2,1)S(1)} %collective-permute-done.10), channel_id=1, source_target_pairs={{0,448},{64,0},{128,64},{192,128},{256,192},{320,256},{384,320},{4... | collective-permute-start | bytes 884744 | tf_op jit(solution)/shard_map/ppermute | solution.py:30
  92.1 11.2 %collective-permute-start.8 = (bf16[96,1536]{1,0:T(8,128)(2,1)S(1)}, bf16[96,1536]{1,0:T(8,128)(2,1)}, u32[]{:S(2)}, u32[]{:S(2)}) collective-permute-start(bf16[96,1536]{1,0:T(8,128)(2,1)S(1)} %collective-permute-done.7), channel_id=1, source_target_pairs={{0,64},{64,128},{128,192},{192,256},{256,320},{320,384},{384,448},... | collective-permute-start | bytes 884744 | tf_op jit(solution)/shard_map/ppermute | solution.py:30
  95.5 11.2 %collective-permute-start.13 = (bf16[192,1536]{1,0:T(8,128)(2,1)}, bf16[192,1536]{1,0:T(8,128)(2,1)}, u32[]{:S(2)}, u32[]{:S(2)}) collective-permute-start(bf16[192,1536]{1,0:T(8,128)(2,1)} %constant_dynamic-update-slice_fusion.12.own_mid), channel_id=1, source_target_pairs={{0,8},{8,0},{1,9},{9,1},{2,10},{10,2},{3,11},{11,3},{4,12},{12,4},... | collective-permute-start | bytes 1769480 | tf_op jit(solution)/shard_map/ppermute | solution.py:30
  100.1 1.0 copy-start.2
  103.3 4.9 %collective-permute-start.14 = (bf16[96,1536]{1,0:T(8,128)(2,1)}, bf16[96,1536]{1,0:T(8,128)(2,1)}, u32[]{:S(2)}, u32[]{:S(2)}) collective-permute-start(bf16[96,1536]{1,0:T(8,128)(2,1)} %collective-permute-done.8.own_last), channel_id=1, source_target_pairs={{0,8},{8,0},{1,9},{9,1},{2,10},{10,2},{3,11},{11,3},{4,12},{12,4},... | collective-permute-start | bytes 884744 | tf_op jit(solution)/shard_map/ppermute | solution.py:30
  108.1 1.0 copy-start.3
  112.2 41.0 %collective-permute-start.15 = (bf16[4,256,384]{2,1,0:T(8,128)(2,1)}, bf16[4,256,384]{2,1,0:T(8,128)(2,1)}, u32[]{:S(2)}, u32[]{:S(2)}) collective-permute-start(bf16[4,256,384]{2,1,0:T(8,128)(2,1)} %gradient_terms.2), channel_id=1, source_target_pairs={{0,1},{1,0},{2,3},{3,2},{4,5},{5,4},{6,7},{7,6},{8,9},{9,8},{10,11... | collective-permute-start | bytes 2359304 | tf_op jit(solution)/shard_map/ppermute | solution.py:266
  116.8 0.9 copy-start.4
  155.7 1.4 copy-start.5
Sparse Core Ops, SparseCore 0:
  79.5 69.5 all-gather.1
  155.8 67.0 reduce-scatter.1

commit v6 on v4

--- a/solution.py
+++ b/solution.py
@@ -70,10 +70,27 @@
     dk_ref[...] = (dot_tn(score_grad, q_ref[...]) * scale).astype(BF16)
 
 
-def terms_kernel(slot_ref, cot_ref, near_ref, far_ref, *refs):
-    near = near_ref.shape[0]
-    total = dot(cot_ref[:, :near], near_ref[...]) + dot(cot_ref[:, near:], far_ref[...])
-    refs[-1][0] = total.astype(BF16)
+def sums_kernel(cot_ref, near_ref, out_ref):
+    out_ref[...] = dot(cot_ref[:, : near_ref.shape[0]], near_ref[...])
+
+
+def terms_kernel(
+    slots, core_ref, cot_ref, own_sum, other_sum, own_far, other_far, out_ref
+):
+    width = out_ref.shape[2]
+    near = cot_ref.shape[1] - own_far.shape[0]
+    for core in range(2):
+
+        @pl.when(core_ref[0] == core)
+        def _():
+            for half, sum_ref, far_ref in (
+                (core, own_sum, own_far),
+                (1 - core, other_sum, other_far),
+            ):
+                for j, slot in enumerate(slots[half]):
+                    cols = slice(j * width, (j + 1) * width)
+                    term = sum_ref[:, cols] + dot(cot_ref[:, near:], far_ref[:, cols])
+                    out_ref[slot] = term.astype(BF16)
 
 
 def output_kernel(slots, core_ref, o_ref, own_near, own_far, other_near, other_far, s_ref, out_ref):
@@ -176,38 +193,44 @@
 
     across, head_out, cot_rows = lax.optimization_barrier((across, head_out, cot_rows))
     blocks, heads_all = ring_gather(first_stage(w_out.T, across), "y", heads_all, 4)
+    vmem = pl.BlockSpec(memory_space=pltpu.VMEM)
+    smem = pl.BlockSpec(memory_space=pltpu.SMEM)
+
+    def sums(near):
+        return pl.pallas_call(
+            sums_kernel,
+            out_shape=jax.ShapeDtypeStruct((row_count, near.shape[1]), F32),
+            in_specs=[vmem] * 2,
+            out_specs=vmem,
+            compiler_params=PARAMS,
+            cost_estimate=cost(row_count * features * group_width * n, 4 << 20),
+            name="gradient_sums",
+        )(cot_rows, near)
+
     early = 2 * ((ny + 2) // 4) + 1
     own_near = jnp.concatenate(blocks[:early], 0)
     other_near = shift(own_near, "core", 1)
+    own_sum = sums(own_near)
+    other_sum = sums(other_near)
     own_far = jnp.concatenate(blocks[early:], 0)
     other_far = shift(own_far, "core", 1)
 
-    def terms(half, near, far, *into):
-        places = jnp.where(half == 0, jnp.asarray(slots[0]), jnp.asarray(slots[1]))
-        return pl.pallas_call(
-            terms_kernel,
-            out_shape=jax.ShapeDtypeStruct((n, row_count, group_width), BF16),
-            grid_spec=pltpu.PrefetchScalarGridSpec(
-                num_scalar_prefetch=1,
-                grid=(n // 2,),
-                in_specs=[
-                    pl.BlockSpec((row_count, features), lambda j, place: (0, 0)),
-                    pl.BlockSpec((near.shape[0], group_width), lambda j, place: (0, j)),
-                    pl.BlockSpec((far.shape[0], group_width), lambda j, place: (0, j)),
-                ]
-                + [pl.BlockSpec(memory_space=pl.ANY)] * len(into),
-                out_specs=pl.BlockSpec(
-                    (1, row_count, group_width), lambda j, place: (place[j], 0, 0)
-                ),
-            ),
-            input_output_aliases={4: 0} if into else {},
-            compiler_params=PARAMS,
-            cost_estimate=cost(row_count * features * group_width * n, 4 << 20),
-            name="gradient_terms",
-        )(places.astype(jnp.int32), cot_rows, near, far, *into)
-
-    terms_all = terms(core, own_near, own_far)
-    terms_all = terms(1 - core, other_near, other_far, terms_all)
+    terms_all = pl.pallas_call(
+        functools.partial(terms_kernel, slots),
+        out_shape=jax.ShapeDtypeStruct((n, row_count, group_width), BF16),
+        in_specs=[smem] + [vmem] * 5,
+        out_specs=vmem,
+        compiler_params=PARAMS,
+        cost_estimate=cost(2 * row_count * features * group_width * n, 8 << 20),
+        name="gradient_terms",
+    )(
+        jnp.reshape(core, (1,)).astype(jnp.int32),
+        cot_rows,
+        own_sum,
+        other_sum,
+        own_far,
+        other_far,
+    )
     grad_out = lax.psum_scatter(
         terms_all, "zl", scatter_dimension=0, tiled=False, axis_index_groups=[line]
     )

time: 181 us -> 175 us (0.967)
  the two profiles are of different devices: /device:TPU:1 before, /device:TPU:10 now
where the time goes in v6:
time: 175 us; the launch traced here: 174 us
  waiting for transfers between devices  78.1 us (45%)
  starting transfers between devices  57.3 us (33%)
  Pallas kernels  14.5 us (8%)
  between operations  14.4 us (8%)
  local copies, waits for them, and re-layouts  7.58 us (4%)
    ppermute x14, starting transfers between devices, shift(): return lax.ppermute(block, axis, [(i, (i + by) % n) for i in range(n)])  57.2 us
    reduce_scatter x1, waiting for transfers between devices, on_device(): lax.psum_scatter(terms_all, 'zl', scatter_dimension=0, tiled=False, axis_...  48.6 us
    ppermute x14, waiting for transfers between devices, shift(): return lax.ppermute(block, axis, [(i, (i + by) % n) for i in range(n)])  20.8 us
    all_gather x1, waiting for transfers between devices, on_device(): heads_all = lax.all_gather(head_out, 'zl', axis=0, axis_index_groups=[line])  8.67 us
    unnamed x25, local copies, waits for them, and re-layouts  6.49 us
    pallas_call x1, Pallas kernels, on_device(): pl.pallas_call(functools.partial(backward_kernel, scale), out_shape=(toke...  3.77 us
    pallas_call x1, Pallas kernels, on_device(): pl.pallas_call(functools.partial(output_kernel, slots), out_shape=jax.Sha...  3.74 us
    pallas_call x1, Pallas kernels, on_device(): pl.pallas_call(functools.partial(forward_kernel, scale), out_shape=(token...  3.55 us
  transfers between devices with their start and end apart: 16, of which 10 were waited for; matrix products, arithmetic and copies ran while one was open for 3% of the time, Pallas kernels for 5%

profile of v6, /device:TPU:10, one launch (start us, length us, event | category | flops | bytes accessed | tf_op | source)
XLA Modules:
  0.0 174.4 jit_solution(5893455199744124747)
XLA Ops:
  7.2 0.0 copy-start
  7.2 0.0 copy-start.7
  7.2 0.0 all-gather.3.cloned.1.call-start
  7.2 19.5 %collective-permute-start = (bf16[6,3072]{1,0:T(8,128)(2,1)}, bf16[6,3072]{1,0:T(8,128)(2,1)S(1)}, u32[]{:S(2)}, u32[]{:S(2)}) collective-permute-start(bf16[6,3072]{1,0:T(8,128)(2,1)} %bitcast.13), channel_id=1, source_target_pairs={{0,512},{512,0},{1,513},{513,1},{2,514},{514,2},{3,515},{515,3},{4... | collective-permute-start | bytes 110600 | tf_op jit(solution)/shard_map/ppermute | solution.py:30
  26.7 0.8 fusion.12
  27.5 0.0 copy-done
  27.5 1.4 fusion.3.cot_ref
  28.9 3.5 %attention_forward.1 = (bf16[256,384]{1,0:T(8,128)(2,1)}, f32[3,256,256]{2,1,0:T(8,128)}) custom-call(bf16[256,384]{1,0:T(8,128)(2,1)} %q_ref.3, bf16[256,384]{1,0:T(8,128)(2,1)} %k_ref.3, bf16[256,384]{1,0:T(8,128)(2,1)} %v_ref.3), custom_call_target="tpu_custom_call" | custom-call | flops 100663296 | bytes 2097152 | tf_op jit(solution)/shard_map/attention_forward/pallas_call | solution.py:177
  32.5 0.0 collective-permute-done
  32.5 0.0 copy-done.7
  32.6 1.9 %collective-permute-start.1 = (bf16[2,6,1536]{2,1,0:T(8,128)(2,1)S(1)}, bf16[2,6,1536]{2,1,0:T(8,128)(2,1)S(1)}, u32[]{:S(2)}, u32[]{:S(2)}) collective-permute-start(bf16[2,6,1536]{2,1,0:T(8,128)(2,1)S(1)} %constant_dynamic-slice_fusion), channel_id=1, source_target_pairs={{0,8},{8,0},{1,9},{9,1},{2,10},{10,2},{3,11},{11,3},{4,12},{12,4},... | collective-permute-start | bytes 110600 | tf_op jit(solution)/shard_map/ppermute | solution.py:30
  34.5 0.0 all-gather.3.cloned.1.call-update
  34.6 0.0 reduce-scatter.2.cloned.1.call-start
  34.6 1.1 collective-permute-done.1
  35.8 3.4 %collective-permute-start.4 = (bf16[24,1536]{1,0:T(8,128)(2,1)S(1)}, bf16[24,1536]{1,0:T(8,128)(2,1)S(1)}, u32[]{:S(2)}, u32[]{:S(2)}) collective-permute-start(bf16[24,1536]{1,0:T(8,128)(2,1)S(1)} %reshape.21), channel_id=1, source_target_pairs={{0,16},{16,32},{32,48},{48,0},{1,17},{17,33},{33,49},{49,1},{2,18}... | collective-permute-start | bytes 221192 | tf_op jit(solution)/shard_map/ppermute | solution.py:30
  39.3 3.0 %collective-permute-start.3 = (bf16[24,1536]{1,0:T(8,128)(2,1)S(1)}, bf16[24,1536]{1,0:T(8,128)(2,1)S(1)}, u32[]{:S(2)}, u32[]{:S(2)}) collective-permute-start(bf16[24,1536]{1,0:T(8,128)(2,1)S(1)} %reshape.21), channel_id=1, source_target_pairs={{0,32},{16,48},{32,0},{48,16},{1,33},{17,49},{33,1},{49,17},{2,34}... | collective-permute-start | bytes 221192 | tf_op jit(solution)/shard_map/ppermute | solution.py:30
  42.3 4.1 %collective-permute-start.2 = (bf16[24,1536]{1,0:T(8,128)(2,1)S(1)}, bf16[24,1536]{1,0:T(8,128)(2,1)S(1)}, u32[]{:S(2)}, u32[]{:S(2)}) collective-permute-start(bf16[24,1536]{1,0:T(8,128)(2,1)S(1)} %reshape.21), channel_id=1, source_target_pairs={{0,48},{16,0},{32,16},{48,32},{1,49},{17,1},{33,17},{49,33},{2,50}... | collective-permute-start | bytes 221192 | tf_op jit(solution)/shard_map/ppermute | solution.py:30
  46.4 2.2 %collective-permute-done.2 = bf16[24,1536]{1,0:T(8,128)(2,1)S(1)} collective-permute-done((bf16[24,1536]{1,0:T(8,128)(2,1)S(1)}, bf16[24,1536]{1,0:T(8,128)(2,1)S(1)}, u32[]{:S(2)}, u32[]{:S(2)}) %collective-permute-start.2) | collective-permute-done | bytes 73760 | tf_op jit(solution)/shard_map/ppermute | solution.py:30
  48.6 0.0 collective-permute-done.3
  48.6 0.0 collective-permute-done.4
  48.7 4.7 %collective-permute-start.8 = (bf16[96,1536]{1,0:T(8,128)(2,1)S(1)}, bf16[96,1536]{1,0:T(8,128)(2,1)S(1)}, u32[]{:S(2)}, u32[]{:S(2)}) collective-permute-start(bf16[96,1536]{1,0:T(8,128)(2,1)S(1)} %get-tuple-element.25), channel_id=1, source_target_pairs={{0,448},{64,0},{128,64},{192,128},{256,192},{320,256},{384,320},{4... | collective-permute-start | bytes 884744 | tf_op jit(solution)/shard_map/ppermute | solution.py:30
  53.4 1.9 %collective-permute-start.5 = (bf16[96,1536]{1,0:T(8,128)(2,1)S(1)}, bf16[96,1536]{1,0:T(8,128)(2,1)S(1)}, u32[]{:S(2)}, u32[]{:S(2)}) collective-permute-start(bf16[96,1536]{1,0:T(8,128)(2,1)S(1)} %get-tuple-element.25), channel_id=1, source_target_pairs={{0,64},{64,128},{128,192},{192,256},{256,320},{320,384},{384,448},... | collective-permute-start | bytes 884744 | tf_op jit(solution)/shard_map/ppermute | solution.py:30
  55.3 3.5 %collective-permute-done.8 = bf16[96,1536]{1,0:T(8,128)(2,1)S(1)} collective-permute-done((bf16[96,1536]{1,0:T(8,128)(2,1)S(1)}, bf16[96,1536]{1,0:T(8,128)(2,1)S(1)}, u32[]{:S(2)}, u32[]{:S(2)}) %collective-permute-start.8) | collective-permute-done | bytes 294944 | tf_op jit(solution)/shard_map/ppermute | solution.py:30
  58.8 3.8 %collective-permute-start.9 = (bf16[96,1536]{1,0:T(8,128)(2,1)S(1)}, bf16[96,1536]{1,0:T(8,128)(2,1)}, u32[]{:S(2)}, u32[]{:S(2)}) collective-permute-start(bf16[96,1536]{1,0:T(8,128)(2,1)S(1)} %collective-permute-done.8), channel_id=1, source_target_pairs={{0,448},{64,0},{128,64},{192,128},{256,192},{320,256},{384,320},{4... | collective-permute-start | bytes 884744 | tf_op jit(solution)/shard_map/ppermute | solution.py:30
  62.6 0.0 collective-permute-done.5
  62.6 2.0 %collective-permute-start.6 = (bf16[96,1536]{1,0:T(8,128)(2,1)S(1)}, bf16[96,1536]{1,0:T(8,128)(2,1)S(1)}, u32[]{:S(2)}, u32[]{:S(2)}) collective-permute-start(bf16[96,1536]{1,0:T(8,128)(2,1)S(1)} %collective-permute-done.5), channel_id=1, source_target_pairs={{0,64},{64,128},{128,192},{192,256},{256,320},{320,384},{384,448},... | collective-permute-start | bytes 884744 | tf_op jit(solution)/shard_map/ppermute | solution.py:30
  64.7 3.5 %collective-permute-done.9 = bf16[96,1536]{1,0:T(8,128)(2,1)} collective-permute-done((bf16[96,1536]{1,0:T(8,128)(2,1)S(1)}, bf16[96,1536]{1,0:T(8,128)(2,1)}, u32[]{:S(2)}, u32[]{:S(2)}) %collective-permute-start.9) | collective-permute-done | bytes 294944 | tf_op jit(solution)/shard_map/ppermute | solution.py:30
  68.2 3.8 %collective-permute-start.10 = (bf16[96,1536]{1,0:T(8,128)(2,1)}, bf16[96,1536]{1,0:T(8,128)(2,1)}, u32[]{:S(2)}, u32[]{:S(2)}) collective-permute-start(bf16[96,1536]{1,0:T(8,128)(2,1)} %collective-permute-done.9), channel_id=1, source_target_pairs={{0,448},{64,0},{128,64},{192,128},{256,192},{320,256},{384,320},{4... | collective-permute-start | bytes 884744 | tf_op jit(solution)/shard_map/ppermute | solution.py:30
  72.0 0.5 collective-permute-done.6
  72.5 1.9 %collective-permute-start.7 = (bf16[96,1536]{1,0:T(8,128)(2,1)S(1)}, bf16[96,1536]{1,0:T(8,128)(2,1)}, u32[]{:S(2)}, u32[]{:S(2)}) collective-permute-start(bf16[96,1536]{1,0:T(8,128)(2,1)S(1)} %collective-permute-done.6), channel_id=1, source_target_pairs={{0,64},{64,128},{128,192},{192,256},{256,320},{320,384},{384,448},... | collective-permute-start | bytes 884744 | tf_op jit(solution)/shard_map/ppermute | solution.py:30
  74.4 1.0 constant_dynamic-update-slice_fusion.4.own_near.near_ref
  75.4 1.9 %collective-permute-start.12 = (bf16[480,1536]{1,0:T(8,128)(2,1)S(1)}, bf16[480,1536]{1,0:T(8,128)(2,1)S(1)}, u32[]{:S(2)}, u32[]{:S(2)}) collective-permute-start(bf16[480,1536]{1,0:T(8,128)(2,1)S(1)} %constant_dynamic-update-slice_fusion.4.own_near.near_ref), channel_id=1, source_target_pairs={{0,8},{8,0},{1,9},{9,1},{2,10},{10,2},{3,11},{11,3},{4,12},{12,4},... | collective-permute-start | bytes 4423688 | tf_op jit(solution)/shard_map/ppermute | solution.py:30
  77.3 5.2 %collective-permute-done.7 = bf16[96,1536]{1,0:T(8,128)(2,1)} collective-permute-done((bf16[96,1536]{1,0:T(8,128)(2,1)S(1)}, bf16[96,1536]{1,0:T(8,128)(2,1)}, u32[]{:S(2)}, u32[]{:S(2)}) %collective-permute-start.7) | collective-permute-done | bytes 294944 | tf_op jit(solution)/shard_map/ppermute | solution.py:30
  82.5 8.7 %all-gather.3.cloned.1.call-done = bf16[2048,384]{1,0:T(8,128)(2,1)} async-done(((bf16[256,384]{1,0:T(8,128)(2,1)}), bf16[2048,384]{1,0:T(8,128)(2,1)}) %all-gather.3.cloned.1.call-update) | async-done | bytes 1572880 | tf_op jit(solution)/shard_map/all_gather | solution.py:190
  91.2 0.0 copy-start.5
  91.2 3.4 %collective-permute-start.11 = (bf16[96,1536]{1,0:T(8,128)(2,1)}, bf16[96,1536]{1,0:T(8,128)(2,1)S(1)}, u32[]{:S(2)}, u32[]{:S(2)}) collective-permute-start(bf16[96,1536]{1,0:T(8,128)(2,1)} %collective-permute-done.7), channel_id=1, source_target_pairs={{0,64},{64,128},{128,192},{192,256},{256,320},{320,384},{384,448},... | collective-permute-start | bytes 884744 | tf_op jit(solution)/shard_map/ppermute | solution.py:30
  94.5 1.0 constant_dynamic-update-slice_fusion.14
  95.5 0.0 collective-permute-done.10
  95.6 1.0 constant_dynamic-update-slice_fusion.13
  96.5 3.6 %collective-permute-done.11 = bf16[96,1536]{1,0:T(8,128)(2,1)S(1)} collective-permute-done((bf16[96,1536]{1,0:T(8,128)(2,1)}, bf16[96,1536]{1,0:T(8,128)(2,1)S(1)}, u32[]{:S(2)}, u32[]{:S(2)}) %collective-permute-start.11) | collective-permute-done | bytes 294944 | tf_op jit(solution)/shard_map/ppermute | solution.py:30
  100.2 0.0 copy-start.1
  100.2 1.9 %collective-permute-start.13 = (bf16[288,1536]{1,0:T(8,128)(2,1)S(1)}, bf16[288,1536]{1,0:T(8,128)(2,1)S(1)}, u32[]{:S(2)}, u32[]{:S(2)}) collective-permute-start(bf16[288,1536]{1,0:T(8,128)(2,1)S(1)} %constant_dynamic-update-slice_fusion.12.own_far), channel_id=1, source_target_pairs={{0,8},{8,0},{1,9},{9,1},{2,10},{10,2},{3,11},{11,3},{4,12},{12,4},... | collective-permute-start | bytes 2654216 | tf_op jit(solution)/shard_map/ppermute | solution.py:30
  102.1 0.0 copy-done.5
  102.1 0.6 gradient_sums.2.own_sum
  102.7 0.0 collective-permute-done.12.other_near.near_ref
  102.7 0.6 gradient_sums.3.other_sum
  103.2 1.2 collective-permute-done.13.other_far
  104.5 0.0 copy-done.1
  104.5 2.3 %gradient_terms.1 = bf16[8,256,384]{2,1,0:T(8,128)(2,1)} custom-call(s32[1]{0:T(128)} %bitcast.core_ref, bf16[256,768]{1,0:T(8,128)(2,1)S(1)} %copy-done.5, f32[256,1536]{1,0:T(8,128)S(1)} %gradient_sums.2.own_sum, f32[256,1536]{1,0:T(8,128)S(1)} %gradient_sums.3.other_sum, bf16[288,1536]{1,0:T(8,128)(2,1)S(1)} %constant_dynamic-update-slice_fusion.12.own_far, ...), custom_call_target="tpu_custom_call" | custom-call | flops 1207959552 | bytes 8388608 | tf_op jit(solution)/shard_map/gradient_terms/pallas_call | solution.py:218
  106.8 0.0 copy-start.3
  106.8 0.9 copy-done.3
  107.7 0.0 reduce-scatter.2.cloned.1.call-update
  107.8 0.0 copy-start.2
  107.8 0.3 fusion.s_ref
  108.0 0.9 copy-done.2
  108.9 0.0 copy-start.4
  108.9 1.2 copy-done.4
  110.1 0.0 copy-start.6
  110.1 1.4 copy-done.6
  111.5 3.7 %output_projection.1 = bf16[256,768]{1,0:T(8,128)(2,1)} custom-call(s32[1]{0:T(128)} %bitcast.core_ref, bf16[8,256,384]{2,1,0:T(8,128)(2,1)S(1)} %bitcast.11, bf16[480,1536]{1,0:T(8,128)(2,1)S(1)} %constant_dynamic-update-slice_fusion.4.own_near.near_ref, bf16[288,1536]{1,0:T(8,128)(2,1)S(1)} %copy-done.2, ...), custom_call_target="tpu_custom_call" | custom-call | flops 1207959552 | bytes 8388608 | tf_op jit(solution)/shard_map/output_projection/pallas_call | solution.py:239
  115.2 48.6 %reduce-scatter.2.cloned.1.call-done = bf16[1,256,384]{2,1,0:T(8,128)(2,1)} async-done(((bf16[8,256,384]{2,1,0:T(8,128)(2,1)}), bf16[1,256,384]{2,1,0:T(8,128)(2,1)}) %reduce-scatter.2.cloned.1.call-update) | async-done | bytes 196624 | tf_op jit(solution)/shard_map/reduce_scatter | solution.py:234
  163.8 3.8 %attention_backward.1 = (bf16[256,384]{1,0:T(8,128)(2,1)}, bf16[256,384]{1,0:T(8,128)(2,1)}, bf16[256,384]{1,0:T(8,128)(2,1)}) custom-call(bf16[256,384]{1,0:T(8,128)(2,1)} %q_ref.3, bf16[256,384]{1,0:T(8,128)(2,1)} %k_ref.3, bf16[256,384]{1,0:T(8,128)(2,1)} %v_ref.3, f32[3,256,256]{2,1,0:T(8,128)} %get-tuple-element.17.p_ref, bf16[256,384]{1,0:T(8,128)(2,1)} %bitcast.12), custom_call_target="tpu_custom_call" | custom-call | flops 201326592 | bytes 2097152 | tf_op jit(solution)/shard_map/attention_backward/pallas_call | solution.py:257
  (15 shorter events, 0.3 us)
Async XLA Ops:
  7.2 20.4 %copy-start = (bf16[256,768]{1,0:T(8,128)(2,1)S(1)}, bf16[256,768]{1,0:T(8,128)(2,1)}, u32[]{:S(2)}) copy-start(bf16[256,768]{1,0:T(8,128)(2,1)} %param.14) | copy-start | bytes 1179652
  7.2 25.3 %copy-start.7 = (bf16[3072,6]{0,1:T(8,128)(2,1)S(1)}, bf16[3072,6]{0,1:T(8,128)(2,1)}, u32[]{:S(2)}) copy-start(bf16[3072,6]{0,1:T(8,128)(2,1)} %param.13) | copy-start | bytes 110596
  7.2 84.0 %all-gather.3.cloned.1.call-start = ((), (), s32[]{:S(2)}) async-start(), calls=%async_computation.2 | async-start | bytes 1769472 | tf_op jit(solution)/shard_map/all_gather | solution.py:190
  7.2 25.3 %collective-permute-start = (bf16[6,3072]{1,0:T(8,128)(2,1)}, bf16[6,3072]{1,0:T(8,128)(2,1)S(1)}, u32[]{:S(2)}, u32[]{:S(2)}) collective-permute-start(bf16[6,3072]{1,0:T(8,128)(2,1)} %bitcast.13), channel_id=1, source_target_pairs={{0,512},{512,0},{1,513},{513,1},{2,514},{514,2},{3,515},{515,3},{4... | collective-permute-start | bytes 110600 | tf_op jit(solution)/shard_map/ppermute | solution.py:30
  32.6 3.1 %collective-permute-start.1 = (bf16[2,6,1536]{2,1,0:T(8,128)(2,1)S(1)}, bf16[2,6,1536]{2,1,0:T(8,128)(2,1)S(1)}, u32[]{:S(2)}, u32[]{:S(2)}) collective-permute-start(bf16[2,6,1536]{2,1,0:T(8,128)(2,1)S(1)} %constant_dynamic-slice_fusion), channel_id=1, source_target_pairs={{0,8},{8,0},{1,9},{9,1},{2,10},{10,2},{3,11},{11,3},{4,12},{12,4},... | collective-permute-start | bytes 110600 | tf_op jit(solution)/shard_map/ppermute | solution.py:30
  34.6 129.2 %reduce-scatter.2.cloned.1.call-start = ((), (), s32[]{:S(2)}) async-start(), calls=%async_computation.1 | async-start | bytes 1769472 | tf_op jit(solution)/shard_map/reduce_scatter | solution.py:234
  35.8 12.8 %collective-permute-start.4 = (bf16[24,1536]{1,0:T(8,128)(2,1)S(1)}, bf16[24,1536]{1,0:T(8,128)(2,1)S(1)}, u32[]{:S(2)}, u32[]{:S(2)}) collective-permute-start(bf16[24,1536]{1,0:T(8,128)(2,1)S(1)} %reshape.21), channel_id=1, source_target_pairs={{0,16},{16,32},{32,48},{48,0},{1,17},{17,33},{33,49},{49,1},{2,18}... | collective-permute-start | bytes 221192 | tf_op jit(solution)/shard_map/ppermute | solution.py:30
  39.3 9.3 %collective-permute-start.3 = (bf16[24,1536]{1,0:T(8,128)(2,1)S(1)}, bf16[24,1536]{1,0:T(8,128)(2,1)S(1)}, u32[]{:S(2)}, u32[]{:S(2)}) collective-permute-start(bf16[24,1536]{1,0:T(8,128)(2,1)S(1)} %reshape.21), channel_id=1, source_target_pairs={{0,32},{16,48},{32,0},{48,16},{1,33},{17,49},{33,1},{49,17},{2,34}... | collective-permute-start | bytes 221192 | tf_op jit(solution)/shard_map/ppermute | solution.py:30
  42.3 6.3 %collective-permute-start.2 = (bf16[24,1536]{1,0:T(8,128)(2,1)S(1)}, bf16[24,1536]{1,0:T(8,128)(2,1)S(1)}, u32[]{:S(2)}, u32[]{:S(2)}) collective-permute-start(bf16[24,1536]{1,0:T(8,128)(2,1)S(1)} %reshape.21), channel_id=1, source_target_pairs={{0,48},{16,0},{32,16},{48,32},{1,49},{17,1},{33,17},{49,33},{2,50}... | collective-permute-start | bytes 221192 | tf_op jit(solution)/shard_map/ppermute | solution.py:30
  48.7 10.1 %collective-permute-start.8 = (bf16[96,1536]{1,0:T(8,128)(2,1)S(1)}, bf16[96,1536]{1,0:T(8,128)(2,1)S(1)}, u32[]{:S(2)}, u32[]{:S(2)}) collective-permute-start(bf16[96,1536]{1,0:T(8,128)(2,1)S(1)} %get-tuple-element.25), channel_id=1, source_target_pairs={{0,448},{64,0},{128,64},{192,128},{256,192},{320,256},{384,320},{4... | collective-permute-start | bytes 884744 | tf_op jit(solution)/shard_map/ppermute | solution.py:30
  53.4 9.2 %collective-permute-start.5 = (bf16[96,1536]{1,0:T(8,128)(2,1)S(1)}, bf16[96,1536]{1,0:T(8,128)(2,1)S(1)}, u32[]{:S(2)}, u32[]{:S(2)}) collective-permute-start(bf16[96,1536]{1,0:T(8,128)(2,1)S(1)} %get-tuple-element.25), channel_id=1, source_target_pairs={{0,64},{64,128},{128,192},{192,256},{256,320},{320,384},{384,448},... | collective-permute-start | bytes 884744 | tf_op jit(solution)/shard_map/ppermute | solution.py:30
  58.8 9.4 %collective-permute-start.9 = (bf16[96,1536]{1,0:T(8,128)(2,1)S(1)}, bf16[96,1536]{1,0:T(8,128)(2,1)}, u32[]{:S(2)}, u32[]{:S(2)}) collective-permute-start(bf16[96,1536]{1,0:T(8,128)(2,1)S(1)} %collective-permute-done.8), channel_id=1, source_target_pairs={{0,448},{64,0},{128,64},{192,128},{256,192},{320,256},{384,320},{4... | collective-permute-start | bytes 884744 | tf_op jit(solution)/shard_map/ppermute | solution.py:30
  62.6 9.8 %collective-permute-start.6 = (bf16[96,1536]{1,0:T(8,128)(2,1)S(1)}, bf16[96,1536]{1,0:T(8,128)(2,1)S(1)}, u32[]{:S(2)}, u32[]{:S(2)}) collective-permute-start(bf16[96,1536]{1,0:T(8,128)(2,1)S(1)} %collective-permute-done.5), channel_id=1, source_target_pairs={{0,64},{64,128},{128,192},{192,256},{256,320},{320,384},{384,448},... | collective-permute-start | bytes 884744 | tf_op jit(solution)/shard_map/ppermute | solution.py:30
  68.2 27.3 %collective-permute-start.10 = (bf16[96,1536]{1,0:T(8,128)(2,1)}, bf16[96,1536]{1,0:T(8,128)(2,1)}, u32[]{:S(2)}, u32[]{:S(2)}) collective-permute-start(bf16[96,1536]{1,0:T(8,128)(2,1)} %collective-permute-done.9), channel_id=1, source_target_pairs={{0,448},{64,0},{128,64},{192,128},{256,192},{320,256},{384,320},{4... | collective-permute-start | bytes 884744 | tf_op jit(solution)/shard_map/ppermute | solution.py:30
  72.5 10.0 %collective-permute-start.7 = (bf16[96,1536]{1,0:T(8,128)(2,1)S(1)}, bf16[96,1536]{1,0:T(8,128)(2,1)}, u32[]{:S(2)}, u32[]{:S(2)}) collective-permute-start(bf16[96,1536]{1,0:T(8,128)(2,1)S(1)} %collective-permute-done.6), channel_id=1, source_target_pairs={{0,64},{64,128},{128,192},{192,256},{256,320},{320,384},{384,448},... | collective-permute-start | bytes 884744 | tf_op jit(solution)/shard_map/ppermute | solution.py:30
  75.4 27.3 %collective-permute-start.12 = (bf16[480,1536]{1,0:T(8,128)(2,1)S(1)}, bf16[480,1536]{1,0:T(8,128)(2,1)S(1)}, u32[]{:S(2)}, u32[]{:S(2)}) collective-permute-start(bf16[480,1536]{1,0:T(8,128)(2,1)S(1)} %constant_dynamic-update-slice_fusion.4.own_near.near_ref), channel_id=1, source_target_pairs={{0,8},{8,0},{1,9},{9,1},{2,10},{10,2},{3,11},{11,3},{4,12},{12,4},... | collective-permute-start | bytes 4423688 | tf_op jit(solution)/shard_map/ppermute | solution.py:30
  91.2 10.9 %copy-start.5 = (bf16[256,768]{1,0:T(8,128)(2,1)S(1)}, bf16[256,768]{1,0:T(8,128)(2,1)}, u32[]{:S(2)}) copy-start(bf16[256,768]{1,0:T(8,128)(2,1)} %fusion.3.cot_ref) | copy-start | bytes 1179652
  91.2 8.9 %collective-permute-start.11 = (bf16[96,1536]{1,0:T(8,128)(2,1)}, bf16[96,1536]{1,0:T(8,128)(2,1)S(1)}, u32[]{:S(2)}, u32[]{:S(2)}) collective-permute-start(bf16[96,1536]{1,0:T(8,128)(2,1)} %collective-permute-done.7), channel_id=1, source_target_pairs={{0,64},{64,128},{128,192},{192,256},{256,320},{320,384},{384,448},... | collective-permute-start | bytes 884744 | tf_op jit(solution)/shard_map/ppermute | solution.py:30
  100.2 4.3 %copy-start.1 = (bf16[288,1536]{1,0:T(8,128)(2,1)}, bf16[288,1536]{1,0:T(8,128)(2,1)S(1)}, u32[]{:S(2)}) copy-start(bf16[288,1536]{1,0:T(8,128)(2,1)S(1)} %constant_dynamic-update-slice_fusion.12.own_far) | copy-start | bytes 2654212
  100.2 4.3 %collective-permute-start.13 = (bf16[288,1536]{1,0:T(8,128)(2,1)S(1)}, bf16[288,1536]{1,0:T(8,128)(2,1)S(1)}, u32[]{:S(2)}, u32[]{:S(2)}) collective-permute-start(bf16[288,1536]{1,0:T(8,128)(2,1)S(1)} %constant_dynamic-update-slice_fusion.12.own_far), channel_id=1, source_target_pairs={{0,8},{8,0},{1,9},{9,1},{2,10},{10,2},{3,11},{11,3},{4,12},{12,4},... | collective-permute-start | bytes 2654216 | tf_op jit(solution)/shard_map/ppermute | solution.py:30
  106.8 0.9 copy-start.3
  107.8 1.2 copy-start.2
  108.9 1.2 copy-start.4
  110.1 1.4 copy-start.6
Sparse Core Ops, SparseCore 0:
  34.7 56.4 all-gather.2
  107.9 55.8 reduce-scatter.1

commit v7 on v6

--- a/solution.py
+++ b/solution.py
@@ -60,14 +60,16 @@
 
 
 def backward_kernel(scale, q_ref, k_ref, v_ref, p_ref, g_ref, dq_ref, dk_ref, dv_ref):
-    soft = p_ref[0]
-    grad = g_ref[...]
-    soft_grad = dot_nt(grad, v_ref[...])
-    inner = jnp.sum(soft_grad * soft, axis=1, keepdims=True)
-    score_grad = (soft * (soft_grad - inner)).astype(BF16)
-    dv_ref[...] = dot_tn(soft.astype(BF16), grad).astype(BF16)
-    dq_ref[...] = (dot(score_grad, k_ref[...]) * scale).astype(BF16)
-    dk_ref[...] = (dot_tn(score_grad, q_ref[...]) * scale).astype(BF16)
+    for head in range(q_ref.shape[1] // HD):
+        cols = slice(head * HD, (head + 1) * HD)
+        soft = p_ref[head]
+        grad = g_ref[:, cols]
+        soft_grad = dot_nt(grad, v_ref[:, cols])
+        inner = jnp.sum(soft_grad * soft, axis=1, keepdims=True)
+        score_grad = (soft * (soft_grad - inner)).astype(BF16)
+        dv_ref[:, cols] = dot_tn(soft.astype(BF16), grad).astype(BF16)
+        dq_ref[:, cols] = (dot(score_grad, k_ref[:, cols]) * scale).astype(BF16)
+        dk_ref[:, cols] = (dot_tn(score_grad, q_ref[:, cols]) * scale).astype(BF16)
 
 
 def sums_kernel(cot_ref, near_ref, out_ref):
@@ -257,9 +259,6 @@
     grads = pl.pallas_call(
         functools.partial(backward_kernel, scale),
         out_shape=(tokens, tokens, tokens),
-        grid=(local_heads,),
-        in_specs=[head] * 3 + [square, head],
-        out_specs=(head, head, head),
         compiler_params=WIDE,
         cost_estimate=cost(4 * attention_flops, 1 << 21),
         name="attention_backward",

time: 175 us -> 175 us (level)
  no operation moved by 1% of the time
where the time goes in v7:
time: 175 us; the launch traced here: 174 us
  waiting for transfers between devices  78.1 us (45%)
  starting transfers between devices  57.3 us (33%)
  between operations  14.4 us (8%)
  Pallas kernels  14 us (8%)
  local copies, waits for them, and re-layouts  7.58 us (4%)
    ppermute x14, starting transfers between devices, shift(): return lax.ppermute(block, axis, [(i, (i + by) % n) for i in range(n)])  57.2 us
    reduce_scatter x1, waiting for transfers between devices, on_device(): lax.psum_scatter(terms_all, 'zl', scatter_dimension=0, tiled=False, axis_...  48.6 us
    ppermute x14, waiting for transfers between devices, shift(): return lax.ppermute(block, axis, [(i, (i + by) % n) for i in range(n)])  20.8 us
    all_gather x1, waiting for transfers between devices, on_device(): heads_all = lax.all_gather(head_out, 'zl', axis=0, axis_index_groups=[line])  8.67 us
    unnamed x25, local copies, waits for them, and re-layouts  6.49 us
    pallas_call x1, Pallas kernels, on_device(): pl.pallas_call(functools.partial(output_kernel, slots), out_shape=jax.Sha...  3.74 us
    pallas_call x1, Pallas kernels, on_device(): pl.pallas_call(functools.partial(forward_kernel, scale), out_shape=(token...  3.55 us
  transfers between devices with their start and end apart: 16, of which 10 were waited for; matrix products, arithmetic and copies ran while one was open for 3% of the time, Pallas kernels for 5%

profile of v7, /device:TPU:10, one launch (start us, length us, event | category | flops | bytes accessed | tf_op | source)
XLA Modules:
  0.0 173.9 jit_solution(14101658907564146952)
XLA Ops:
  7.2 0.0 copy-start
  7.2 0.0 copy-start.7
  7.2 0.0 all-gather.3.cloned.1.call-start
  7.2 19.5 %collective-permute-start = (bf16[6,3072]{1,0:T(8,128)(2,1)}, bf16[6,3072]{1,0:T(8,128)(2,1)S(1)}, u32[]{:S(2)}, u32[]{:S(2)}) collective-permute-start(bf16[6,3072]{1,0:T(8,128)(2,1)} %bitcast.13), channel_id=1, source_target_pairs={{0,512},{512,0},{1,513},{513,1},{2,514},{514,2},{3,515},{515,3},{4... | collective-permute-start | bytes 110600 | tf_op jit(solution)/shard_map/ppermute | solution.py:30
  26.7 0.8 fusion.12
  27.5 0.0 copy-done
  27.5 1.4 fusion.3.cot_ref
  28.9 3.5 %attention_forward.1 = (bf16[256,384]{1,0:T(8,128)(2,1)}, f32[3,256,256]{2,1,0:T(8,128)}) custom-call(bf16[256,384]{1,0:T(8,128)(2,1)} %q_ref.3, bf16[256,384]{1,0:T(8,128)(2,1)} %k_ref.3, bf16[256,384]{1,0:T(8,128)(2,1)} %v_ref.3), custom_call_target="tpu_custom_call" | custom-call | flops 100663296 | bytes 2097152 | tf_op jit(solution)/shard_map/attention_forward/pallas_call | solution.py:179
  32.5 0.0 collective-permute-done
  32.5 0.0 copy-done.7
  32.6 1.9 %collective-permute-start.1 = (bf16[2,6,1536]{2,1,0:T(8,128)(2,1)S(1)}, bf16[2,6,1536]{2,1,0:T(8,128)(2,1)S(1)}, u32[]{:S(2)}, u32[]{:S(2)}) collective-permute-start(bf16[2,6,1536]{2,1,0:T(8,128)(2,1)S(1)} %constant_dynamic-slice_fusion), channel_id=1, source_target_pairs={{0,8},{8,0},{1,9},{9,1},{2,10},{10,2},{3,11},{11,3},{4,12},{12,4},... | collective-permute-start | bytes 110600 | tf_op jit(solution)/shard_map/ppermute | solution.py:30
  34.5 0.0 all-gather.3.cloned.1.call-update
  34.6 0.0 reduce-scatter.2.cloned.1.call-start
  34.6 1.1 collective-permute-done.1
  35.8 3.4 %collective-permute-start.4 = (bf16[24,1536]{1,0:T(8,128)(2,1)S(1)}, bf16[24,1536]{1,0:T(8,128)(2,1)S(1)}, u32[]{:S(2)}, u32[]{:S(2)}) collective-permute-start(bf16[24,1536]{1,0:T(8,128)(2,1)S(1)} %reshape.21), channel_id=1, source_target_pairs={{0,16},{16,32},{32,48},{48,0},{1,17},{17,33},{33,49},{49,1},{2,18}... | collective-permute-start | bytes 221192 | tf_op jit(solution)/shard_map/ppermute | solution.py:30
  39.3 3.0 %collective-permute-start.3 = (bf16[24,1536]{1,0:T(8,128)(2,1)S(1)}, bf16[24,1536]{1,0:T(8,128)(2,1)S(1)}, u32[]{:S(2)}, u32[]{:S(2)}) collective-permute-start(bf16[24,1536]{1,0:T(8,128)(2,1)S(1)} %reshape.21), channel_id=1, source_target_pairs={{0,32},{16,48},{32,0},{48,16},{1,33},{17,49},{33,1},{49,17},{2,34}... | collective-permute-start | bytes 221192 | tf_op jit(solution)/shard_map/ppermute | solution.py:30
  42.3 4.1 %collective-permute-start.2 = (bf16[24,1536]{1,0:T(8,128)(2,1)S(1)}, bf16[24,1536]{1,0:T(8,128)(2,1)S(1)}, u32[]{:S(2)}, u32[]{:S(2)}) collective-permute-start(bf16[24,1536]{1,0:T(8,128)(2,1)S(1)} %reshape.21), channel_id=1, source_target_pairs={{0,48},{16,0},{32,16},{48,32},{1,49},{17,1},{33,17},{49,33},{2,50}... | collective-permute-start | bytes 221192 | tf_op jit(solution)/shard_map/ppermute | solution.py:30
  46.4 2.2 %collective-permute-done.2 = bf16[24,1536]{1,0:T(8,128)(2,1)S(1)} collective-permute-done((bf16[24,1536]{1,0:T(8,128)(2,1)S(1)}, bf16[24,1536]{1,0:T(8,128)(2,1)S(1)}, u32[]{:S(2)}, u32[]{:S(2)}) %collective-permute-start.2) | collective-permute-done | bytes 73760 | tf_op jit(solution)/shard_map/ppermute | solution.py:30
  48.6 0.0 collective-permute-done.3
  48.6 0.0 collective-permute-done.4
  48.7 4.7 %collective-permute-start.8 = (bf16[96,1536]{1,0:T(8,128)(2,1)S(1)}, bf16[96,1536]{1,0:T(8,128)(2,1)S(1)}, u32[]{:S(2)}, u32[]{:S(2)}) collective-permute-start(bf16[96,1536]{1,0:T(8,128)(2,1)S(1)} %get-tuple-element.25), channel_id=1, source_target_pairs={{0,448},{64,0},{128,64},{192,128},{256,192},{320,256},{384,320},{4... | collective-permute-start | bytes 884744 | tf_op jit(solution)/shard_map/ppermute | solution.py:30
  53.4 1.9 %collective-permute-start.5 = (bf16[96,1536]{1,0:T(8,128)(2,1)S(1)}, bf16[96,1536]{1,0:T(8,128)(2,1)S(1)}, u32[]{:S(2)}, u32[]{:S(2)}) collective-permute-start(bf16[96,1536]{1,0:T(8,128)(2,1)S(1)} %get-tuple-element.25), channel_id=1, source_target_pairs={{0,64},{64,128},{128,192},{192,256},{256,320},{320,384},{384,448},... | collective-permute-start | bytes 884744 | tf_op jit(solution)/shard_map/ppermute | solution.py:30
  55.3 3.5 %collective-permute-done.8 = bf16[96,1536]{1,0:T(8,128)(2,1)S(1)} collective-permute-done((bf16[96,1536]{1,0:T(8,128)(2,1)S(1)}, bf16[96,1536]{1,0:T(8,128)(2,1)S(1)}, u32[]{:S(2)}, u32[]{:S(2)}) %collective-permute-start.8) | collective-permute-done | bytes 294944 | tf_op jit(solution)/shard_map/ppermute | solution.py:30
  58.8 3.8 %collective-permute-start.9 = (bf16[96,1536]{1,0:T(8,128)(2,1)S(1)}, bf16[96,1536]{1,0:T(8,128)(2,1)}, u32[]{:S(2)}, u32[]{:S(2)}) collective-permute-start(bf16[96,1536]{1,0:T(8,128)(2,1)S(1)} %collective-permute-done.8), channel_id=1, source_target_pairs={{0,448},{64,0},{128,64},{192,128},{256,192},{320,256},{384,320},{4... | collective-permute-start | bytes 884744 | tf_op jit(solution)/shard_map/ppermute | solution.py:30
  62.6 0.0 collective-permute-done.5
  62.6 2.0 %collective-permute-start.6 = (bf16[96,1536]{1,0:T(8,128)(2,1)S(1)}, bf16[96,1536]{1,0:T(8,128)(2,1)S(1)}, u32[]{:S(2)}, u32[]{:S(2)}) collective-permute-start(bf16[96,1536]{1,0:T(8,128)(2,1)S(1)} %collective-permute-done.5), channel_id=1, source_target_pairs={{0,64},{64,128},{128,192},{192,256},{256,320},{320,384},{384,448},... | collective-permute-start | bytes 884744 | tf_op jit(solution)/shard_map/ppermute | solution.py:30
  64.7 3.5 %collective-permute-done.9 = bf16[96,1536]{1,0:T(8,128)(2,1)} collective-permute-done((bf16[96,1536]{1,0:T(8,128)(2,1)S(1)}, bf16[96,1536]{1,0:T(8,128)(2,1)}, u32[]{:S(2)}, u32[]{:S(2)}) %collective-permute-start.9) | collective-permute-done | bytes 294944 | tf_op jit(solution)/shard_map/ppermute | solution.py:30
  68.2 3.8 %collective-permute-start.10 = (bf16[96,1536]{1,0:T(8,128)(2,1)}, bf16[96,1536]{1,0:T(8,128)(2,1)}, u32[]{:S(2)}, u32[]{:S(2)}) collective-permute-start(bf16[96,1536]{1,0:T(8,128)(2,1)} %collective-permute-done.9), channel_id=1, source_target_pairs={{0,448},{64,0},{128,64},{192,128},{256,192},{320,256},{384,320},{4... | collective-permute-start | bytes 884744 | tf_op jit(solution)/shard_map/ppermute | solution.py:30
  72.0 0.5 collective-permute-done.6
  72.5 1.9 %collective-permute-start.7 = (bf16[96,1536]{1,0:T(8,128)(2,1)S(1)}, bf16[96,1536]{1,0:T(8,128)(2,1)}, u32[]{:S(2)}, u32[]{:S(2)}) collective-permute-start(bf16[96,1536]{1,0:T(8,128)(2,1)S(1)} %collective-permute-done.6), channel_id=1, source_target_pairs={{0,64},{64,128},{128,192},{192,256},{256,320},{320,384},{384,448},... | collective-permute-start | bytes 884744 | tf_op jit(solution)/shard_map/ppermute | solution.py:30
  74.4 1.0 constant_dynamic-update-slice_fusion.4.own_near.near_ref
  75.4 1.9 %collective-permute-start.12 = (bf16[480,1536]{1,0:T(8,128)(2,1)S(1)}, bf16[480,1536]{1,0:T(8,128)(2,1)S(1)}, u32[]{:S(2)}, u32[]{:S(2)}) collective-permute-start(bf16[480,1536]{1,0:T(8,128)(2,1)S(1)} %constant_dynamic-update-slice_fusion.4.own_near.near_ref), channel_id=1, source_target_pairs={{0,8},{8,0},{1,9},{9,1},{2,10},{10,2},{3,11},{11,3},{4,12},{12,4},... | collective-permute-start | bytes 4423688 | tf_op jit(solution)/shard_map/ppermute | solution.py:30
  77.3 5.2 %collective-permute-done.7 = bf16[96,1536]{1,0:T(8,128)(2,1)} collective-permute-done((bf16[96,1536]{1,0:T(8,128)(2,1)S(1)}, bf16[96,1536]{1,0:T(8,128)(2,1)}, u32[]{:S(2)}, u32[]{:S(2)}) %collective-permute-start.7) | collective-permute-done | bytes 294944 | tf_op jit(solution)/shard_map/ppermute | solution.py:30
  82.5 8.7 %all-gather.3.cloned.1.call-done = bf16[2048,384]{1,0:T(8,128)(2,1)} async-done(((bf16[256,384]{1,0:T(8,128)(2,1)}), bf16[2048,384]{1,0:T(8,128)(2,1)}) %all-gather.3.cloned.1.call-update) | async-done | bytes 1572880 | tf_op jit(solution)/shard_map/all_gather | solution.py:192
  91.2 0.0 copy-start.5
  91.2 3.4 %collective-permute-start.11 = (bf16[96,1536]{1,0:T(8,128)(2,1)}, bf16[96,1536]{1,0:T(8,128)(2,1)S(1)}, u32[]{:S(2)}, u32[]{:S(2)}) collective-permute-start(bf16[96,1536]{1,0:T(8,128)(2,1)} %collective-permute-done.7), channel_id=1, source_target_pairs={{0,64},{64,128},{128,192},{192,256},{256,320},{320,384},{384,448},... | collective-permute-start | bytes 884744 | tf_op jit(solution)/shard_map/ppermute | solution.py:30
  94.5 1.0 constant_dynamic-update-slice_fusion.14
  95.5 0.0 collective-permute-done.10
  95.6 1.0 constant_dynamic-update-slice_fusion.13
  96.5 3.6 %collective-permute-done.11 = bf16[96,1536]{1,0:T(8,128)(2,1)S(1)} collective-permute-done((bf16[96,1536]{1,0:T(8,128)(2,1)}, bf16[96,1536]{1,0:T(8,128)(2,1)S(1)}, u32[]{:S(2)}, u32[]{:S(2)}) %collective-permute-start.11) | collective-permute-done | bytes 294944 | tf_op jit(solution)/shard_map/ppermute | solution.py:30
  100.2 0.0 copy-start.1
  100.2 1.9 %collective-permute-start.13 = (bf16[288,1536]{1,0:T(8,128)(2,1)S(1)}, bf16[288,1536]{1,0:T(8,128)(2,1)S(1)}, u32[]{:S(2)}, u32[]{:S(2)}) collective-permute-start(bf16[288,1536]{1,0:T(8,128)(2,1)S(1)} %constant_dynamic-update-slice_fusion.12.own_far), channel_id=1, source_target_pairs={{0,8},{8,0},{1,9},{9,1},{2,10},{10,2},{3,11},{11,3},{4,12},{12,4},... | collective-permute-start | bytes 2654216 | tf_op jit(solution)/shard_map/ppermute | solution.py:30
  102.1 0.0 copy-done.5
  102.1 0.6 gradient_sums.2.own_sum
  102.7 0.0 collective-permute-done.12.other_near.near_ref
  102.7 0.6 gradient_sums.3.other_sum
  103.2 1.2 collective-permute-done.13.other_far
  104.5 0.0 copy-done.1
  104.5 2.3 %gradient_terms.1 = bf16[8,256,384]{2,1,0:T(8,128)(2,1)} custom-call(s32[1]{0:T(128)} %bitcast.core_ref, bf16[256,768]{1,0:T(8,128)(2,1)S(1)} %copy-done.5, f32[256,1536]{1,0:T(8,128)S(1)} %gradient_sums.2.own_sum, f32[256,1536]{1,0:T(8,128)S(1)} %gradient_sums.3.other_sum, bf16[288,1536]{1,0:T(8,128)(2,1)S(1)} %constant_dynamic-update-slice_fusion.12.own_far, ...), custom_call_target="tpu_custom_call" | custom-call | flops 1207959552 | bytes 8388608 | tf_op jit(solution)/shard_map/gradient_terms/pallas_call | solution.py:220
  106.8 0.0 copy-start.3
  106.8 0.9 copy-done.3
  107.7 0.0 reduce-scatter.2.cloned.1.call-update
  107.8 0.0 copy-start.2
  107.8 0.3 fusion.s_ref
  108.0 0.9 copy-done.2
  108.9 0.0 copy-start.4
  108.9 1.2 copy-done.4
  110.1 0.0 copy-start.6
  110.1 1.4 copy-done.6
  111.5 3.7 %output_projection.1 = bf16[256,768]{1,0:T(8,128)(2,1)} custom-call(s32[1]{0:T(128)} %bitcast.core_ref, bf16[8,256,384]{2,1,0:T(8,128)(2,1)S(1)} %bitcast.11, bf16[480,1536]{1,0:T(8,128)(2,1)S(1)} %constant_dynamic-update-slice_fusion.4.own_near.near_ref, bf16[288,1536]{1,0:T(8,128)(2,1)S(1)} %copy-done.2, ...), custom_call_target="tpu_custom_call" | custom-call | flops 1207959552 | bytes 8388608 | tf_op jit(solution)/shard_map/output_projection/pallas_call | solution.py:241
  115.2 48.6 %reduce-scatter.2.cloned.1.call-done = bf16[1,256,384]{2,1,0:T(8,128)(2,1)} async-done(((bf16[8,256,384]{2,1,0:T(8,128)(2,1)}), bf16[1,256,384]{2,1,0:T(8,128)(2,1)}) %reduce-scatter.2.cloned.1.call-update) | async-done | bytes 196624 | tf_op jit(solution)/shard_map/reduce_scatter | solution.py:236
  163.8 3.2 %attention_backward.1 = (bf16[256,384]{1,0:T(8,128)(2,1)}, bf16[256,384]{1,0:T(8,128)(2,1)}, bf16[256,384]{1,0:T(8,128)(2,1)}) custom-call(bf16[256,384]{1,0:T(8,128)(2,1)} %q_ref.3, bf16[256,384]{1,0:T(8,128)(2,1)} %k_ref.3, bf16[256,384]{1,0:T(8,128)(2,1)} %v_ref.3, f32[3,256,256]{2,1,0:T(8,128)} %get-tuple-element.17.p_ref, bf16[256,384]{1,0:T(8,128)(2,1)} %bitcast.12), custom_call_target="tpu_custom_call" | custom-call | flops 201326592 | bytes 2097152 | tf_op jit(solution)/shard_map/attention_backward/pallas_call | solution.py:259
  (15 shorter events, 0.3 us)
Async XLA Ops:
  7.2 20.4 %copy-start = (bf16[256,768]{1,0:T(8,128)(2,1)S(1)}, bf16[256,768]{1,0:T(8,128)(2,1)}, u32[]{:S(2)}) copy-start(bf16[256,768]{1,0:T(8,128)(2,1)} %param.14) | copy-start | bytes 1179652
  7.2 25.3 %copy-start.7 = (bf16[3072,6]{0,1:T(8,128)(2,1)S(1)}, bf16[3072,6]{0,1:T(8,128)(2,1)}, u32[]{:S(2)}) copy-start(bf16[3072,6]{0,1:T(8,128)(2,1)} %param.13) | copy-start | bytes 110596
  7.2 84.0 %all-gather.3.cloned.1.call-start = ((), (), s32[]{:S(2)}) async-start(), calls=%async_computation.2 | async-start | bytes 1769472 | tf_op jit(solution)/shard_map/all_gather | solution.py:192
  7.2 25.3 %collective-permute-start = (bf16[6,3072]{1,0:T(8,128)(2,1)}, bf16[6,3072]{1,0:T(8,128)(2,1)S(1)}, u32[]{:S(2)}, u32[]{:S(2)}) collective-permute-start(bf16[6,3072]{1,0:T(8,128)(2,1)} %bitcast.13), channel_id=1, source_target_pairs={{0,512},{512,0},{1,513},{513,1},{2,514},{514,2},{3,515},{515,3},{4... | collective-permute-start | bytes 110600 | tf_op jit(solution)/shard_map/ppermute | solution.py:30
  32.6 3.1 %collective-permute-start.1 = (bf16[2,6,1536]{2,1,0:T(8,128)(2,1)S(1)}, bf16[2,6,1536]{2,1,0:T(8,128)(2,1)S(1)}, u32[]{:S(2)}, u32[]{:S(2)}) collective-permute-start(bf16[2,6,1536]{2,1,0:T(8,128)(2,1)S(1)} %constant_dynamic-slice_fusion), channel_id=1, source_target_pairs={{0,8},{8,0},{1,9},{9,1},{2,10},{10,2},{3,11},{11,3},{4,12},{12,4},... | collective-permute-start | bytes 110600 | tf_op jit(solution)/shard_map/ppermute | solution.py:30
  34.6 129.2 %reduce-scatter.2.cloned.1.call-start = ((), (), s32[]{:S(2)}) async-start(), calls=%async_computation.1 | async-start | bytes 1769472 | tf_op jit(solution)/shard_map/reduce_scatter | solution.py:236
  35.8 12.8 %collective-permute-start.4 = (bf16[24,1536]{1,0:T(8,128)(2,1)S(1)}, bf16[24,1536]{1,0:T(8,128)(2,1)S(1)}, u32[]{:S(2)}, u32[]{:S(2)}) collective-permute-start(bf16[24,1536]{1,0:T(8,128)(2,1)S(1)} %reshape.21), channel_id=1, source_target_pairs={{0,16},{16,32},{32,48},{48,0},{1,17},{17,33},{33,49},{49,1},{2,18}... | collective-permute-start | bytes 221192 | tf_op jit(solution)/shard_map/ppermute | solution.py:30
  39.3 9.3 %collective-permute-start.3 = (bf16[24,1536]{1,0:T(8,128)(2,1)S(1)}, bf16[24,1536]{1,0:T(8,128)(2,1)S(1)}, u32[]{:S(2)}, u32[]{:S(2)}) collective-permute-start(bf16[24,1536]{1,0:T(8,128)(2,1)S(1)} %reshape.21), channel_id=1, source_target_pairs={{0,32},{16,48},{32,0},{48,16},{1,33},{17,49},{33,1},{49,17},{2,34}... | collective-permute-start | bytes 221192 | tf_op jit(solution)/shard_map/ppermute | solution.py:30
  42.3 6.3 %collective-permute-start.2 = (bf16[24,1536]{1,0:T(8,128)(2,1)S(1)}, bf16[24,1536]{1,0:T(8,128)(2,1)S(1)}, u32[]{:S(2)}, u32[]{:S(2)}) collective-permute-start(bf16[24,1536]{1,0:T(8,128)(2,1)S(1)} %reshape.21), channel_id=1, source_target_pairs={{0,48},{16,0},{32,16},{48,32},{1,49},{17,1},{33,17},{49,33},{2,50}... | collective-permute-start | bytes 221192 | tf_op jit(solution)/shard_map/ppermute | solution.py:30
  48.7 10.1 %collective-permute-start.8 = (bf16[96,1536]{1,0:T(8,128)(2,1)S(1)}, bf16[96,1536]{1,0:T(8,128)(2,1)S(1)}, u32[]{:S(2)}, u32[]{:S(2)}) collective-permute-start(bf16[96,1536]{1,0:T(8,128)(2,1)S(1)} %get-tuple-element.25), channel_id=1, source_target_pairs={{0,448},{64,0},{128,64},{192,128},{256,192},{320,256},{384,320},{4... | collective-permute-start | bytes 884744 | tf_op jit(solution)/shard_map/ppermute | solution.py:30
  53.4 9.2 %collective-permute-start.5 = (bf16[96,1536]{1,0:T(8,128)(2,1)S(1)}, bf16[96,1536]{1,0:T(8,128)(2,1)S(1)}, u32[]{:S(2)}, u32[]{:S(2)}) collective-permute-start(bf16[96,1536]{1,0:T(8,128)(2,1)S(1)} %get-tuple-element.25), channel_id=1, source_target_pairs={{0,64},{64,128},{128,192},{192,256},{256,320},{320,384},{384,448},... | collective-permute-start | bytes 884744 | tf_op jit(solution)/shard_map/ppermute | solution.py:30
  58.8 9.4 %collective-permute-start.9 = (bf16[96,1536]{1,0:T(8,128)(2,1)S(1)}, bf16[96,1536]{1,0:T(8,128)(2,1)}, u32[]{:S(2)}, u32[]{:S(2)}) collective-permute-start(bf16[96,1536]{1,0:T(8,128)(2,1)S(1)} %collective-permute-done.8), channel_id=1, source_target_pairs={{0,448},{64,0},{128,64},{192,128},{256,192},{320,256},{384,320},{4... | collective-permute-start | bytes 884744 | tf_op jit(solution)/shard_map/ppermute | solution.py:30
  62.6 9.8 %collective-permute-start.6 = (bf16[96,1536]{1,0:T(8,128)(2,1)S(1)}, bf16[96,1536]{1,0:T(8,128)(2,1)S(1)}, u32[]{:S(2)}, u32[]{:S(2)}) collective-permute-start(bf16[96,1536]{1,0:T(8,128)(2,1)S(1)} %collective-permute-done.5), channel_id=1, source_target_pairs={{0,64},{64,128},{128,192},{192,256},{256,320},{320,384},{384,448},... | collective-permute-start | bytes 884744 | tf_op jit(solution)/shard_map/ppermute | solution.py:30
  68.2 27.3 %collective-permute-start.10 = (bf16[96,1536]{1,0:T(8,128)(2,1)}, bf16[96,1536]{1,0:T(8,128)(2,1)}, u32[]{:S(2)}, u32[]{:S(2)}) collective-permute-start(bf16[96,1536]{1,0:T(8,128)(2,1)} %collective-permute-done.9), channel_id=1, source_target_pairs={{0,448},{64,0},{128,64},{192,128},{256,192},{320,256},{384,320},{4... | collective-permute-start | bytes 884744 | tf_op jit(solution)/shard_map/ppermute | solution.py:30
  72.5 10.0 %collective-permute-start.7 = (bf16[96,1536]{1,0:T(8,128)(2,1)S(1)}, bf16[96,1536]{1,0:T(8,128)(2,1)}, u32[]{:S(2)}, u32[]{:S(2)}) collective-permute-start(bf16[96,1536]{1,0:T(8,128)(2,1)S(1)} %collective-permute-done.6), channel_id=1, source_target_pairs={{0,64},{64,128},{128,192},{192,256},{256,320},{320,384},{384,448},... | collective-permute-start | bytes 884744 | tf_op jit(solution)/shard_map/ppermute | solution.py:30
  75.4 27.3 %collective-permute-start.12 = (bf16[480,1536]{1,0:T(8,128)(2,1)S(1)}, bf16[480,1536]{1,0:T(8,128)(2,1)S(1)}, u32[]{:S(2)}, u32[]{:S(2)}) collective-permute-start(bf16[480,1536]{1,0:T(8,128)(2,1)S(1)} %constant_dynamic-update-slice_fusion.4.own_near.near_ref), channel_id=1, source_target_pairs={{0,8},{8,0},{1,9},{9,1},{2,10},{10,2},{3,11},{11,3},{4,12},{12,4},... | collective-permute-start | bytes 4423688 | tf_op jit(solution)/shard_map/ppermute | solution.py:30
  91.2 10.9 %copy-start.5 = (bf16[256,768]{1,0:T(8,128)(2,1)S(1)}, bf16[256,768]{1,0:T(8,128)(2,1)}, u32[]{:S(2)}) copy-start(bf16[256,768]{1,0:T(8,128)(2,1)} %fusion.3.cot_ref) | copy-start | bytes 1179652
  91.2 8.9 %collective-permute-start.11 = (bf16[96,1536]{1,0:T(8,128)(2,1)}, bf16[96,1536]{1,0:T(8,128)(2,1)S(1)}, u32[]{:S(2)}, u32[]{:S(2)}) collective-permute-start(bf16[96,1536]{1,0:T(8,128)(2,1)} %collective-permute-done.7), channel_id=1, source_target_pairs={{0,64},{64,128},{128,192},{192,256},{256,320},{320,384},{384,448},... | collective-permute-start | bytes 884744 | tf_op jit(solution)/shard_map/ppermute | solution.py:30
  100.2 4.3 %copy-start.1 = (bf16[288,1536]{1,0:T(8,128)(2,1)}, bf16[288,1536]{1,0:T(8,128)(2,1)S(1)}, u32[]{:S(2)}) copy-start(bf16[288,1536]{1,0:T(8,128)(2,1)S(1)} %constant_dynamic-update-slice_fusion.12.own_far) | copy-start | bytes 2654212
  100.2 4.3 %collective-permute-start.13 = (bf16[288,1536]{1,0:T(8,128)(2,1)S(1)}, bf16[288,1536]{1,0:T(8,128)(2,1)S(1)}, u32[]{:S(2)}, u32[]{:S(2)}) collective-permute-start(bf16[288,1536]{1,0:T(8,128)(2,1)S(1)} %constant_dynamic-update-slice_fusion.12.own_far), channel_id=1, source_target_pairs={{0,8},{8,0},{1,9},{9,1},{2,10},{10,2},{3,11},{11,3},{4,12},{12,4},... | collective-permute-start | bytes 2654216 | tf_op jit(solution)/shard_map/ppermute | solution.py:30
  106.8 0.9 copy-start.3
  107.8 1.2 copy-start.2
  108.9 1.2 copy-start.4
  110.1 1.4 copy-start.6
Sparse Core Ops, SparseCore 0:
  34.7 56.4 all-gather.2
  107.9 55.8 reduce-scatter.1
